TPU v7x, 32 devices: a whole 2x2x4 slice. The times are simulated.
32 devices in a mesh: row: 32 (over z, y, x, core), col: 1.
Axes of the slice: x: 2, y: 2, z: 4, core: 2. Of those that a mesh axis runs over, the one named last changes fastest.
Arguments:
- homolog_features: bfloat16 [64, 128, 256], P(None, ('col', 'row')), may hold values from -6 to 6
- standardize_multiplier: float32 [256], replicated, may hold values from 0.1 to 1.9
- first_factor_weights: bfloat16 [256, 32], replicated, may hold values from -0.375 to 0.375
- second_factor_weights: bfloat16 [256, 32], replicated, may hold values from -0.375 to 0.375
- output_projection_matrix: bfloat16 [1024, 128], replicated, may hold values from -1.5 to 1.5
- output_bias: float32 [128], replicated, may hold values from -3 to 3
- pair_cotangent: bfloat16 [128, 128, 128], P('row', 'col'), may hold values from -2 to 2
Outputs:
- pair_delta: bfloat16 [128, 128, 128], P('row', 'col')
- alignment_gradient: bfloat16 [64, 128, 256], P(None, ('col', 'row'))
- gain_gradient: float32 [256], replicated
- left_projection_gradient: float32 [256, 32], replicated
- right_projection_gradient: float32 [256, 32], replicated
- output_projection_gradient: float32 [1024, 128], P(('row', 'col'))
- output_bias_gradient: float32 [128], replicated
All inputs are finite; a program needn't handle non-finite values.
Results may differ from a plain program's by a relative error of at most 0.0072.
Values may be sent and summed in bfloat16 or wider, within the bound.
No kernel may reach another device: no remote copies, remote signals or barrier semaphores. Data moves between devices by JAX's collectives and lax.ppermute only.
A program may use at most 64 MiB of HBM per device.

v0:
```python
import math

import jax
import jax.numpy as jnp
from jax import lax
from jax.sharding import PartitionSpec as P

ln_epsilon = 1e-05


def from_root(value, axis, root):
    mine = lax.axis_index(axis) == root
    return lax.psum(jnp.where(mine, value, jnp.zeros_like(value)), axis)


def layer_norm_output(homolog_features, standardize_multiplier):
    value_entries = homolog_features.astype(jnp.float32)
    centred = value_entries - jnp.mean(value_entries, axis=-1, keepdims=True)
    reciprocal_deviation = lax.rsqrt(
        jnp.mean(centred * centred, axis=-1, keepdims=True) + ln_epsilon
    )
    scaled_rows = centred * reciprocal_deviation
    normalized_rows = (scaled_rows * standardize_multiplier).astype(jnp.bfloat16)
    return (scaled_rows, reciprocal_deviation, normalized_rows)


def on_device(
    homolog_features,
    standardize_multiplier,
    first_factor_weights,
    second_factor_weights,
    output_projection_matrix,
    output_bias,
    pair_cotangent,
):
    sequence_count, local_residues, channel_count = homolog_features.shape
    hidden = first_factor_weights.shape[1]
    pair_channels = output_projection_matrix.shape[1]
    row_count = lax.axis_size("row")
    col_count = lax.axis_size("col")
    ratio = row_count // col_count
    row_index = lax.axis_index("row")
    col_index = lax.axis_index("col")
    scaled_rows, reciprocal_deviation, normalized_rows = layer_norm_output(
        homolog_features, standardize_multiplier
    )
    left_own = jnp.dot(
        normalized_rows, first_factor_weights, preferred_element_type=jnp.float32
    ).astype(jnp.bfloat16)
    right_own = jnp.dot(
        normalized_rows, second_factor_weights, preferred_element_type=jnp.float32
    ).astype(jnp.bfloat16)
    left_cols, right_cols = (
        lax.all_gather(
            left_own.reshape(sequence_count, local_residues * hidden), "row", axis=1, tiled=True
        ),
        lax.all_gather(
            right_own.reshape(sequence_count, local_residues * hidden), "row", axis=1, tiled=True
        ),
    )
    col_res = local_residues * row_count
    row_res = col_res // ratio
    offset = row_index % ratio * row_res
    piece_flat = lax.dynamic_slice_in_dim(left_cols, offset * hidden, row_res * hidden, 1)
    left_rows = from_root(piece_flat, "col", row_index // ratio).reshape(
        sequence_count, row_res, hidden
    )
    right_block = right_cols.reshape(sequence_count, col_res, hidden)
    group = math.gcd(row_res, max(1, 512 // col_res))
    blocks = row_res // group
    left_steps = jnp.transpose(
        left_rows.reshape(sequence_count, blocks, group, hidden), (1, 0, 2, 3)
    )
    grad_steps = pair_cotangent.reshape(blocks, group, col_res, pair_channels)
    per_homolog_weight = 1.0 / sequence_count

    def pair_step(carried, inputs):
        out_acc, right_acc = carried
        left_blk, grad_blk = inputs
        outer = (
            jnp.einsum("sic,sjd->ijcd", left_blk, right_block, preferred_element_type=jnp.float32)
            * per_homolog_weight
        )
        outer_bf = outer.reshape(group * col_res, hidden * hidden).astype(jnp.bfloat16)
        update = (
            jnp.dot(outer_bf, output_projection_matrix, preferred_element_type=jnp.float32)
            + output_bias
        ).astype(jnp.bfloat16)
        grad_rows = grad_blk.reshape(group * col_res, pair_channels)
        out_acc = out_acc + lax.dot_general(
            outer_bf, grad_rows, (((0,), (0,)), ((), ())), preferred_element_type=jnp.float32
        )
        outer_grad = jnp.dot(
            grad_rows, output_projection_matrix.T, preferred_element_type=jnp.float32
        ).astype(jnp.bfloat16)
        outer_grad = outer_grad.reshape(group, col_res, hidden, hidden)
        left_blk_grad = (
            jnp.einsum("ijcd,sjd->sic", outer_grad, right_block, preferred_element_type=jnp.float32)
            * per_homolog_weight
        )
        right_acc = (
            right_acc
            + jnp.einsum("ijcd,sic->sjd", outer_grad, left_blk, preferred_element_type=jnp.float32)
            * per_homolog_weight
        )
        return (
            (out_acc, right_acc),
            (update.reshape(group, col_res, pair_channels), left_blk_grad),
        )

    initial_carry = (
        jnp.zeros((hidden * hidden, pair_channels), jnp.float32),
        jnp.zeros((sequence_count, col_res, hidden), jnp.float32),
    )
    (out_acc, right_part), (updates, first_factor_pieces) = lax.scan(
        pair_step, initial_carry, (left_steps, grad_steps)
    )
    pair_delta = updates.reshape(row_res, col_res, pair_channels)
    left_part = jnp.transpose(first_factor_pieces, (1, 0, 2, 3)).reshape(
        sequence_count, row_res * hidden
    )
    right_flat = right_part.reshape(sequence_count, col_res * hidden)
    left_row = lax.psum(left_part, "col")
    owner = row_index // ratio == col_index
    slotted = lax.dynamic_update_slice_in_dim(
        jnp.zeros((sequence_count, col_res * hidden), jnp.float32),
        jnp.where(owner, left_row, 0.0),
        offset * hidden,
        1,
    )
    first_factor_total, right_sum = (
        lax.psum_scatter(slotted, "row", scatter_dimension=1, tiled=True),
        lax.psum_scatter(right_flat, "row", scatter_dimension=1, tiled=True),
    )
    left_bf = first_factor_total.reshape(sequence_count, local_residues, hidden).astype(
        jnp.bfloat16
    )
    right_bf = right_sum.reshape(sequence_count, local_residues, hidden).astype(jnp.bfloat16)
    normed_grad = jnp.dot(
        left_bf, first_factor_weights.T, preferred_element_type=jnp.float32
    ) + jnp.dot(right_bf, second_factor_weights.T, preferred_element_type=jnp.float32)
    scaled_gradient = normed_grad * standardize_multiplier
    centering_term = jnp.mean(scaled_gradient, axis=-1, keepdims=True)
    gradient_slope_term = jnp.mean(scaled_gradient * scaled_rows, axis=-1, keepdims=True)
    alignment_gradient = (
        reciprocal_deviation
        * (scaled_gradient - centering_term - scaled_rows * gradient_slope_term)
    ).astype(jnp.bfloat16)
    gain_part = jnp.sum(normed_grad * scaled_rows, axis=(0, 1))
    left_weight = jnp.einsum(
        "srm,srh->mh", normalized_rows, left_bf, preferred_element_type=jnp.float32
    )
    right_weight = jnp.einsum(
        "srm,srh->mh", normalized_rows, right_bf, preferred_element_type=jnp.float32
    )
    bias_part = jnp.sum(pair_cotangent, axis=(0, 1), dtype=jnp.float32)
    left_total, right_total, gain_total, bias_total = lax.psum(
        (left_weight, right_weight, gain_part, bias_part), ("row", "col")
    )
    out_share = lax.psum_scatter(out_acc, ("row", "col"), scatter_dimension=0, tiled=True)
    scale = 1.0 / (local_residues * row_count * col_count)
    return (
        pair_delta,
        alignment_gradient,
        gain_total * scale,
        left_total * scale,
        right_total * scale,
        out_share * scale,
        bias_total * scale,
    )


def solution(mesh):
    in_specs = (P(None, ("col", "row"), None), P(), P(), P(), P(), P(), P("row", "col", None))
    out_specs = (
        P("row", "col", None),
        P(None, ("col", "row"), None),
        P(),
        P(),
        P(),
        P(("row", "col"), None),
        P(),
    )
    return jax.shard_map(
        on_device, mesh=mesh, in_specs=in_specs, out_specs=out_specs, check_vma=False
    )
```

profile of v0, /device:TPU:0, one launch (start us, length us, event | category | flops | bytes accessed | tf_op | source)
XLA Modules:
  0.0 634.7 jit_solution(4190816909433938646)
XLA Ops:
  7.3 1.0 convert_reduce_fusion
  8.3 1.1 fusion.26
  9.4 1.2 convolution_convert_fusion.1
  10.6 1.2 convolution_convert_fusion.2
  11.7 46.2 %all_gather.6 = bf16[64,4096]{0,1:T(8,128)(2,1)S(1)} all-gather(bf16[64,128]{0,1:T(8,128)(2,1)S(1)} %bitcast.83), channel_id=1, replica_groups=mesh['row'=32,'col'=1] {'row'}, dimensions={1}, use_global_device_ids=true | all-gather | bytes 540672 | tf_op jit(solution)/shard_map/all_gather | solution.py:57
  57.9 39.5 %all_gather.7 = bf16[64,4096]{0,1:T(8,128)(2,1)S(1)} all-gather(bf16[64,128]{0,1:T(8,128)(2,1)S(1)} %bitcast.82), channel_id=1, replica_groups=mesh['row'=32,'col'=1] {'row'}, dimensions={1}, use_global_device_ids=true | all-gather | bytes 540672 | tf_op jit(solution)/shard_map/all_gather | solution.py:54
  97.4 0.6 fusion
  98.6 1.0 copy-done.2
  99.5 1.2 fusion.5
  100.9 1.9 copy.22
  103.2 0.5 copy.21
  104.1 0.7 copy-done.6
  104.8 0.8 fusion.4
  105.8 1.3 copy-done.1
  107.2 1.5 fusion.1
  108.8 2.8 copy.25
  111.7 0.6 convert_reduce_fusion.1
  112.3 1.1 fusion.2
  113.4 118.8 %reduce-scatter.8.cloned.1.call-done = f32[32,128]{1,0:T(8,128)} async-done(((f32[1024,128]{1,0:T(8,128)}), f32[32,128]{1,0:T(8,128)}) %reduce-scatter.8.cloned.1.call-update) | async-done | bytes 16400 | tf_op jit(solution)/shard_map/reduce_scatter | solution.py:160
  232.2 1.3 broadcast_multiply_fusion.2
  233.5 133.7 %reduce-scatter.4.cloned.1.call-done = f32[64,128]{0,1:T(8,128)} async-done(((f32[64,4096]{0,1:T(8,128)}), f32[64,128]{0,1:T(8,128)}) %reduce-scatter.4.cloned.1.call-update) | async-done | bytes 32784 | tf_op jit(solution)/shard_map/reduce_scatter | solution.py:132
  367.2 0.8 convert_element_type.59
  368.1 0.9 convolution_bitcast_fusion.3
  369.2 133.0 %reduce-scatter.6.cloned.1.call-done = f32[64,128]{0,1:T(8,128)} async-done(((f32[64,4096]{0,1:T(8,128)}), f32[64,128]{0,1:T(8,128)}) %reduce-scatter.6.cloned.1.call-update) | async-done | bytes 32784 | tf_op jit(solution)/shard_map/reduce_scatter | solution.py:133
  502.1 0.8 convert_element_type.61
  503.0 0.9 convolution_bitcast_fusion.2
  503.8 0.8 fusion.25
  504.9 0.8 copy.26
  505.6 118.9 %all-reduce.3.cloned.1.call-done = (f32[256]{0:T(256)}, f32[256,32]{0,1:T(8,128)}, f32[256,32]{0,1:T(8,128)}, f32[128]{0:T(128)}) async-done(((f32[256]{0:T(256)}, f32[256,32]{0,1:T(8,128)}, f32[256,32]{0,1:T(8,128)}, f32[128]{0:T(128)}), (f32[256]{0:T(256)}, f32[256,32]{0,1:T(8,128)}, f32[256,32]{0,1:T(8,128)}, f32[128]{0:T(128)})) %all-reduce.3.cloned.1.call-update) | async-done | bytes 67088 | tf_op jit(solution)/shard_map/psum | solution.py:157
  624.5 1.2 broadcast_multiply_fusion.6
  625.7 1.1 broadcast_multiply_fusion.7
  626.8 1.4 broadcast_multiply_fusion
  (40 shorter events, 2.1 us)
Async XLA Ops:
  7.2 95.6 %copy-start = (bf16[1024,128]{1,0:T(8,128)(2,1)S(1)}, bf16[1024,128]{1,0:T(8,128)(2,1)}, u32[]{:S(2)}) copy-start(bf16[1024,128]{1,0:T(8,128)(2,1)} %param.11) | copy-start | bytes 786436
  7.2 225.0 %reduce-scatter.8.cloned.1.call-start = ((), (), s32[]{:S(2)}) async-start(), calls=%async_computation.5 | async-start | bytes 540672 | tf_op jit(solution)/shard_map/reduce_scatter | solution.py:160
  97.4 5.8 copy-start.7
  97.4 2.1 copy-start.5
  98.6 1.0 copy-start.2
  100.8 266.4 %reduce-scatter.4.cloned.1.call-start = ((), (), s32[]{:S(2)}) async-start(), calls=%async_computation.3 | async-start | bytes 2162688 | tf_op jit(solution)/shard_map/reduce_scatter | solution.py:132
  103.7 1.0 copy-start.6
  105.8 1.4 copy-start.1
  107.2 394.9 %reduce-scatter.6.cloned.1.call-start = ((), (), s32[]{:S(2)}) async-start(), calls=%async_computation.4 | async-start | bytes 2162688 | tf_op jit(solution)/shard_map/reduce_scatter | solution.py:133
  108.8 3.5 copy-start.3
  108.8 3.5 copy-start.11
  111.6 256.5 %copy-start.4 = (bf16[64,4,256]{2,1,0:T(4,128)(2,1)S(1)}, bf16[64,4,256]{2,1,0:T(4,128)(2,1)}, u32[]{:S(2)}) copy-start(bf16[64,4,256]{2,1,0:T(4,128)(2,1)} %param.7) | copy-start | bytes 393220
  111.6 256.5 %copy-start.10 = (f32[256]{0:T(256)S(1)}, f32[256]{0:T(256)}, u32[]{:S(2)}) copy-start(f32[256]{0:T(256)} %param.8) | copy-start | bytes 3076
  111.6 257.4 %copy-start.8 = (bf16[256,32]{0,1:T(8,128)(2,1)S(1)}, bf16[256,32]{0,1:T(8,128)(2,1)}, u32[]{:S(2)}) copy-start(bf16[256,32]{0,1:T(8,128)(2,1)} %param.9) | copy-start | bytes 49156
  111.6 392.2 %copy-start.9 = (bf16[256,32]{0,1:T(8,128)(2,1)S(1)}, bf16[256,32]{0,1:T(8,128)(2,1)}, u32[]{:S(2)}) copy-start(bf16[256,32]{0,1:T(8,128)(2,1)} %param.10) | copy-start | bytes 49156
  111.6 512.9 %all-reduce.3.cloned.1.call-start = ((), (), s32[]{:S(2)}) async-start(), calls=%async_computation.6 | async-start | bytes 134144 | tf_op jit(solution)/shard_map/psum | solution.py:157
Sparse Core Ops, SparseCore 0:
  100.9 131.2 reduce-scatter.7
  234.6 132.5 reduce-scatter.3
  369.5 132.5 reduce-scatter.5
  509.7 114.7 all-reduce.2
where the time goes:
time: 637 us; the launch traced here: 635 us
  waiting for transfers between devices  504 us (79%)
  blocking collectives  85.6 us (13%)
  between operations  14 us (2%)
  matrix products  10.9 us (2%)
  local copies, waits for them, and re-layouts  10 us (2%)
  other arithmetic  9.65 us (2%)
    reduce_scatter x1, waiting for transfers between devices, on_device(): lax.psum_scatter(slotted, 'row', scatter_dimension=1, tiled=True)  134 us
    reduce_scatter x1, waiting for transfers between devices, on_device(): lax.psum_scatter(right_flat, 'row', scatter_dimension=1, tiled=True)  133 us
    psum x1, waiting for transfers between devices, on_device(): lax.psum((left_weight, right_weight, gain_part, bias_part), ('row', 'col'))  119 us
    reduce_scatter x1, waiting for transfers between devices, on_device(): lax.psum_scatter(out_acc, ('row', 'col'), scatter_dimension=0, tiled=True)  119 us
    all_gather x1, blocking collectives, on_device(): lax.all_gather(right_own.reshape(sequence_count, local_residues * hidden)...  46.2 us
    all_gather x1, blocking collectives, on_device(): lax.all_gather(left_own.reshape(sequence_count, local_residues * hidden),...  39.5 us
  transfers between devices with their start and end apart: 4, of which 4 were waited for; matrix products, arithmetic and copies ran while one was open for 2% of the time, Pallas kernels for 0%

commit v1 on v0

--- a/solution.py
+++ b/solution.py
@@ -3,6 +3,8 @@
 import jax
 import jax.numpy as jnp
 from jax import lax
+from jax.experimental import pallas as pl
+from jax.experimental.pallas import tpu as pltpu
 from jax.sharding import PartitionSpec as P
 
 ln_epsilon = 1e-05
@@ -170,6 +172,335 @@
     )
 
 
+f32 = jnp.float32
+bf16 = jnp.bfloat16
+
+
+def mm(a, b):
+    return lax.dot_general(a, b, (((1,), (0,)), ((), ())), preferred_element_type=f32)
+
+
+def mm_t(a, b):
+    return lax.dot_general(a, b, (((1,), (1,)), ((), ())), preferred_element_type=f32)
+
+
+def factor_kernel(
+    x_ref, gain_ref, w1_ref, w2_ref, cot_ref,
+    wire_ref, send_ref, scaled_ref, normed_ref, recip_ref, diag_ref,
+    rows, recips, twin, cots, moved,
+):
+    seqs, res, _ = x_ref.shape
+    hidden = w1_ref.shape[0]
+    columns = cot_ref.shape[1]
+    devices = columns // res
+    x = x_ref[...].astype(f32)
+    centred = x - jnp.mean(x, axis=-1, keepdims=True)
+    recip = lax.rsqrt(jnp.mean(centred * centred, axis=-1, keepdims=True) + ln_epsilon)
+    rows[...] = centred * recip
+    recips[...] = jnp.broadcast_to(recip, recips.shape)
+    both = jnp.concatenate([w1_ref[...], w2_ref[...]], axis=0)
+    low = lax.broadcasted_iota(jnp.int32, (hidden, 2 * seqs), 1) < seqs
+    for r in range(res):
+        scaled = rows[:, r, :]
+        at = slice(r * seqs, (r + 1) * seqs)
+        scaled_ref[at, :] = scaled
+        recip_ref[at, :] = recips[:, r, :]
+        normed = (scaled * gain_ref[...]).astype(bf16)
+        normed_ref[at, :] = normed
+        twin[...] = mm_t(both, jnp.concatenate([normed, normed], axis=0))
+        even = twin[pl.ds(0, hidden, stride=2), :]
+        odd = twin[pl.ds(1, hidden, stride=2), :]
+        wire_ref[r * hidden : (r + 1) * hidden, :] = jnp.where(low, even, odd).astype(bf16)
+        left = twin[:hidden, :]
+        zero = jnp.zeros_like(left)
+        lanes = slice(r * 2 * seqs, (r + 1) * 2 * seqs)
+        diag_ref[:hidden, lanes] = jnp.where(low, left, zero).astype(bf16)
+        diag_ref[hidden:, lanes] = jnp.where(low, zero, left).astype(bf16)
+    for r in range(res):
+        cots[r * columns : (r + 1) * columns, :] = cot_ref[r].astype(f32)
+    for r in range(res):
+        for q in range(res):
+            block = cots[pl.ds(r * columns + q, devices, stride=res), :]
+            moved[pl.ds(r * res + q, devices, stride=res * res), :] = block
+    send_ref[...] = moved[...].astype(bf16)
+
+
+def prepare_kernel(
+    normed_ref, w1_ref, out_w_ref, cot_ref,
+    mixed_ref, cot_t_ref, twin_w_ref, bias_ref,
+    wide,
+):
+    hidden = w1_ref.shape[0]
+    res = cot_ref.shape[0]
+    pairs = out_w_ref.shape[1]
+    seqs = normed_ref.shape[0] // res
+    left = mm_t(normed_ref[...], w1_ref[...]).astype(bf16)
+    wide[...] = out_w_ref[...].astype(f32)
+    for d in range(hidden):
+        w_d = wide[pl.ds(d, hidden, stride=hidden), :].astype(bf16)
+        at = (d % 2) * hidden
+        twin_w_ref[at : at + hidden, (d // 2) * pairs : (d // 2 + 1) * pairs] = w_d
+        mixed = mm(left, w_d).astype(bf16)
+        for r in range(res):
+            mixed_ref[d * seqs : (d + 1) * seqs, r * pairs : (r + 1) * pairs] = mixed[
+                r * seqs : (r + 1) * seqs, :
+            ]
+    total = jnp.zeros((1, pairs), f32)
+    for r in range(res):
+        cot = cot_ref[r].astype(f32)
+        total = total + jnp.sum(cot, axis=0, keepdims=True)
+        cot_t_ref[r * pairs : (r + 1) * pairs, :] = cot.T.astype(bf16)
+    bias_ref[...] = jnp.broadcast_to(total, bias_ref.shape)
+
+
+def pair_kernel(
+    mine_ref, other_ref, mixed_ref, cot_t_ref, twin_w_ref, diag_ref, bias_ref,
+    delta_ref, out_ref, sum_ref, lefts_ref,
+    wide, rights, spread, outs,
+):
+    columns = rights.shape[0]
+    lanes = mine_ref.shape[2]
+    height = mine_ref.shape[1]
+    half = mine_ref.shape[0]
+    res = delta_ref.shape[0]
+    pairs = delta_ref.shape[2]
+    hidden = diag_ref.shape[0] // 2
+    core = lax.rem(lax.axis_index("row"), 2)
+    for b in range(half):
+        device = (b % 4) * 8 + (b // 4) * 2
+        at = pl.multiple_of((device + core) * height, height)
+        wide[pl.ds(at, height), :] = mine_ref[b].astype(f32)
+        at = pl.multiple_of((device + 1 - core) * height, height)
+        wide[pl.ds(at, height), :] = other_ref[b].astype(f32)
+    twins = hidden // 2
+    for q in range(twins):
+        here = slice(q * lanes, (q + 1) * lanes)
+        lefts_ref[:, here] = wide[pl.ds(q, columns, stride=hidden), :].astype(bf16)
+        rights[:, here] = wide[pl.ds(twins + q, columns, stride=hidden), :].astype(bf16)
+    weight = 2.0 / lanes
+    delta = mm(rights[...], mixed_ref[...]) * weight
+    for r in range(res):
+        delta_ref[r] = (delta[:, r * pairs : (r + 1) * pairs] + bias_ref[...]).astype(bf16)
+        block = mm(cot_t_ref[r * pairs : (r + 1) * pairs, :], rights[...]).astype(bf16)
+        for q in range(twins):
+            spread[q * pairs : (q + 1) * pairs, r * lanes : (r + 1) * lanes] = block[
+                :, q * lanes : (q + 1) * lanes
+            ]
+    grad = mm_t(diag_ref[...], spread[...]) * weight
+    for d in range(hidden):
+        at = (d % 2) * hidden
+        outs[pl.ds(d, hidden, stride=hidden), :] = grad[
+            at : at + hidden, (d // 2) * pairs : (d // 2 + 1) * pairs
+        ]
+    for c in range(hidden):
+        place = int(format(c, "05b")[::-1], 2)
+        out_ref[place * hidden : (place + 1) * hidden, :] = outs[
+            c * hidden : (c + 1) * hidden, :
+        ].astype(bf16)
+    sum_ref[...] = mm(twin_w_ref[...], spread[...])
+
+
+def input_kernel(
+    lefts_ref, got_ref, out_w_ref, sum_ref, normed_ref, scaled_ref, recip_ref, gain_ref,
+    w1_ref, w2_ref, bias_ref,
+    grad_ref, small_ref,
+    cots, spread, twin_w, rows,
+):
+    columns = lefts_ref.shape[0]
+    seqs, res, channels = grad_ref.shape
+    pairs = got_ref.shape[1]
+    hidden = w1_ref.shape[0]
+    lanes = 2 * seqs
+    twins = hidden // 2
+    cots[...] = got_ref[...].astype(f32)
+    for q in range(twins):
+        twin_w[:, q * pairs : (q + 1) * pairs] = out_w_ref[q * 2 * hidden : (q + 1) * 2 * hidden, :]
+    for r in range(res):
+        cot_t = cots[pl.ds(r, columns, stride=res), :].T.astype(bf16)
+        block = mm(cot_t, lefts_ref[...]).astype(bf16)
+        for q in range(twins):
+            spread[q * pairs : (q + 1) * pairs, r * lanes : (r + 1) * lanes] = block[
+                :, q * lanes : (q + 1) * lanes
+            ]
+    right_t = mm(twin_w[...], spread[...]).T
+    left_t = sum_ref[...].T
+
+    def untwin(t):
+        parts = [
+            t[r * lanes : r * lanes + seqs, :hidden] + t[r * lanes + seqs : (r + 1) * lanes, hidden:]
+            for r in range(res)
+        ]
+        return jnp.concatenate(parts, axis=0) * (1.0 / seqs)
+
+    left_sum = untwin(left_t)
+    right_sum = untwin(right_t)
+    left_bf = left_sum.astype(bf16)
+    right_bf = right_sum.astype(bf16)
+    normed_grad = mm(left_bf, w1_ref[...]) + mm(right_bf, w2_ref[...])
+    scaled = scaled_ref[...]
+    scaled_grad = normed_grad * gain_ref[...]
+    centre = jnp.mean(scaled_grad, axis=-1, keepdims=True)
+    slope = jnp.mean(scaled_grad * scaled, axis=-1, keepdims=True)
+    grad = recip_ref[:, :1] * (scaled_grad - centre - scaled * slope)
+    for r in range(res):
+        rows[:, r, :] = grad[r * seqs : (r + 1) * seqs, :]
+    grad_ref[...] = rows[...].astype(bf16)
+    factors_t = jnp.concatenate([left_sum, right_sum], axis=1).T.astype(bf16)
+    small_ref[: 2 * hidden, :] = mm(factors_t, normed_ref[...])
+    gain_part = jnp.sum(normed_grad * scaled, axis=0, keepdims=True)
+    bias_part = jnp.concatenate([bias_ref[:1, :]] * (channels // pairs), axis=1)
+    line = lax.broadcasted_iota(jnp.int32, (8, channels), 0)
+    small_ref[2 * hidden :, :] = jnp.where(
+        line == 0, gain_part, jnp.where(line == 1, bias_part, jnp.zeros((8, channels), f32))
+    )
+
+
+def call(kernel, args, outs, scratch, flops, side):
+    moved = sum(a.size * a.dtype.itemsize for a in args)
+    return pl.pallas_call(
+        kernel,
+        out_shape=[jax.ShapeDtypeStruct(s, d) for s, d in outs],
+        in_specs=[pl.BlockSpec(memory_space=pltpu.VMEM)] * len(args),
+        out_specs=[pl.BlockSpec(memory_space=pltpu.VMEM)] * len(outs),
+        scratch_shapes=[pltpu.VMEM(s, d) for s, d in scratch],
+        compiler_params=pltpu.CompilerParams(vmem_limit_bytes=32 * 1024 * 1024),
+        cost_estimate=pl.CostEstimate(flops=flops, bytes_accessed=moved, transcendentals=0),
+        name=side,
+    )(*args)
+
+
+def swap(value, step):
+    count = lax.axis_size("row")
+    return lax.ppermute(value, "row", [(i, i ^ step) for i in range(count)])
+
+
+def gather_digit(value, digit, base, unit):
+    full = jnp.zeros((base,) + value.shape, value.dtype)
+    full = lax.dynamic_update_index_in_dim(full, value, digit, 0)
+    for k in range(1, base):
+        full = lax.dynamic_update_index_in_dim(
+            full, swap(value, k * unit), lax.bitwise_xor(digit, k), 0
+        )
+    return full
+
+
+def on_device_row(
+    homolog_features,
+    standardize_multiplier,
+    first_factor_weights,
+    second_factor_weights,
+    output_projection_matrix,
+    output_bias,
+    pair_cotangent,
+):
+    seqs, res, channels = homolog_features.shape
+    hidden = first_factor_weights.shape[1]
+    pairs = output_projection_matrix.shape[1]
+    count = lax.axis_size("row")
+    columns = res * count
+    index = lax.axis_index("row")
+    z, yx, core = index // 8, index // 2 % 4, index % 2
+    own = seqs * res
+    lanes = 2 * seqs
+    gain = standardize_multiplier.reshape(1, channels)
+    bias = output_bias.reshape(1, pairs)
+    w1, w2 = first_factor_weights.T, second_factor_weights.T
+
+    wire, send, scaled, normed, recip, diag = call(
+        factor_kernel,
+        (homolog_features, gain, w1, w2, pair_cotangent),
+        [
+            ((res * hidden, lanes), bf16),
+            ((res * columns, pairs), bf16),
+            ((own, channels), f32),
+            ((own, channels), bf16),
+            ((own, 128), f32),
+            ((2 * hidden, res * lanes), bf16),
+        ],
+        [
+            ((seqs, res, channels), f32),
+            ((seqs, res, 128), f32),
+            ((2 * hidden, lanes), f32),
+            ((res * columns, pairs), f32),
+            ((res * columns, pairs), f32),
+        ],
+        10**7,
+        "factors",
+    )
+    got = lax.all_to_all(send, "row", 0, 0, tiled=True)
+    plane = gather_digit(wire, z, 4, 8)
+    mine = gather_digit(plane, yx, 4, 2).reshape(count // 2, res * hidden, lanes)
+    other = swap(mine, 1)
+
+    mixed, cot_t, twin_w, bias_part = call(
+        prepare_kernel,
+        (normed, w1, output_projection_matrix, pair_cotangent),
+        [
+            ((hidden * seqs, res * pairs), bf16),
+            ((res * pairs, columns), bf16),
+            ((2 * hidden, hidden // 2 * pairs), bf16),
+            ((8, pairs), f32),
+        ],
+        [((hidden * hidden, pairs), f32)],
+        10**8,
+        "prepare",
+    )
+    delta, out_part, left_part, lefts = call(
+        pair_kernel,
+        (mine, other, mixed, cot_t, twin_w, diag, bias),
+        [
+            ((res, columns, pairs), bf16),
+            ((hidden * hidden, pairs), bf16),
+            ((2 * hidden, res * lanes), f32),
+            ((columns, hidden * seqs), bf16),
+        ],
+        [
+            ((columns * hidden, lanes), f32),
+            ((columns, hidden * seqs), bf16),
+            ((hidden // 2 * pairs, res * lanes), bf16),
+            ((hidden * hidden, pairs), f32),
+        ],
+        10**9,
+        "pairs",
+    )
+    grad, small = call(
+        input_kernel,
+        (
+            lefts, got, output_projection_matrix, left_part, normed, scaled, recip, gain,
+            w1, w2, bias_part,
+        ),
+        [((seqs, res, channels), bf16), ((2 * hidden + 8, channels), f32)],
+        [
+            ((columns * res, pairs), f32),
+            ((hidden // 2 * pairs, res * lanes), bf16),
+            ((2 * hidden, hidden // 2 * pairs), bf16),
+            ((seqs, res, channels), f32),
+        ],
+        10**9,
+        "inputs",
+    )
+    step = 1
+    while step < count:
+        bit = index // step % 2
+        half = out_part.shape[0] // 2
+        keep = lax.dynamic_slice_in_dim(out_part, bit * half, half, 0)
+        give = lax.dynamic_slice_in_dim(out_part, (1 - bit) * half, half, 0)
+        out_part = keep + swap(give, step)
+        small = small + swap(small, step)
+        step *= 2
+    scale = 1.0 / columns
+    small = small * scale
+    return (
+        delta,
+        grad,
+        small[2 * hidden],
+        small[:hidden].T,
+        small[hidden : 2 * hidden].T,
+        out_part.astype(f32) * scale,
+        small[2 * hidden + 1, :pairs],
+    )
+
+
 def solution(mesh):
     in_specs = (P(None, ("col", "row"), None), P(), P(), P(), P(), P(), P("row", "col", None))
     out_specs = (
@@ -181,6 +512,8 @@
         P(("row", "col"), None),
         P(),
     )
+    one_row = mesh.shape["row"] == 32 and mesh.shape["col"] == 1
+    body = on_device_row if one_row else on_device
     return jax.shard_map(
-        on_device, mesh=mesh, in_specs=in_specs, out_specs=out_specs, check_vma=False
-    )
+        body, mesh=mesh, in_specs=in_specs, out_specs=out_specs, check_vma=False
+    )

time: 637 us -> 62.7 us (0.10)
  waiting for transfers between devices: 504 us -> 27.1 us
  blocking collectives: 85.6 us -> 0 us
  starting transfers between devices: 0.16 us -> 19.4 us
  between operations: 14 us -> 0.96 us
  matrix products: 10.9 us -> 0 us
  other arithmetic: 9.65 us -> 0.75 us
  Pallas kernels: 0 us -> 8.21 us
    reduce_scatter x3 -> x0, waiting for transfers between devices: 385 us -> none  [the longest x1 134 us: on_device(): lax.psum_scatter(slotted, 'row', scatter_dimension=1, tiled=True)]
    psum x1 -> x0, waiting for transfers between devices: 119 us -> none  [on_device(): lax.psum((left_weight, right_weight, gain_part, bias_part), ('row', 'col'))]
    all_gather x2 -> x0, blocking collectives: 85.6 us -> none  [the longest x1 46.2 us: on_device(): lax.all_gather(right_own.reshape(sequence_count, local_residues * hidden)...]
    ppermute x0 -> x17, waiting for transfers between devices: none -> 23.8 us  [swap(): return lax.ppermute(value, 'row', [(i, i ^ step) for i in range(count)])]
    ppermute x0 -> x17, starting transfers between devices: none -> 16.8 us  [swap(): return lax.ppermute(value, 'row', [(i, i ^ step) for i in range(count)])]
    dot_general x12 -> x0, matrix products: 10.9 us -> none  [the longest x1 1.54 us: pair_step(): jnp.einsum('ijcd,sic->sjd', outer_grad, left_blk, preferred_element_type=...]
    pallas_call x0 -> x4, Pallas kernels: none -> 8.21 us  [call(): pl.pallas_call(kernel, out_shape=[jax.ShapeDtypeStruct(s, d) for s, d in...]
  transfers between devices with their start and end apart: 4 -> 18, of which waited for: 4 -> 15; matrix products, arithmetic and copies ran while one was open for 2% -> 2% of each run, Pallas kernels for 0% -> 11%
where the time goes in v1:
time: 62.7 us; the launch traced here: 62.3 us
  waiting for transfers between devices  27.1 us (43%)
  starting transfers between devices  19.4 us (31%)
  Pallas kernels  8.21 us (13%)
  local copies, waits for them, and re-layouts  5.96 us (10%)
  between operations  0.96 us (2%)
  other arithmetic  0.75 us (1%)
    ppermute x17, waiting for transfers between devices, swap(): return lax.ppermute(value, 'row', [(i, i ^ step) for i in range(count)])  23.8 us
    ppermute x17, starting transfers between devices, swap(): return lax.ppermute(value, 'row', [(i, i ^ step) for i in range(count)])  16.8 us
    pallas_call x4, Pallas kernels, call(): pl.pallas_call(kernel, out_shape=[jax.ShapeDtypeStruct(s, d) for s, d in...  8.21 us
    unnamed x22, local copies, waits for them, and re-layouts  3.95 us
    all_to_all x1, waiting for transfers between devices, on_device_row(): got = lax.all_to_all(send, 'row', 0, 0, tiled=True)  3.28 us
    all_to_all x1, starting transfers between devices, on_device_row(): got = lax.all_to_all(send, 'row', 0, 0, tiled=True)  2.59 us
  transfers between devices with their start and end apart: 18, of which 15 were waited for; matrix products, arithmetic and copies ran while one was open for 2% of the time, Pallas kernels for 11%

profile of v1, /device:TPU:0, one launch (start us, length us, event | category | flops | bytes accessed | tf_op | source)
XLA Modules:
  0.0 62.3 jit_solution(17997361842581697110)
XLA Ops:
  0.7 0.9 %copy-done = bf16[4,128,128]{2,1,0:T(8,128)(2,1)S(1)} copy-done((bf16[4,128,128]{2,1,0:T(8,128)(2,1)S(1)}, bf16[4,128,128]{2,1,0:T(8,128)(2,1)}, u32[]{:S(2)}) %copy-start) | copy-done | bytes 131096
  1.6 0.9 %copy-done.3 = bf16[64,4,256]{2,1,0:T(4,128)(2,1)S(1)} copy-done((bf16[64,4,256]{2,1,0:T(4,128)(2,1)S(1)}, bf16[64,4,256]{2,1,0:T(4,128)(2,1)}, u32[]{:S(2)}) %copy-start.3) | copy-done | bytes 131096
  2.5 0.7 %copy-done.4 = bf16[256,32]{0,1:T(8,128)(2,1)S(1)} copy-done((bf16[256,32]{0,1:T(8,128)(2,1)S(1)}, bf16[256,32]{0,1:T(8,128)(2,1)}, u32[]{:S(2)}) %copy-start.4) | copy-done | bytes 16408
  3.2 0.7 %copy-done.6 = bf16[256,32]{0,1:T(8,128)(2,1)S(1)} copy-done((bf16[256,32]{0,1:T(8,128)(2,1)S(1)}, bf16[256,32]{0,1:T(8,128)(2,1)}, u32[]{:S(2)}) %copy-start.6) | copy-done | bytes 16408
  3.9 0.7 %copy-done.8 = f32[256]{0:T(256)S(1)} copy-done((f32[256]{0:T(256)S(1)}, f32[256]{0:T(256)}, u32[]{:S(2)}) %copy-start.8) | copy-done | bytes 1048
  4.6 1.3 %factors.1 = (bf16[128,128]{1,0:T(8,128)(2,1)S(1)}, bf16[512,128]{1,0:T(8,128)(2,1)}, f32[256,256]{1,0:T(8,128)S(1)}, bf16[256,256]{1,0:T(8,128)(2,1)S(1)}, f32[...) custom-call(bf16[64,4,256]{2,1,0:T(4,128)(2,1)S(1)} %copy-done.3, f32[1,256]{1,0:T(1,128)S(1)} %bitcast.38, ...), custom_call_target="tpu_custom_call" | custom-call | flops 10000000 | bytes 295936 | tf_op jit(solution)/shard_map/factors/pallas_call | solution.py:360
  5.9 3.0 %collective-permute-start = (bf16[128,128]{1,0:T(8,128)(2,1)S(1)}, bf16[128,128]{1,0:T(8,128)(2,1)S(1)}, u32[]{:S(2)}, u32[]{:S(2)}) collective-permute-start(bf16[128,128]{1,0:T(8,128)(2,1)S(1)} %get-tuple-element.23), channel_id=1, source_target_pairs={{0,8},{1,9},{2,10},{3,11},{4,12},{5,13},{6,14},{7,15},{8,0},{9,1},... | collective-permute-start | bytes 98312 | tf_op jit(solution)/shard_map/ppermute | solution.py:374
  8.9 2.6 %collective-permute-start.1 = (bf16[128,128]{1,0:T(8,128)(2,1)S(1)}, bf16[128,128]{1,0:T(8,128)(2,1)S(1)}, u32[]{:S(2)}, u32[]{:S(2)}) collective-permute-start(bf16[128,128]{1,0:T(8,128)(2,1)S(1)} %get-tuple-element.23), channel_id=1, source_target_pairs={{0,16},{1,17},{2,18},{3,19},{4,20},{5,21},{6,22},{7,23},{8,24},{9,... | collective-permute-start | bytes 98312 | tf_op jit(solution)/shard_map/ppermute | solution.py:374
  11.6 2.7 %collective-permute-done.1 = bf16[128,128]{1,0:T(8,128)(2,1)S(1)} collective-permute-done((bf16[128,128]{1,0:T(8,128)(2,1)S(1)}, bf16[128,128]{1,0:T(8,128)(2,1)S(1)}, u32[]{:S(2)}, u32[]{:S(2)}) %collective-permute-start.1) | collective-permute-done | bytes 32800 | tf_op jit(solution)/shard_map/ppermute | solution.py:374
  14.3 2.9 %collective-permute-done.2 = bf16[128,128]{1,0:T(8,128)(2,1)S(1)} collective-permute-done((bf16[128,128]{1,0:T(8,128)(2,1)S(1)}, bf16[128,128]{1,0:T(8,128)(2,1)S(1)}, u32[]{:S(2)}, u32[]{:S(2)}) %collective-permute-start.2) | collective-permute-done | bytes 32800 | tf_op jit(solution)/shard_map/ppermute | solution.py:374
  17.2 1.5 %collective-permute-start.3 = (bf16[4,128,128]{2,1,0:T(8,128)(2,1)S(1)}, bf16[4,128,128]{2,1,0:T(8,128)(2,1)S(1)}, u32[]{:S(2)}, u32[]{:S(2)}) collective-permute-start(bf16[4,128,128]{2,1,0:T(8,128)(2,1)S(1)} %bitcast_dynamic-update-slice_fusion.4), channel_id=1, source_target_pairs={{0,2},{1,3},{2,0},{3,1},{4,6},{5,7},{6,4},{7,5},{8,10},{9,11},{10,... | collective-permute-start | bytes 393224 | tf_op jit(solution)/shard_map/ppermute | solution.py:374
  18.7 1.5 %collective-permute-start.4 = (bf16[4,128,128]{2,1,0:T(8,128)(2,1)S(1)}, bf16[4,128,128]{2,1,0:T(8,128)(2,1)S(1)}, u32[]{:S(2)}, u32[]{:S(2)}) collective-permute-start(bf16[4,128,128]{2,1,0:T(8,128)(2,1)S(1)} %bitcast_dynamic-update-slice_fusion.4), channel_id=1, source_target_pairs={{0,4},{1,5},{2,6},{3,7},{4,0},{5,1},{6,2},{7,3},{8,12},{9,13},{10,... | collective-permute-start | bytes 393224 | tf_op jit(solution)/shard_map/ppermute | solution.py:374
  20.8 2.4 %collective-permute-done.3 = bf16[4,128,128]{2,1,0:T(8,128)(2,1)S(1)} collective-permute-done((bf16[4,128,128]{2,1,0:T(8,128)(2,1)S(1)}, bf16[4,128,128]{2,1,0:T(8,128)(2,1)S(1)}, u32[]{:S(2)}, u32[]{:S(2)}) %collective-permute-start.3) | collective-permute-done | bytes 131104 | tf_op jit(solution)/shard_map/ppermute | solution.py:374
  23.2 1.2 %collective-permute-done.4 = bf16[4,128,128]{2,1,0:T(8,128)(2,1)S(1)} collective-permute-done((bf16[4,128,128]{2,1,0:T(8,128)(2,1)S(1)}, bf16[4,128,128]{2,1,0:T(8,128)(2,1)S(1)}, u32[]{:S(2)}, u32[]{:S(2)}) %collective-permute-start.4) | collective-permute-done | bytes 131104 | tf_op jit(solution)/shard_map/ppermute | solution.py:374
  24.5 1.6 %collective-permute-done.5 = bf16[4,128,128]{2,1,0:T(8,128)(2,1)S(1)} collective-permute-done((bf16[4,128,128]{2,1,0:T(8,128)(2,1)S(1)}, bf16[4,128,128]{2,1,0:T(8,128)(2,1)S(1)}, u32[]{:S(2)}, u32[]{:S(2)}) %collective-permute-start.5) | collective-permute-done | bytes 131104 | tf_op jit(solution)/shard_map/ppermute | solution.py:374
  26.2 2.6 %all-to-all-start = ((bf16[32,16,128]{2,1,0:T(8,128)(2,1)}), bf16[32,16,128]{2,1,0:T(8,128)(2,1)S(1)}, u32[]{:S(2)}, u32[]{:S(2)}) async-start(bf16[32,16,128]{2,1,0:T(8,128)(2,1)} %bitcast.13), calls=%async_computation | async-start | bytes 262144 | tf_op jit(solution)/shard_map/all_to_all | solution.py:430
  28.8 0.9 %prepare.1 = (bf16[2048,512]{1,0:T(8,128)(2,1)S(1)}, bf16[512,128]{1,0:T(8,128)(2,1)S(1)}, bf16[64,2048]{1,0:T(8,128)(2,1)S(1)}, f32[8,128]{1,0:T(8,128)S(1)}) custom-call(bf16[256,256]{1,0:T(8,128)(2,1)S(1)} %get-tuple-element.24.normed_ref, bf16[32,256]{1,0:T(8,128)(2,1)S(1)} %bitcast.34, bf16[1024,128]{1,0:T(8,128)(2,1)S(1)} %copy-done.2, ...), custom_call_target="tpu_custom_call" | custom-call | flops 100000000 | bytes 540672 | tf_op jit(solution)/shard_map/prepare/pallas_call | solution.py:360
  29.8 3.6 %pairs.1 = (bf16[4,128,128]{2,1,0:T(8,128)(2,1)}, bf16[1024,128]{1,0:T(8,128)(2,1)S(1)}, f32[64,512]{1,0:T(8,128)S(1)}, bf16[128,2048]{1,0:T(8,128)(2,1)S(1)}) custom-call(bf16[16,128,128]{2,1,0:T(8,128)(2,1)S(1)} %bitcast.31, bf16[16,128,128]{2,1,0:T(8,128)(2,1)S(1)} %collective-permute-done.6.other_ref, bf16[2048,512]{1,0:T(8,128)(2,1)S(1)} %get-tuple-element.25.mixed_ref, ...), custom_call_target="tpu_custom_call" | custom-call | flops 1000000000 | bytes 3604992 | tf_op jit(solution)/shard_map/pairs/pallas_call | solution.py:360
  33.7 3.3 %all-to-all-done = bf16[32,16,128]{2,1,0:T(8,128)(2,1)S(1)} async-done(((bf16[32,16,128]{2,1,0:T(8,128)(2,1)}), bf16[32,16,128]{2,1,0:T(8,128)(2,1)S(1)}, u32[]{:S(2)}, u32[]{:S(2)}) %all-to-all-start) | async-done | bytes 131104 | tf_op jit(solution)/shard_map/all_to_all | solution.py:430
  37.0 2.4 %inputs.1 = (bf16[64,4,256]{2,1,0:T(4,128)(2,1)}, f32[72,256]{1,0:T(8,128)S(1)}) custom-call(bf16[128,2048]{1,0:T(8,128)(2,1)S(1)} %get-tuple-element.30.lefts_ref, bf16[512,128]{1,0:T(8,128)(2,1)S(1)} %bitcast.32, bf16[1024,128]{1,0:T(8,128)(2,1)S(1)} %copy-done.2, f32[64,512]{1,0:T(8,128)S(1)} %get-tuple-element.32.sum_ref, ...), custom_call_target="tpu_custom_call" | custom-call | flops 1000000000 | bytes 1610752 | tf_op jit(solution)/shard_map/inputs/pallas_call | solution.py:360
  40.7 1.2 %collective-permute-start.8 = (f32[72,256]{1,0:T(8,128)S(1)}, f32[72,256]{1,0:T(8,128)S(1)}, u32[]{:S(2)}, u32[]{:S(2)}) collective-permute-start(f32[72,256]{1,0:T(8,128)S(1)} %add.119), channel_id=1, source_target_pairs={{0,2},{1,3},{2,0},{3,1},{4,6},{5,7},{6,4},{7,5},{8,10},{9,11},{10,... | collective-permute-start | bytes 221192 | tf_op jit(solution)/shard_map/ppermute | solution.py:374
  41.9 2.7 %collective-permute-done.13 = bf16[256,128]{1,0:T(8,128)(2,1)S(1)} collective-permute-done((bf16[256,128]{1,0:T(8,128)(2,1)S(1)}, bf16[256,128]{1,0:T(8,128)(2,1)S(1)}, u32[]{:S(2)}, u32[]{:S(2)}) %collective-permute-start.13) | collective-permute-done | bytes 65568 | tf_op jit(solution)/shard_map/ppermute | solution.py:374
  44.6 0.6 %collective-permute-start.14 = (bf16[128,128]{1,0:T(8,128)(2,1)S(1)}, bf16[128,128]{1,0:T(8,128)(2,1)S(1)}, u32[]{:S(2)}, u32[]{:S(2)}) collective-permute-start(bf16[128,128]{1,0:T(8,128)(2,1)S(1)} %constant_dynamic-slice_fusion.2), channel_id=1, source_target_pairs={{0,4},{1,5},{2,6},{3,7},{4,0},{5,1},{6,2},{7,3},{8,12},{9,13},{10,... | collective-permute-start | bytes 98312 | tf_op jit(solution)/shard_map/ppermute | solution.py:374
  45.6 1.1 %collective-permute-start.9 = (f32[72,256]{1,0:T(8,128)S(1)}, f32[72,256]{1,0:T(8,128)S(1)}, u32[]{:S(2)}, u32[]{:S(2)}) collective-permute-start(f32[72,256]{1,0:T(8,128)S(1)} %add.120), channel_id=1, source_target_pairs={{0,4},{1,5},{2,6},{3,7},{4,0},{5,1},{6,2},{7,3},{8,12},{9,13},{10,... | collective-permute-start | bytes 221192 | tf_op jit(solution)/shard_map/ppermute | solution.py:374
  46.7 2.2 %collective-permute-done.14 = bf16[128,128]{1,0:T(8,128)(2,1)S(1)} collective-permute-done((bf16[128,128]{1,0:T(8,128)(2,1)S(1)}, bf16[128,128]{1,0:T(8,128)(2,1)S(1)}, u32[]{:S(2)}, u32[]{:S(2)}) %collective-permute-start.14) | collective-permute-done | bytes 32800 | tf_op jit(solution)/shard_map/ppermute | solution.py:374
  50.1 1.0 %collective-permute-start.10 = (f32[72,256]{1,0:T(8,128)S(1)}, f32[72,256]{1,0:T(8,128)S(1)}, u32[]{:S(2)}, u32[]{:S(2)}) collective-permute-start(f32[72,256]{1,0:T(8,128)S(1)} %add.121), channel_id=1, source_target_pairs={{0,8},{1,9},{2,10},{3,11},{4,12},{5,13},{6,14},{7,15},{8,0},{9,1},... | collective-permute-start | bytes 221192 | tf_op jit(solution)/shard_map/ppermute | solution.py:374
  51.1 1.6 %collective-permute-done.15 = bf16[64,128]{1,0:T(8,128)(2,1)S(1)} collective-permute-done((bf16[64,128]{1,0:T(8,128)(2,1)S(1)}, bf16[64,128]{1,0:T(8,128)(2,1)S(1)}, u32[]{:S(2)}, u32[]{:S(2)}) %collective-permute-start.15) | collective-permute-done | bytes 16416 | tf_op jit(solution)/shard_map/ppermute | solution.py:374
  52.8 0.7 %collective-permute-start.16 = (bf16[32,128]{1,0:T(8,128)(2,1)S(1)}, bf16[32,128]{1,0:T(8,128)(2,1)S(1)}, u32[]{:S(2)}, u32[]{:S(2)}) collective-permute-start(bf16[32,128]{1,0:T(8,128)(2,1)S(1)} %constant_dynamic-slice_fusion), channel_id=1, source_target_pairs={{0,16},{1,17},{2,18},{3,19},{4,20},{5,21},{6,22},{7,23},{8,24},{9,... | collective-permute-start | bytes 24584 | tf_op jit(solution)/shard_map/ppermute | solution.py:374
  53.5 1.0 %collective-permute-done.10 = f32[72,256]{1,0:T(8,128)S(1)} collective-permute-done((f32[72,256]{1,0:T(8,128)S(1)}, f32[72,256]{1,0:T(8,128)S(1)}, u32[]{:S(2)}, u32[]{:S(2)}) %collective-permute-start.10) | collective-permute-done | bytes 73760 | tf_op jit(solution)/shard_map/ppermute | solution.py:374
  54.5 1.3 %collective-permute-start.11 = (f32[72,256]{1,0:T(8,128)S(1)}, f32[72,256]{1,0:T(8,128)S(1)}, u32[]{:S(2)}, u32[]{:S(2)}) collective-permute-start(f32[72,256]{1,0:T(8,128)S(1)} %add.122), channel_id=1, source_target_pairs={{0,16},{1,17},{2,18},{3,19},{4,20},{5,21},{6,22},{7,23},{8,24},{9,... | collective-permute-start | bytes 221192 | tf_op jit(solution)/shard_map/ppermute | solution.py:374
  55.8 1.8 %collective-permute-done.16 = bf16[32,128]{1,0:T(8,128)(2,1)S(1)} collective-permute-done((bf16[32,128]{1,0:T(8,128)(2,1)S(1)}, bf16[32,128]{1,0:T(8,128)(2,1)S(1)}, u32[]{:S(2)}, u32[]{:S(2)}) %collective-permute-start.16) | collective-permute-done | bytes 8224 | tf_op jit(solution)/shard_map/ppermute | solution.py:374
  58.2 2.4 %collective-permute-done.11 = f32[72,256]{1,0:T(8,128)S(1)} collective-permute-done((f32[72,256]{1,0:T(8,128)S(1)}, f32[72,256]{1,0:T(8,128)S(1)}, u32[]{:S(2)}, u32[]{:S(2)}) %collective-permute-start.11) | collective-permute-done | bytes 73760 | tf_op jit(solution)/shard_map/ppermute | solution.py:374
  (58 shorter events, 6.4 us)
Async XLA Ops:
  0.6 29.1 %copy-start.10 = (f32[128]{0:T(128)S(1)}, f32[128]{0:T(128)}, u32[]{:S(2)}) copy-start(f32[128]{0:T(128)} %param.12) | copy-start | bytes 1540
  0.6 0.9 %copy-start = (bf16[4,128,128]{2,1,0:T(8,128)(2,1)S(1)}, bf16[4,128,128]{2,1,0:T(8,128)(2,1)}, u32[]{:S(2)}) copy-start(bf16[4,128,128]{2,1,0:T(8,128)(2,1)} %cot_ref.3) | copy-start | bytes 393220
  1.6 0.9 %copy-start.3 = (bf16[64,4,256]{2,1,0:T(4,128)(2,1)S(1)}, bf16[64,4,256]{2,1,0:T(4,128)(2,1)}, u32[]{:S(2)}) copy-start(bf16[64,4,256]{2,1,0:T(4,128)(2,1)} %x_ref.1) | copy-start | bytes 393220
  2.5 0.7 %copy-start.4 = (bf16[256,32]{0,1:T(8,128)(2,1)S(1)}, bf16[256,32]{0,1:T(8,128)(2,1)}, u32[]{:S(2)}) copy-start(bf16[256,32]{0,1:T(8,128)(2,1)} %param.9) | copy-start | bytes 49156
  3.2 0.7 %copy-start.6 = (bf16[256,32]{0,1:T(8,128)(2,1)S(1)}, bf16[256,32]{0,1:T(8,128)(2,1)}, u32[]{:S(2)}) copy-start(bf16[256,32]{0,1:T(8,128)(2,1)} %param.10) | copy-start | bytes 49156
  3.9 0.7 %copy-start.8 = (f32[256]{0:T(256)S(1)}, f32[256]{0:T(256)}, u32[]{:S(2)}) copy-start(f32[256]{0:T(256)} %param.8) | copy-start | bytes 3076
  4.6 24.2 %copy-start.1 = (bf16[4,128,128]{2,1,0:T(8,128)(2,1)S(1)}, bf16[4,128,128]{2,1,0:T(8,128)(2,1)}, u32[]{:S(2)}) copy-start(bf16[4,128,128]{2,1,0:T(8,128)(2,1)} %cot_ref.3) | copy-start | bytes 393220
  4.6 24.2 %copy-start.2 = (bf16[1024,128]{1,0:T(8,128)(2,1)S(1)}, bf16[1024,128]{1,0:T(8,128)(2,1)}, u32[]{:S(2)}) copy-start(bf16[1024,128]{1,0:T(8,128)(2,1)} %out_w_ref.3) | copy-start | bytes 786436
  4.6 24.2 %copy-start.5 = (bf16[256,32]{0,1:T(8,128)(2,1)S(1)}, bf16[256,32]{0,1:T(8,128)(2,1)}, u32[]{:S(2)}) copy-start(bf16[256,32]{0,1:T(8,128)(2,1)} %param.9) | copy-start | bytes 49156
  5.9 5.7 %collective-permute-start = (bf16[128,128]{1,0:T(8,128)(2,1)S(1)}, bf16[128,128]{1,0:T(8,128)(2,1)S(1)}, u32[]{:S(2)}, u32[]{:S(2)}) collective-permute-start(bf16[128,128]{1,0:T(8,128)(2,1)S(1)} %get-tuple-element.23), channel_id=1, source_target_pairs={{0,8},{1,9},{2,10},{3,11},{4,12},{5,13},{6,14},{7,15},{8,0},{9,1},... | collective-permute-start | bytes 98312 | tf_op jit(solution)/shard_map/ppermute | solution.py:374
  8.9 5.4 %collective-permute-start.1 = (bf16[128,128]{1,0:T(8,128)(2,1)S(1)}, bf16[128,128]{1,0:T(8,128)(2,1)S(1)}, u32[]{:S(2)}, u32[]{:S(2)}) collective-permute-start(bf16[128,128]{1,0:T(8,128)(2,1)S(1)} %get-tuple-element.23), channel_id=1, source_target_pairs={{0,16},{1,17},{2,18},{3,19},{4,20},{5,21},{6,22},{7,23},{8,24},{9,... | collective-permute-start | bytes 98312 | tf_op jit(solution)/shard_map/ppermute | solution.py:374
  11.5 5.7 %collective-permute-start.2 = (bf16[128,128]{1,0:T(8,128)(2,1)S(1)}, bf16[128,128]{1,0:T(8,128)(2,1)S(1)}, u32[]{:S(2)}, u32[]{:S(2)}) collective-permute-start(bf16[128,128]{1,0:T(8,128)(2,1)S(1)} %get-tuple-element.23), channel_id=1, source_target_pairs={{0,24},{1,25},{2,26},{3,27},{4,28},{5,29},{6,30},{7,31},{8,16},{9,... | collective-permute-start | bytes 98312 | tf_op jit(solution)/shard_map/ppermute | solution.py:374
  17.2 6.0 %collective-permute-start.3 = (bf16[4,128,128]{2,1,0:T(8,128)(2,1)S(1)}, bf16[4,128,128]{2,1,0:T(8,128)(2,1)S(1)}, u32[]{:S(2)}, u32[]{:S(2)}) collective-permute-start(bf16[4,128,128]{2,1,0:T(8,128)(2,1)S(1)} %bitcast_dynamic-update-slice_fusion.4), channel_id=1, source_target_pairs={{0,2},{1,3},{2,0},{3,1},{4,6},{5,7},{6,4},{7,5},{8,10},{9,11},{10,... | collective-permute-start | bytes 393224 | tf_op jit(solution)/shard_map/ppermute | solution.py:374
  18.7 5.8 %collective-permute-start.4 = (bf16[4,128,128]{2,1,0:T(8,128)(2,1)S(1)}, bf16[4,128,128]{2,1,0:T(8,128)(2,1)S(1)}, u32[]{:S(2)}, u32[]{:S(2)}) collective-permute-start(bf16[4,128,128]{2,1,0:T(8,128)(2,1)S(1)} %bitcast_dynamic-update-slice_fusion.4), channel_id=1, source_target_pairs={{0,4},{1,5},{2,6},{3,7},{4,0},{5,1},{6,2},{7,3},{8,12},{9,13},{10,... | collective-permute-start | bytes 393224 | tf_op jit(solution)/shard_map/ppermute | solution.py:374
  20.2 5.9 %collective-permute-start.5 = (bf16[4,128,128]{2,1,0:T(8,128)(2,1)S(1)}, bf16[4,128,128]{2,1,0:T(8,128)(2,1)S(1)}, u32[]{:S(2)}, u32[]{:S(2)}) collective-permute-start(bf16[4,128,128]{2,1,0:T(8,128)(2,1)S(1)} %bitcast_dynamic-update-slice_fusion.4), channel_id=1, source_target_pairs={{0,6},{1,7},{2,4},{3,5},{4,2},{5,3},{6,0},{7,1},{8,14},{9,15},{10,... | collective-permute-start | bytes 393224 | tf_op jit(solution)/shard_map/ppermute | solution.py:374
  26.1 3.7 %collective-permute-start.6 = (bf16[16,128,128]{2,1,0:T(8,128)(2,1)S(1)}, bf16[16,128,128]{2,1,0:T(8,128)(2,1)S(1)}, u32[]{:S(2)}, u32[]{:S(2)}) collective-permute-start(bf16[16,128,128]{2,1,0:T(8,128)(2,1)S(1)} %bitcast.30), channel_id=1, source_target_pairs={{0,1},{1,0},{2,3},{3,2},{4,5},{5,4},{6,7},{7,6},{8,9},{9,8},{10,11... | collective-permute-start | bytes 1572872 | tf_op jit(solution)/shard_map/ppermute | solution.py:374
  26.2 10.8 %all-to-all-start = ((bf16[32,16,128]{2,1,0:T(8,128)(2,1)}), bf16[32,16,128]{2,1,0:T(8,128)(2,1)S(1)}, u32[]{:S(2)}, u32[]{:S(2)}) async-start(bf16[32,16,128]{2,1,0:T(8,128)(2,1)} %bitcast.13), calls=%async_computation | async-start | bytes 262144 | tf_op jit(solution)/shard_map/all_to_all | solution.py:430
  29.7 7.3 %copy-start.7 = (bf16[256,32]{0,1:T(8,128)(2,1)S(1)}, bf16[256,32]{0,1:T(8,128)(2,1)}, u32[]{:S(2)}) copy-start(bf16[256,32]{0,1:T(8,128)(2,1)} %param.10) | copy-start | bytes 49156
  29.7 7.3 %copy-start.9 = (f32[256]{0:T(256)S(1)}, f32[256]{0:T(256)}, u32[]{:S(2)}) copy-start(f32[256]{0:T(256)} %param.8) | copy-start | bytes 3076
  33.5 6.2 %collective-permute-start.12 = (bf16[512,128]{1,0:T(8,128)(2,1)S(1)}, bf16[512,128]{1,0:T(8,128)(2,1)S(1)}, u32[]{:S(2)}, u32[]{:S(2)}) collective-permute-start(bf16[512,128]{1,0:T(8,128)(2,1)S(1)} %constant_dynamic-slice_fusion.4), channel_id=1, source_target_pairs={{0,1},{1,0},{2,3},{3,2},{4,5},{5,4},{6,7},{7,6},{8,9},{9,8},{10,11... | collective-permute-start | bytes 393224 | tf_op jit(solution)/shard_map/ppermute | solution.py:374
  39.4 1.3 %collective-permute-start.7 = (f32[72,256]{1,0:T(8,128)S(1)}, f32[72,256]{1,0:T(8,128)S(1)}, u32[]{:S(2)}, u32[]{:S(2)}) collective-permute-start(f32[72,256]{1,0:T(8,128)S(1)} %get-tuple-element.37), channel_id=1, source_target_pairs={{0,1},{1,0},{2,3},{3,2},{4,5},{5,4},{6,7},{7,6},{8,9},{9,8},{10,11... | collective-permute-start | bytes 221192 | tf_op jit(solution)/shard_map/ppermute | solution.py:374
  39.7 4.8 %collective-permute-start.13 = (bf16[256,128]{1,0:T(8,128)(2,1)S(1)}, bf16[256,128]{1,0:T(8,128)(2,1)S(1)}, u32[]{:S(2)}, u32[]{:S(2)}) collective-permute-start(bf16[256,128]{1,0:T(8,128)(2,1)S(1)} %constant_dynamic-slice_fusion.3), channel_id=1, source_target_pairs={{0,2},{1,3},{2,0},{3,1},{4,6},{5,7},{6,4},{7,5},{8,10},{9,11},{10,... | collective-permute-start | bytes 196616 | tf_op jit(solution)/shard_map/ppermute | solution.py:374
  40.7 4.9 %collective-permute-start.8 = (f32[72,256]{1,0:T(8,128)S(1)}, f32[72,256]{1,0:T(8,128)S(1)}, u32[]{:S(2)}, u32[]{:S(2)}) collective-permute-start(f32[72,256]{1,0:T(8,128)S(1)} %add.119), channel_id=1, source_target_pairs={{0,2},{1,3},{2,0},{3,1},{4,6},{5,7},{6,4},{7,5},{8,10},{9,11},{10,... | collective-permute-start | bytes 221192 | tf_op jit(solution)/shard_map/ppermute | solution.py:374
  44.6 4.3 %collective-permute-start.14 = (bf16[128,128]{1,0:T(8,128)(2,1)S(1)}, bf16[128,128]{1,0:T(8,128)(2,1)S(1)}, u32[]{:S(2)}, u32[]{:S(2)}) collective-permute-start(bf16[128,128]{1,0:T(8,128)(2,1)S(1)} %constant_dynamic-slice_fusion.2), channel_id=1, source_target_pairs={{0,4},{1,5},{2,6},{3,7},{4,0},{5,1},{6,2},{7,3},{8,12},{9,13},{10,... | collective-permute-start | bytes 98312 | tf_op jit(solution)/shard_map/ppermute | solution.py:374
  45.6 4.4 %collective-permute-start.9 = (f32[72,256]{1,0:T(8,128)S(1)}, f32[72,256]{1,0:T(8,128)S(1)}, u32[]{:S(2)}, u32[]{:S(2)}) collective-permute-start(f32[72,256]{1,0:T(8,128)S(1)} %add.120), channel_id=1, source_target_pairs={{0,4},{1,5},{2,6},{3,7},{4,0},{5,1},{6,2},{7,3},{8,12},{9,13},{10,... | collective-permute-start | bytes 221192 | tf_op jit(solution)/shard_map/ppermute | solution.py:374
  48.9 3.8 %collective-permute-start.15 = (bf16[64,128]{1,0:T(8,128)(2,1)S(1)}, bf16[64,128]{1,0:T(8,128)(2,1)S(1)}, u32[]{:S(2)}, u32[]{:S(2)}) collective-permute-start(bf16[64,128]{1,0:T(8,128)(2,1)S(1)} %constant_dynamic-slice_fusion.1), channel_id=1, source_target_pairs={{0,8},{1,9},{2,10},{3,11},{4,12},{5,13},{6,14},{7,15},{8,0},{9,1},... | collective-permute-start | bytes 49160 | tf_op jit(solution)/shard_map/ppermute | solution.py:374
  50.1 4.4 %collective-permute-start.10 = (f32[72,256]{1,0:T(8,128)S(1)}, f32[72,256]{1,0:T(8,128)S(1)}, u32[]{:S(2)}, u32[]{:S(2)}) collective-permute-start(f32[72,256]{1,0:T(8,128)S(1)} %add.121), channel_id=1, source_target_pairs={{0,8},{1,9},{2,10},{3,11},{4,12},{5,13},{6,14},{7,15},{8,0},{9,1},... | collective-permute-start | bytes 221192 | tf_op jit(solution)/shard_map/ppermute | solution.py:374
  52.8 4.8 %collective-permute-start.16 = (bf16[32,128]{1,0:T(8,128)(2,1)S(1)}, bf16[32,128]{1,0:T(8,128)(2,1)S(1)}, u32[]{:S(2)}, u32[]{:S(2)}) collective-permute-start(bf16[32,128]{1,0:T(8,128)(2,1)S(1)} %constant_dynamic-slice_fusion), channel_id=1, source_target_pairs={{0,16},{1,17},{2,18},{3,19},{4,20},{5,21},{6,22},{7,23},{8,24},{9,... | collective-permute-start | bytes 24584 | tf_op jit(solution)/shard_map/ppermute | solution.py:374
  54.5 6.1 %collective-permute-start.11 = (f32[72,256]{1,0:T(8,128)S(1)}, f32[72,256]{1,0:T(8,128)S(1)}, u32[]{:S(2)}, u32[]{:S(2)}) collective-permute-start(f32[72,256]{1,0:T(8,128)S(1)} %add.122), channel_id=1, source_target_pairs={{0,16},{1,17},{2,18},{3,19},{4,20},{5,21},{6,22},{7,23},{8,24},{9,... | collective-permute-start | bytes 221192 | tf_op jit(solution)/shard_map/ppermute | solution.py:374

commit v2 on v0

--- a/solution.py
+++ b/solution.py
@@ -1,8 +1,11 @@
+import functools
 import math
 
 import jax
 import jax.numpy as jnp
 from jax import lax
+from jax.experimental import pallas as pl
+from jax.experimental.pallas import tpu as pltpu
 from jax.sharding import PartitionSpec as P
 
 ln_epsilon = 1e-05
@@ -170,6 +173,431 @@
     )
 
 
+f32 = jnp.float32
+bf16 = jnp.bfloat16
+
+
+def mm(a, b):
+    return lax.dot_general(a, b, (((1,), (0,)), ((), ())), preferred_element_type=f32)
+
+
+def mm_t(a, b):
+    return lax.dot_general(a, b, (((1,), (1,)), ((), ())), preferred_element_type=f32)
+
+
+def fetch(pairs, sems):
+    copies = [pltpu.make_async_copy(a, b, sems.at[n]) for n, (a, b) in enumerate(pairs)]
+    for copy in copies:
+        copy.start()
+    return copies
+
+
+def factor_kernel(
+    x_hbm, gain_hbm, w1_hbm, w2_hbm, cot_hbm,
+    send0_ref, send1_ref, send2_ref, send3_ref, scaled_ref, normed_ref, recip_ref, diag_ref,
+    x_ref, gain_ref, w1_ref, w2_ref, cot_ref, rows, recips, twin, cots, moved, sems,
+):
+    copies = fetch(
+        [(x_hbm, x_ref), (gain_hbm, gain_ref), (w1_hbm, w1_ref), (w2_hbm, w2_ref), (cot_hbm, cot_ref)],
+        sems,
+    )
+    sends = (send0_ref, send1_ref, send2_ref, send3_ref)
+    seqs, res, _ = x_ref.shape
+    hidden = w1_ref.shape[0]
+    columns = cot_ref.shape[1]
+    devices = columns // res
+    copies[0].wait()
+    x = x_ref[...].astype(f32)
+    centred = x - jnp.mean(x, axis=-1, keepdims=True)
+    recip = lax.rsqrt(jnp.mean(centred * centred, axis=-1, keepdims=True) + ln_epsilon)
+    rows[...] = centred * recip
+    recips[...] = jnp.broadcast_to(recip, recips.shape)
+    for copy in copies[1:]:
+        copy.wait()
+    both = jnp.concatenate([w1_ref[...], w2_ref[...]], axis=0)
+    low = lax.broadcasted_iota(jnp.int32, (hidden, 2 * seqs), 1) < seqs
+    for r in range(res):
+        scaled = rows[:, r, :]
+        at = slice(r * seqs, (r + 1) * seqs)
+        scaled_ref[at, :] = scaled
+        recip_ref[at, :] = recips[:, r, :]
+        normed = (scaled * gain_ref[...]).astype(bf16)
+        normed_ref[at, :] = normed
+        twin[r] = mm_t(both, jnp.concatenate([normed, normed], axis=0))
+        even = twin[r, pl.ds(0, hidden, stride=2), :]
+        odd = twin[r, pl.ds(1, hidden, stride=2), :]
+        piece = jnp.where(low, even, odd).astype(bf16)
+        for send_ref in sends:
+            send_ref[r * hidden : (r + 1) * hidden, :] = piece
+        left = twin[r, :hidden, :]
+        zero = jnp.zeros_like(left)
+        lanes = slice(r * 2 * seqs, (r + 1) * 2 * seqs)
+        diag_ref[:hidden, lanes] = jnp.where(low, left, zero).astype(bf16)
+        diag_ref[hidden:, lanes] = jnp.where(low, zero, left).astype(bf16)
+    for r in range(res):
+        cots[r * columns : (r + 1) * columns, :] = cot_ref[r].astype(f32)
+    for r in range(res):
+        for q in range(res):
+            block = cots[pl.ds(r * columns + q, devices, stride=res), :]
+            moved[pl.ds(r * res + q, devices, stride=res * res), :] = block
+    index = lax.axis_index("row")
+    per = res * res
+    plane = devices // len(sends)
+    for n in range(devices):
+        at = pl.multiple_of(lax.bitwise_xor(index, n) * per, per)
+        to = res * hidden + n % plane * per
+        sends[n // plane][to : to + per, :] = moved[pl.ds(at, per), :].astype(bf16)
+
+
+def pack_kernel(height, *refs):
+    held, sent = refs[: len(refs) // 2], refs[len(refs) // 2 :]
+    cut = (held[0].shape[0] - height) // len(sent)
+    for z, h in enumerate(held):
+        factors = h[:height, :]
+        for yx, s in enumerate(sent):
+            s[z * height : (z + 1) * height, :] = factors
+            to = len(held) * height + z * cut
+            s[to : to + cut, :] = h[height + yx * cut : height + (yx + 1) * cut, :]
+
+
+def prepare_kernel(
+    out_w_ref, cot_ref,
+    cot_t_ref, twin_left_ref, twin_right_ref, bias_ref,
+    wide,
+):
+    hidden = twin_left_ref.shape[0] // 2
+    res, columns, pairs = cot_ref.shape
+    wide[...] = out_w_ref[...].astype(f32)
+    for d in range(hidden):
+        at = (d % 2) * hidden
+        twin_left_ref[at : at + hidden, (d // 2) * pairs : (d // 2 + 1) * pairs] = wide[
+            pl.ds(d, hidden, stride=hidden), :
+        ].astype(bf16)
+    for q in range(hidden // 2):
+        twin_right_ref[:, q * pairs : (q + 1) * pairs] = out_w_ref[
+            q * 2 * hidden : (q + 1) * 2 * hidden, :
+        ]
+    total = jnp.zeros((1, pairs), f32)
+    for r in range(res):
+        cot = cot_ref[r].astype(f32)
+        total = total + jnp.sum(cot, axis=0, keepdims=True)
+        cot_t_ref[r * pairs : (r + 1) * pairs, :] = cot.T.astype(bf16)
+    bias_ref[...] = jnp.broadcast_to(total, bias_ref.shape)
+
+
+def sums_kernel(
+    mine_ref, other_ref, cot_t_ref, twin_left_ref, twin_right_ref, normed_ref, scaled_ref,
+    w1_ref, w2_ref, bias_ref,
+    small_ref, rights_ref, spread_ref, grad_ref,
+    wide, lefts, turned, cots, got_t,
+):
+    columns = rights_ref.shape[0]
+    yxs, _, lanes = mine_ref.shape
+    seqs = lanes // 2
+    channels = normed_ref.shape[1]
+    hidden = w1_ref.shape[0]
+    twins = hidden // 2
+    pairs = bias_ref.shape[1]
+    res = spread_ref.shape[1] // lanes
+    index = lax.axis_index("row")
+    height = res * hidden
+    per = res * res
+    zs = wide.shape[0] // (2 * yxs * height)
+    for yx in range(yxs):
+        for z in range(zs):
+            factors = slice(z * height, (z + 1) * height)
+            first = zs * height + z * 2 * per
+            for core, ref in enumerate((mine_ref, other_ref)):
+                device = lax.bitwise_xor(index, z * 2 * yxs + yx * 2 + core)
+                at = pl.multiple_of(device * height, height)
+                wide[pl.ds(at, height), :] = ref[yx, factors, :].astype(f32)
+                block = ref[yx, first + core * per : first + (core + 1) * per, :]
+                at = pl.multiple_of(device * per, per)
+                cots[pl.ds(at, per), :] = block.astype(f32)
+    for r in range(res):
+        got_t[r * pairs : (r + 1) * pairs, :] = cots[pl.ds(r, columns, stride=res), :].T.astype(bf16)
+    for q in range(twins):
+        here = slice(q * lanes, (q + 1) * lanes)
+        lefts[:, here] = wide[pl.ds(q, columns, stride=hidden), :].astype(bf16)
+        rights_ref[:, here] = wide[pl.ds(twins + q, columns, stride=hidden), :].astype(bf16)
+
+    def summed(cots, factors, weights, out):
+        for r in range(res):
+            block = mm(cots[r * pairs : (r + 1) * pairs, :], factors[...]).astype(bf16)
+            for q in range(twins):
+                out[q * pairs : (q + 1) * pairs, r * lanes : (r + 1) * lanes] = block[
+                    :, q * lanes : (q + 1) * lanes
+                ]
+        t = mm(weights[...], out[...]).T
+        parts = [
+            t[r * lanes : r * lanes + seqs, :hidden] + t[r * lanes + seqs : (r + 1) * lanes, hidden:]
+            for r in range(res)
+        ]
+        return jnp.concatenate(parts, axis=0) * (1.0 / seqs)
+
+    left_sum = summed(cot_t_ref, rights_ref, twin_left_ref, spread_ref)
+    right_sum = summed(got_t, lefts, twin_right_ref, turned)
+    normed_grad = mm(left_sum.astype(bf16), w1_ref[...]) + mm(right_sum.astype(bf16), w2_ref[...])
+    grad_ref[...] = normed_grad
+    factors_t = jnp.concatenate([left_sum, right_sum], axis=1).T.astype(bf16)
+    small_ref[: 2 * hidden, :] = mm(factors_t, normed_ref[...])
+    gain_part = jnp.sum(normed_grad * scaled_ref[...], axis=0, keepdims=True)
+    bias_part = jnp.concatenate([bias_ref[:1, :]] * (channels // pairs), axis=1)
+    line = lax.broadcasted_iota(jnp.int32, (16, channels), 0)
+    small_ref[2 * hidden :, :] = jnp.where(
+        line == 0, gain_part, jnp.where(line == 1, bias_part, jnp.zeros((16, channels), f32))
+    )
+
+
+def share_kernel(res, diag_ref, spread_ref, out_ref, outs):
+    hidden = diag_ref.shape[0] // 2
+    pairs = out_ref.shape[1]
+    seqs = diag_ref.shape[1] // (2 * res)
+    grad = mm_t(diag_ref[...], spread_ref[...]) * (1.0 / seqs)
+    for d in range(hidden):
+        at = (d % 2) * hidden
+        outs[pl.ds(d, hidden, stride=hidden), :] = grad[
+            at : at + hidden, (d // 2) * pairs : (d // 2 + 1) * pairs
+        ]
+    index = lax.axis_index("row")
+    for place in range(hidden):
+        chunk = lax.bitwise_xor(index, int(format(place, "05b")[::-1], 2))
+        at = pl.multiple_of(chunk * hidden, hidden)
+        out_ref[place * hidden : (place + 1) * hidden, :] = outs[pl.ds(at, hidden), :]
+
+
+def result_kernel(
+    rights_ref, twin_left_ref, w1_ref, normed_ref, bias_ref, normed_grad_ref, scaled_ref, recip_ref, gain_ref,
+    delta_ref, grad_ref,
+    rows, mixed,
+):
+    res, _, pairs = delta_ref.shape
+    seqs = grad_ref.shape[0]
+    hidden = w1_ref.shape[0]
+    left = mm_t(normed_ref[...], w1_ref[...]).astype(bf16)
+    for d in range(hidden):
+        at = (d % 2) * hidden
+        part = mm(left, twin_left_ref[at : at + hidden, (d // 2) * pairs : (d // 2 + 1) * pairs])
+        part = part.astype(bf16)
+        for r in range(res):
+            mixed[d * seqs : (d + 1) * seqs, r * pairs : (r + 1) * pairs] = part[
+                r * seqs : (r + 1) * seqs, :
+            ]
+    delta = mm(rights_ref[...], mixed[...]) * (1.0 / seqs)
+    for r in range(res):
+        delta_ref[r] = (delta[:, r * pairs : (r + 1) * pairs] + bias_ref[...]).astype(bf16)
+    scaled = scaled_ref[...]
+    scaled_grad = normed_grad_ref[...] * gain_ref[...]
+    centre = jnp.mean(scaled_grad, axis=-1, keepdims=True)
+    slope = jnp.mean(scaled_grad * scaled, axis=-1, keepdims=True)
+    grad = recip_ref[:, :1] * (scaled_grad - centre - scaled * slope)
+    for r in range(res):
+        rows[:, r, :] = grad[r * seqs : (r + 1) * seqs, :]
+    grad_ref[...] = rows[...].astype(bf16)
+
+
+def finish_kernel(
+    scale, own_ref, came_ref, keep_ref, shared_ref,
+    gain_hbm, left_hbm, right_hbm, out_hbm, bias_hbm,
+    total, out, sems,
+):
+    hidden = left_hbm.shape[0]
+    pairs = bias_hbm.shape[1]
+    total[...] = (own_ref[...].astype(f32) + came_ref[...].astype(f32)) * scale
+    out[...] = (keep_ref[...] + shared_ref[...].astype(f32)) * scale
+    copies = fetch(
+        [
+            (total.at[2 * hidden : 2 * hidden + 1, :], gain_hbm),
+            (total.at[:hidden, :], left_hbm),
+            (total.at[hidden : 2 * hidden, :], right_hbm),
+            (out, out_hbm),
+            (total.at[2 * hidden + 1 : 2 * hidden + 2, :pairs], bias_hbm),
+        ],
+        sems,
+    )
+    for copy in copies:
+        copy.wait()
+
+
+def call(kernel, name, args, outs, scratch, flops, remote_in=False, remote_out=False, vmem=16):
+    moved = sum(a.size * a.dtype.itemsize for a in args)
+    space = lambda far: pl.BlockSpec(memory_space=pltpu.HBM if far else pltpu.VMEM)
+    sems = max(len(args) * remote_in, len(outs) * remote_out)
+    shapes = [pltpu.VMEM(s, d) for s, d in scratch]
+    if sems:
+        shapes.append(pltpu.SemaphoreType.DMA((sems,)))
+    return pl.pallas_call(
+        kernel,
+        out_shape=[jax.ShapeDtypeStruct(s, d) for s, d in outs],
+        in_specs=[space(remote_in)] * len(args),
+        out_specs=[space(remote_out)] * len(outs),
+        scratch_shapes=shapes,
+        compiler_params=pltpu.CompilerParams(vmem_limit_bytes=vmem * 1024 * 1024),
+        cost_estimate=pl.CostEstimate(flops=flops, bytes_accessed=moved, transcendentals=0),
+        name=name,
+    )(*args)
+
+
+def swap(value, step):
+    count = lax.axis_size("row")
+    return lax.ppermute(value, "row", [(i, i ^ step) for i in range(count)])
+
+
+def on_device_row(
+    homolog_features,
+    standardize_multiplier,
+    first_factor_weights,
+    second_factor_weights,
+    output_projection_matrix,
+    output_bias,
+    pair_cotangent,
+):
+    seqs, res, channels = homolog_features.shape
+    hidden = first_factor_weights.shape[1]
+    pairs = output_projection_matrix.shape[1]
+    count = lax.axis_size("row")
+    columns = res * count
+    own = seqs * res
+    lanes = 2 * seqs
+    twins = hidden // 2
+    gain = standardize_multiplier.reshape(1, channels)
+    bias = output_bias.reshape(1, pairs)
+    w1, w2 = first_factor_weights.T, second_factor_weights.T
+    wide = (2 * hidden, twins * pairs)
+
+    zs, yxs = 4, 4
+    height = res * hidden
+    *sends, scaled, normed, recip, diag = call(
+        factor_kernel,
+        "factors",
+        (homolog_features, gain, w1, w2, pair_cotangent),
+        [
+            *[((height + res * columns // zs, lanes), bf16)] * zs,
+            ((own, channels), f32),
+            ((own, channels), bf16),
+            ((own, 128), f32),
+            ((2 * hidden, res * lanes), bf16),
+        ],
+        [
+            ((seqs, res, channels), bf16),
+            ((1, channels), f32),
+            ((hidden, channels), bf16),
+            ((hidden, channels), bf16),
+            ((res, columns, pairs), bf16),
+            ((seqs, res, channels), f32),
+            ((seqs, res, 128), f32),
+            ((res, 2 * hidden, lanes), f32),
+            ((res * columns, pairs), f32),
+            ((res * columns, pairs), f32),
+        ],
+        10**6,
+        remote_in=True,
+        vmem=60,
+    )
+    swapped = {z: swap(sends[z], z * 2 * yxs) for z in (3, 2, 1)}
+    sent = call(
+        functools.partial(pack_kernel, height),
+        "pack",
+        [sends[0]] + [swapped[z] for z in range(1, zs)],
+        [((zs * height + zs * 2 * res * res, lanes), bf16)] * yxs,
+        [],
+        10**6,
+    )
+    mine = jnp.stack([sent[0]] + [swap(sent[yx], yx * 2) for yx in range(1, yxs)])
+    other = swap(mine, 1)
+    cot_t, twin_left, twin_right, bias_part = call(
+        prepare_kernel,
+        "prepare",
+        (output_projection_matrix, pair_cotangent),
+        [
+            ((res * pairs, columns), bf16),
+            (wide, bf16),
+            (wide, bf16),
+            ((8, pairs), f32),
+        ],
+        [((hidden * hidden, pairs), f32)],
+        10**6,
+    )
+    small, rights, spread, normed_grad = call(
+        sums_kernel,
+        "sums",
+        (
+            mine, other, cot_t, twin_left, twin_right, normed, scaled, w1, w2, bias_part,
+        ),
+        [
+            ((2 * hidden + 16, channels), f32),
+            ((columns, hidden * seqs), bf16),
+            ((twins * pairs, res * lanes), bf16),
+            ((own, channels), f32),
+        ],
+        [
+            ((columns * hidden, lanes), f32),
+            ((columns, hidden * seqs), bf16),
+            ((twins * pairs, res * lanes), bf16),
+            ((res * columns, pairs), f32),
+            ((res * pairs, columns), bf16),
+        ],
+        10**6,
+    )
+    (out_part,) = call(
+        functools.partial(share_kernel, res),
+        "shares",
+        (diag, spread),
+        [((hidden * hidden, pairs), f32)],
+        [((hidden * hidden, pairs), f32)],
+        10**6,
+    )
+    delta, grad = call(
+        result_kernel,
+        "results",
+        (rights, twin_left, w1, normed, bias, normed_grad, scaled, recip, gain),
+        [((res, columns, pairs), bf16), ((seqs, res, channels), bf16)],
+        [((seqs, res, channels), f32), ((hidden * seqs, res * pairs), bf16)],
+        10**6,
+    )
+    half = hidden * hidden // 2
+    small = (small + swap(small, 1)).astype(bf16)
+    step = 1
+    while step < count:
+        keep, give = out_part[:half], out_part[half:].astype(bf16)
+        if 2 * step < count:
+            out_part = keep + swap(give, step).astype(f32)
+        if step > 1:
+            small = lax.optimization_barrier(small)
+            came = swap(small, step + 1)
+            if 2 * step < count:
+                small = small + came
+            if step == 2:
+                small, delta, grad = lax.optimization_barrier((small, delta, grad))
+        step *= 2
+        half //= 2
+    shared = swap(give, count // 2)
+    gain_out, left_out, right_out, out_share, bias_out = call(
+        functools.partial(finish_kernel, 1.0 / columns),
+        "finish",
+        (small, came, keep, shared),
+        [
+            ((1, channels), f32),
+            ((hidden, channels), f32),
+            ((hidden, channels), f32),
+            ((hidden * hidden // count, pairs), f32),
+            ((1, pairs), f32),
+        ],
+        [((2 * hidden + 16, channels), f32), ((hidden * hidden // count, pairs), f32)],
+        10**6,
+        remote_out=True,
+    )
+    return (
+        delta,
+        grad,
+        gain_out.reshape(channels),
+        left_out.T,
+        right_out.T,
+        out_share,
+        bias_out.reshape(pairs),
+    )
+
+
 def solution(mesh):
     in_specs = (P(None, ("col", "row"), None), P(), P(), P(), P(), P(), P("row", "col", None))
     out_specs = (
@@ -181,6 +609,8 @@
         P(("row", "col"), None),
         P(),
     )
+    one_row = mesh.shape["row"] == 32 and mesh.shape["col"] == 1
+    body = on_device_row if one_row else on_device
     return jax.shard_map(
-        on_device, mesh=mesh, in_specs=in_specs, out_specs=out_specs, check_vma=False
-    )
+        body, mesh=mesh, in_specs=in_specs, out_specs=out_specs, check_vma=False
+    )

time: 637 us -> 55.1 us (0.09)
  waiting for transfers between devices: 504 us -> 20.8 us
  blocking collectives: 85.6 us -> 0 us
  starting transfers between devices: 0.16 us -> 19 us
  between operations: 14 us -> 0.88 us
  matrix products: 10.9 us -> 0 us
  Pallas kernels: 0 us -> 10.3 us
  other arithmetic: 9.65 us -> 0.19 us
    reduce_scatter x3 -> x0, waiting for transfers between devices: 385 us -> none  [the longest x1 134 us: on_device(): lax.psum_scatter(slotted, 'row', scatter_dimension=1, tiled=True)]
    psum x1 -> x0, waiting for transfers between devices: 119 us -> none  [on_device(): lax.psum((left_weight, right_weight, gain_part, bias_part), ('row', 'col'))]
    all_gather x2 -> x0, blocking collectives: 85.6 us -> none  [the longest x1 46.2 us: on_device(): lax.all_gather(right_own.reshape(sequence_count, local_residues * hidden)...]
    ppermute x0 -> x17, waiting for transfers between devices: none -> 20.8 us  [swap(): return lax.ppermute(value, 'row', [(i, i ^ step) for i in range(count)])]
    ppermute x0 -> x17, starting transfers between devices: none -> 19 us  [swap(): return lax.ppermute(value, 'row', [(i, i ^ step) for i in range(count)])]
    dot_general x12 -> x0, matrix products: 10.9 us -> none  [the longest x1 1.54 us: pair_step(): jnp.einsum('ijcd,sic->sjd', outer_grad, left_blk, preferred_element_type=...]
    pallas_call x0 -> x7, Pallas kernels: none -> 10.3 us  [call(): pl.pallas_call(kernel, out_shape=[jax.ShapeDtypeStruct(s, d) for s, d in...]
  transfers between devices with their start and end apart: 4 -> 17, of which waited for: 4 -> 11; matrix products, arithmetic and copies ran while one was open for 2% -> 0% of each run, Pallas kernels for 0% -> 4%
where the time goes in v2:
time: 55.1 us; the launch traced here: 54.9 us
  waiting for transfers between devices  20.8 us (38%)
  starting transfers between devices  19 us (34%)
  Pallas kernels  10.3 us (19%)
  local copies, waits for them, and re-layouts  3.67 us (7%)
  between operations  0.88 us (2%)
    ppermute x17, waiting for transfers between devices, swap(): return lax.ppermute(value, 'row', [(i, i ^ step) for i in range(count)])  20.8 us
    ppermute x17, starting transfers between devices, swap(): return lax.ppermute(value, 'row', [(i, i ^ step) for i in range(count)])  19 us
    pallas_call x7, Pallas kernels, call(): pl.pallas_call(kernel, out_shape=[jax.ShapeDtypeStruct(s, d) for s, d in...  10.3 us
    unnamed x24, local copies, waits for them, and re-layouts  3.63 us
  transfers between devices with their start and end apart: 17, of which 11 were waited for; matrix products, arithmetic and copies ran while one was open for 0% of the time, Pallas kernels for 4%

profile of v2, /device:TPU:0, one launch (start us, length us, event | category | flops | bytes accessed | tf_op | source)
XLA Modules:
  0.0 54.9 jit_solution(651185039623016395)
XLA Ops:
  0.7 2.4 %factors.1 = (bf16[256,128]{1,0:T(8,128)(2,1)}, bf16[256,128]{1,0:T(8,128)(2,1)}, bf16[256,128]{1,0:T(8,128)(2,1)}, bf16[256,128]{1,0:T(8,128)(2,1)}, f32[256,25...) custom-call(bf16[64,4,256]{2,1,0:T(4,128)(2,1)} %x_hbm.1, ...), custom_call_target="tpu_custom_call" | custom-call | flops 1000000 | bytes 295936 | tf_op jit(solution)/shard_map/factors/pallas_call | solution.py:429
  3.1 3.1 %collective-permute-start = (bf16[256,128]{1,0:T(8,128)(2,1)}, bf16[256,128]{1,0:T(8,128)(2,1)S(1)}, u32[]{:S(2)}, u32[]{:S(2)}) collective-permute-start(bf16[256,128]{1,0:T(8,128)(2,1)} %get-tuple-element.38), channel_id=1, source_target_pairs={{0,8},{1,9},{2,10},{3,11},{4,12},{5,13},{6,14},{7,15},{8,0},{9,1},... | collective-permute-start | bytes 196616 | tf_op jit(solution)/shard_map/ppermute | solution.py:443
  6.1 2.6 %collective-permute-start.1 = (bf16[256,128]{1,0:T(8,128)(2,1)}, bf16[256,128]{1,0:T(8,128)(2,1)S(1)}, u32[]{:S(2)}, u32[]{:S(2)}) collective-permute-start(bf16[256,128]{1,0:T(8,128)(2,1)} %get-tuple-element.39), channel_id=1, source_target_pairs={{0,16},{1,17},{2,18},{3,19},{4,20},{5,21},{6,22},{7,23},{8,24},{9,... | collective-permute-start | bytes 196616 | tf_op jit(solution)/shard_map/ppermute | solution.py:443
  8.7 4.9 %collective-permute-done.1.refs_2_ = bf16[256,128]{1,0:T(8,128)(2,1)S(1)} collective-permute-done((bf16[256,128]{1,0:T(8,128)(2,1)}, bf16[256,128]{1,0:T(8,128)(2,1)S(1)}, u32[]{:S(2)}, u32[]{:S(2)}) %collective-permute-start.1) | collective-permute-done | bytes 65568 | tf_op jit(solution)/shard_map/ppermute | solution.py:443
  13.6 1.4 %collective-permute-done.2.refs_3_ = bf16[256,128]{1,0:T(8,128)(2,1)S(1)} collective-permute-done((bf16[256,128]{1,0:T(8,128)(2,1)}, bf16[256,128]{1,0:T(8,128)(2,1)S(1)}, u32[]{:S(2)}, u32[]{:S(2)}) %collective-permute-start.2) | collective-permute-done | bytes 65568 | tf_op jit(solution)/shard_map/ppermute | solution.py:443
  15.0 0.8 %copy-done.8 = bf16[256,128]{1,0:T(8,128)(2,1)S(1)} copy-done((bf16[256,128]{1,0:T(8,128)(2,1)S(1)}, bf16[256,128]{1,0:T(8,128)(2,1)}, u32[]{:S(2)}) %copy-start.8) | copy-done | bytes 65560
  16.0 1.6 %collective-permute-start.3 = (bf16[640,128]{1,0:T(8,128)(2,1)S(1)}, bf16[640,128]{1,0:T(8,128)(2,1)S(1)}, u32[]{:S(2)}, u32[]{:S(2)}) collective-permute-start(bf16[640,128]{1,0:T(8,128)(2,1)S(1)} %get-tuple-element.42), channel_id=1, source_target_pairs={{0,2},{1,3},{2,0},{3,1},{4,6},{5,7},{6,4},{7,5},{8,10},{9,11},{10,... | collective-permute-start | bytes 491528 | tf_op jit(solution)/shard_map/ppermute | solution.py:443
  17.5 1.5 %collective-permute-start.4 = (bf16[640,128]{1,0:T(8,128)(2,1)S(1)}, bf16[640,128]{1,0:T(8,128)(2,1)S(1)}, u32[]{:S(2)}, u32[]{:S(2)}) collective-permute-start(bf16[640,128]{1,0:T(8,128)(2,1)S(1)} %get-tuple-element.43), channel_id=1, source_target_pairs={{0,4},{1,5},{2,6},{3,7},{4,0},{5,1},{6,2},{7,3},{8,12},{9,13},{10,... | collective-permute-start | bytes 491528 | tf_op jit(solution)/shard_map/ppermute | solution.py:443
  19.5 3.2 %collective-permute-done.3 = bf16[640,128]{1,0:T(8,128)(2,1)S(1)} collective-permute-done((bf16[640,128]{1,0:T(8,128)(2,1)S(1)}, bf16[640,128]{1,0:T(8,128)(2,1)S(1)}, u32[]{:S(2)}, u32[]{:S(2)}) %collective-permute-start.3) | collective-permute-done | bytes 163872 | tf_op jit(solution)/shard_map/ppermute | solution.py:443
  22.7 3.0 %collective-permute-done.4 = bf16[640,128]{1,0:T(8,128)(2,1)S(1)} collective-permute-done((bf16[640,128]{1,0:T(8,128)(2,1)S(1)}, bf16[640,128]{1,0:T(8,128)(2,1)S(1)}, u32[]{:S(2)}, u32[]{:S(2)}) %collective-permute-start.4) | collective-permute-done | bytes 163872 | tf_op jit(solution)/shard_map/ppermute | solution.py:443
  25.9 0.9 %copy-done.3 = bf16[4,128,128]{2,1,0:T(8,128)(2,1)S(1)} copy-done((bf16[4,128,128]{2,1,0:T(8,128)(2,1)S(1)}, bf16[4,128,128]{2,1,0:T(8,128)(2,1)}, u32[]{:S(2)}) %copy-start.3) | copy-done | bytes 131096
  26.8 0.9 %copy-done.4 = bf16[1024,128]{1,0:T(8,128)(2,1)S(1)} copy-done((bf16[1024,128]{1,0:T(8,128)(2,1)S(1)}, bf16[1024,128]{1,0:T(8,128)(2,1)}, u32[]{:S(2)}) %copy-start.4) | copy-done | bytes 262168
  28.3 0.9 %copy-done.1 = bf16[256,256]{1,0:T(8,128)(2,1)S(1)} copy-done((bf16[256,256]{1,0:T(8,128)(2,1)S(1)}, bf16[256,256]{1,0:T(8,128)(2,1)}, u32[]{:S(2)}) %copy-start.1) | copy-done | bytes 131096
  29.1 3.8 %sums.1 = (f32[80,256]{1,0:T(8,128)S(1)}, bf16[128,2048]{1,0:T(8,128)(2,1)S(1)}, bf16[2048,512]{1,0:T(8,128)(2,1)S(1)}, f32[256,256]{1,0:T(8,128)S(1)}) custom-call(bf16[4,640,128]{2,1,0:T(8,128)(2,1)S(1)} %pad_maximum_fusion.mine_ref, bf16[4,640,128]{2,1,0:T(8,128)(2,1)S(1)} %collective-permute-done.6.other_ref, ...), custom_call_target="tpu_custom_call" | custom-call | flops 1000000 | bytes 2396160 | tf_op jit(solution)/shard_map/sums/pallas_call | solution.py:429
  33.0 1.0 %shares.1 = f32[1024,128]{1,0:T(8,128)S(1)} custom-call(bf16[64,512]{1,0:T(8,128)(2,1)S(1)} %copy-done.9, bf16[2048,512]{1,0:T(8,128)(2,1)S(1)} %get-tuple-element.61.spread_ref), custom_call_target="tpu_custom_call" | custom-call | flops 1000000 | bytes 2162688 | tf_op jit(solution)/shard_map/shares/pallas_call | solution.py:429
  34.0 0.6 %collective-permute-start.12 = (bf16[512,128]{1,0:T(8,128)(2,1)S(1)}, bf16[512,128]{1,0:T(8,128)(2,1)S(1)}, u32[]{:S(2)}, u32[]{:S(2)}) collective-permute-start(bf16[512,128]{1,0:T(8,128)(2,1)S(1)} %slice.64), channel_id=1, source_target_pairs={{0,1},{1,0},{2,3},{3,2},{4,5},{5,4},{6,7},{7,6},{8,9},{9,8},{10,11... | collective-permute-start | bytes 393224 | tf_op jit(solution)/shard_map/ppermute | solution.py:443
  34.7 0.9 %collective-permute-done.12 = bf16[512,128]{1,0:T(8,128)(2,1)S(1)} collective-permute-done((bf16[512,128]{1,0:T(8,128)(2,1)S(1)}, bf16[512,128]{1,0:T(8,128)(2,1)S(1)}, u32[]{:S(2)}, u32[]{:S(2)}) %collective-permute-start.12) | collective-permute-done | bytes 131104 | tf_op jit(solution)/shard_map/ppermute | solution.py:443
  35.6 0.6 %collective-permute-start.13 = (bf16[256,128]{1,0:T(8,128)(2,1)S(1)}, bf16[256,128]{1,0:T(8,128)(2,1)S(1)}, u32[]{:S(2)}, u32[]{:S(2)}) collective-permute-start(bf16[256,128]{1,0:T(8,128)(2,1)S(1)} %slice.65), channel_id=1, source_target_pairs={{0,2},{1,3},{2,0},{3,1},{4,6},{5,7},{6,4},{7,5},{8,10},{9,11},{10,... | collective-permute-start | bytes 196616 | tf_op jit(solution)/shard_map/ppermute | solution.py:443
  36.3 1.2 %collective-permute-start.8 = (bf16[80,256]{1,0:T(8,128)(2,1)S(1)}, bf16[80,256]{1,0:T(8,128)(2,1)S(1)}, u32[]{:S(2)}, u32[]{:S(2)}) collective-permute-start(bf16[80,256]{1,0:T(8,128)(2,1)S(1)} %add_convert_fusion), channel_id=1, source_target_pairs={{0,3},{1,2},{2,1},{3,0},{4,7},{5,6},{6,5},{7,4},{8,11},{9,10},{10,... | collective-permute-start | bytes 122888 | tf_op jit(solution)/shard_map/ppermute | solution.py:443
  37.5 1.9 %results.1 = (bf16[4,128,128]{2,1,0:T(8,128)(2,1)}, bf16[64,4,256]{2,1,0:T(4,128)(2,1)}) custom-call(bf16[128,2048]{1,0:T(8,128)(2,1)S(1)} %get-tuple-element.52.rights_ref, bf16[64,2048]{1,0:T(8,128)(2,1)S(1)} %get-tuple-element.46.twin_left_ref, bf16[32,256]{1,0:T(8,128)(2,1)S(1)} %bitcast.15, bf16[256,256]{1,0:T(8,128)(2,1)S(1)} %copy-done.2, ...), custom_call_target="tpu_custom_call" | custom-call | flops 1000000 | bytes 1590784 | tf_op jit(solution)/shard_map/results/pallas_call | solution.py:429
  39.4 0.9 %collective-permute-done.8 = bf16[80,256]{1,0:T(8,128)(2,1)S(1)} collective-permute-done((bf16[80,256]{1,0:T(8,128)(2,1)S(1)}, bf16[80,256]{1,0:T(8,128)(2,1)S(1)}, u32[]{:S(2)}, u32[]{:S(2)}) %collective-permute-start.8) | collective-permute-done | bytes 40992 | tf_op jit(solution)/shard_map/ppermute | solution.py:443
  40.4 1.1 %collective-permute-start.9 = (bf16[80,256]{1,0:T(8,128)(2,1)S(1)}, bf16[80,256]{1,0:T(8,128)(2,1)S(1)}, u32[]{:S(2)}, u32[]{:S(2)}) collective-permute-start(bf16[80,256]{1,0:T(8,128)(2,1)S(1)} %add.25), channel_id=1, source_target_pairs={{0,5},{1,4},{2,7},{3,6},{4,1},{5,0},{6,3},{7,2},{8,13},{9,12},{10,... | collective-permute-start | bytes 122888 | tf_op jit(solution)/shard_map/ppermute | solution.py:443
  41.5 1.1 %collective-permute-start.14 = (bf16[128,128]{1,0:T(8,128)(2,1)S(1)}, bf16[128,128]{1,0:T(8,128)(2,1)S(1)}, u32[]{:S(2)}, u32[]{:S(2)}) collective-permute-start(bf16[128,128]{1,0:T(8,128)(2,1)S(1)} %slice.66), channel_id=1, source_target_pairs={{0,4},{1,5},{2,6},{3,7},{4,0},{5,1},{6,2},{7,3},{8,12},{9,13},{10,... | collective-permute-start | bytes 98312 | tf_op jit(solution)/shard_map/ppermute | solution.py:443
  42.6 1.3 %collective-permute-done.9 = bf16[80,256]{1,0:T(8,128)(2,1)S(1)} collective-permute-done((bf16[80,256]{1,0:T(8,128)(2,1)S(1)}, bf16[80,256]{1,0:T(8,128)(2,1)S(1)}, u32[]{:S(2)}, u32[]{:S(2)}) %collective-permute-start.9) | collective-permute-done | bytes 40992 | tf_op jit(solution)/shard_map/ppermute | solution.py:443
  44.4 1.0 %collective-permute-done.14 = bf16[128,128]{1,0:T(8,128)(2,1)S(1)} collective-permute-done((bf16[128,128]{1,0:T(8,128)(2,1)S(1)}, bf16[128,128]{1,0:T(8,128)(2,1)S(1)}, u32[]{:S(2)}, u32[]{:S(2)}) %collective-permute-start.14) | collective-permute-done | bytes 32800 | tf_op jit(solution)/shard_map/ppermute | solution.py:443
  45.5 0.7 %collective-permute-start.15 = (bf16[64,128]{1,0:T(8,128)(2,1)S(1)}, bf16[64,128]{1,0:T(8,128)(2,1)S(1)}, u32[]{:S(2)}, u32[]{:S(2)}) collective-permute-start(bf16[64,128]{1,0:T(8,128)(2,1)S(1)} %slice.67), channel_id=1, source_target_pairs={{0,8},{1,9},{2,10},{3,11},{4,12},{5,13},{6,14},{7,15},{8,0},{9,1},... | collective-permute-start | bytes 49160 | tf_op jit(solution)/shard_map/ppermute | solution.py:443
  46.2 1.2 %collective-permute-done.10 = bf16[80,256]{1,0:T(8,128)(2,1)S(1)} collective-permute-done((bf16[80,256]{1,0:T(8,128)(2,1)S(1)}, bf16[80,256]{1,0:T(8,128)(2,1)S(1)}, u32[]{:S(2)}, u32[]{:S(2)}) %collective-permute-start.10) | collective-permute-done | bytes 40992 | tf_op jit(solution)/shard_map/ppermute | solution.py:443
  47.4 2.1 %collective-permute-start.11 = (bf16[80,256]{1,0:T(8,128)(2,1)S(1)}, bf16[80,256]{1,0:T(8,128)(2,1)S(1)}, u32[]{:S(2)}, u32[]{:S(2)}) collective-permute-start(bf16[80,256]{1,0:T(8,128)(2,1)S(1)} %add.27.own_ref), channel_id=1, source_target_pairs={{0,17},{1,16},{2,19},{3,18},{4,21},{5,20},{6,23},{7,22},{8,25},{9,... | collective-permute-start | bytes 122888 | tf_op jit(solution)/shard_map/ppermute | solution.py:443
  49.5 1.8 %collective-permute-start.16 = (bf16[32,128]{1,0:T(8,128)(2,1)S(1)}, bf16[32,128]{1,0:T(8,128)(2,1)S(1)}, u32[]{:S(2)}, u32[]{:S(2)}) collective-permute-start(bf16[32,128]{1,0:T(8,128)(2,1)S(1)} %slice.68), channel_id=1, source_target_pairs={{0,16},{1,17},{2,18},{3,19},{4,20},{5,21},{6,22},{7,23},{8,24},{9,... | collective-permute-start | bytes 24584 | tf_op jit(solution)/shard_map/ppermute | solution.py:443
  51.3 1.7 %collective-permute-done.11.came_ref = bf16[80,256]{1,0:T(8,128)(2,1)S(1)} collective-permute-done((bf16[80,256]{1,0:T(8,128)(2,1)S(1)}, bf16[80,256]{1,0:T(8,128)(2,1)S(1)}, u32[]{:S(2)}, u32[]{:S(2)}) %collective-permute-start.11) | collective-permute-done | bytes 40992 | tf_op jit(solution)/shard_map/ppermute | solution.py:443
  53.0 1.2 %collective-permute-done.16.shared_ref = bf16[32,128]{1,0:T(8,128)(2,1)S(1)} collective-permute-done((bf16[32,128]{1,0:T(8,128)(2,1)S(1)}, bf16[32,128]{1,0:T(8,128)(2,1)S(1)}, u32[]{:S(2)}, u32[]{:S(2)}) %collective-permute-start.16) | collective-permute-done | bytes 8224 | tf_op jit(solution)/shard_map/ppermute | solution.py:443
  54.2 0.7 %finish.1 = (f32[1,256]{1,0:T(1,128)}, f32[32,256]{1,0:T(8,128)}, f32[32,256]{1,0:T(8,128)}, f32[32,128]{1,0:T(8,128)}, f32[1,128]{1,0:T(1,128)}) custom-call(bf16[80,256]{1,0:T(8,128)(2,1)S(1)} %add.27.own_ref, bf16[80,256]{1,0:T(8,128)(2,1)S(1)} %collective-permute-done.11.came_ref, f32[32,128]{1,0:T(8,128)S(1)} %slice.53.keep_ref, ...), custom_call_target="tpu_custom_call" | custom-call | flops 1000000 | bytes 106496 | tf_op jit(solution)/shard_map/finish/pallas_call | solution.py:429
  (48 shorter events, 1.9 us)
Async XLA Ops:
  0.6 27.6 %copy-start.7 = (bf16[256,32]{0,1:T(8,128)(2,1)S(1)}, bf16[256,32]{0,1:T(8,128)(2,1)}, u32[]{:S(2)}) copy-start(bf16[256,32]{0,1:T(8,128)(2,1)} %param.10) | copy-start | bytes 49156
  0.6 27.6 %copy-start.5 = (bf16[256,32]{0,1:T(8,128)(2,1)S(1)}, bf16[256,32]{0,1:T(8,128)(2,1)}, u32[]{:S(2)}) copy-start(bf16[256,32]{0,1:T(8,128)(2,1)} %param.9) | copy-start | bytes 49156
  3.0 25.2 %copy-start = (f32[256,256]{1,0:T(8,128)S(1)}, f32[256,256]{1,0:T(8,128)}, u32[]{:S(2)}) copy-start(f32[256,256]{1,0:T(8,128)} %get-tuple-element.49.scaled_ref) | copy-start | bytes 786436
  3.1 5.7 %collective-permute-start = (bf16[256,128]{1,0:T(8,128)(2,1)}, bf16[256,128]{1,0:T(8,128)(2,1)S(1)}, u32[]{:S(2)}, u32[]{:S(2)}) collective-permute-start(bf16[256,128]{1,0:T(8,128)(2,1)} %get-tuple-element.38), channel_id=1, source_target_pairs={{0,8},{1,9},{2,10},{3,11},{4,12},{5,13},{6,14},{7,15},{8,0},{9,1},... | collective-permute-start | bytes 196616 | tf_op jit(solution)/shard_map/ppermute | solution.py:443
  6.1 7.5 %collective-permute-start.1 = (bf16[256,128]{1,0:T(8,128)(2,1)}, bf16[256,128]{1,0:T(8,128)(2,1)S(1)}, u32[]{:S(2)}, u32[]{:S(2)}) collective-permute-start(bf16[256,128]{1,0:T(8,128)(2,1)} %get-tuple-element.39), channel_id=1, source_target_pairs={{0,16},{1,17},{2,18},{3,19},{4,20},{5,21},{6,22},{7,23},{8,24},{9,... | collective-permute-start | bytes 196616 | tf_op jit(solution)/shard_map/ppermute | solution.py:443
  8.7 6.3 %collective-permute-start.2 = (bf16[256,128]{1,0:T(8,128)(2,1)}, bf16[256,128]{1,0:T(8,128)(2,1)S(1)}, u32[]{:S(2)}, u32[]{:S(2)}) collective-permute-start(bf16[256,128]{1,0:T(8,128)(2,1)} %get-tuple-element.40), channel_id=1, source_target_pairs={{0,24},{1,25},{2,26},{3,27},{4,28},{5,29},{6,30},{7,31},{8,16},{9,... | collective-permute-start | bytes 196616 | tf_op jit(solution)/shard_map/ppermute | solution.py:443
  15.0 0.8 %copy-start.8 = (bf16[256,128]{1,0:T(8,128)(2,1)S(1)}, bf16[256,128]{1,0:T(8,128)(2,1)}, u32[]{:S(2)}) copy-start(bf16[256,128]{1,0:T(8,128)(2,1)} %get-tuple-element.37.refs_0_) | copy-start | bytes 196612
  15.9 17.0 %copy-start.9 = (bf16[64,512]{1,0:T(8,128)(2,1)S(1)}, bf16[64,512]{1,0:T(8,128)(2,1)}, u32[]{:S(2)}) copy-start(bf16[64,512]{1,0:T(8,128)(2,1)} %get-tuple-element.60.diag_ref) | copy-start | bytes 196612
  16.0 6.8 %collective-permute-start.3 = (bf16[640,128]{1,0:T(8,128)(2,1)S(1)}, bf16[640,128]{1,0:T(8,128)(2,1)S(1)}, u32[]{:S(2)}, u32[]{:S(2)}) collective-permute-start(bf16[640,128]{1,0:T(8,128)(2,1)S(1)} %get-tuple-element.42), channel_id=1, source_target_pairs={{0,2},{1,3},{2,0},{3,1},{4,6},{5,7},{6,4},{7,5},{8,10},{9,11},{10,... | collective-permute-start | bytes 491528 | tf_op jit(solution)/shard_map/ppermute | solution.py:443
  17.5 8.2 %collective-permute-start.4 = (bf16[640,128]{1,0:T(8,128)(2,1)S(1)}, bf16[640,128]{1,0:T(8,128)(2,1)S(1)}, u32[]{:S(2)}, u32[]{:S(2)}) collective-permute-start(bf16[640,128]{1,0:T(8,128)(2,1)S(1)} %get-tuple-element.43), channel_id=1, source_target_pairs={{0,4},{1,5},{2,6},{3,7},{4,0},{5,1},{6,2},{7,3},{8,12},{9,13},{10,... | collective-permute-start | bytes 491528 | tf_op jit(solution)/shard_map/ppermute | solution.py:443
  19.0 6.7 %collective-permute-start.5 = (bf16[640,128]{1,0:T(8,128)(2,1)S(1)}, bf16[640,128]{1,0:T(8,128)(2,1)S(1)}, u32[]{:S(2)}, u32[]{:S(2)}) collective-permute-start(bf16[640,128]{1,0:T(8,128)(2,1)S(1)} %get-tuple-element.44), channel_id=1, source_target_pairs={{0,6},{1,7},{2,4},{3,5},{4,2},{5,3},{6,0},{7,1},{8,14},{9,15},{10,... | collective-permute-start | bytes 491528 | tf_op jit(solution)/shard_map/ppermute | solution.py:443
  25.9 2.4 %collective-permute-start.6 = (bf16[4,640,128]{2,1,0:T(8,128)(2,1)S(1)}, bf16[4,640,128]{2,1,0:T(8,128)(2,1)S(1)}, u32[]{:S(2)}, u32[]{:S(2)}) collective-permute-start(bf16[4,640,128]{2,1,0:T(8,128)(2,1)S(1)} %pad_maximum_fusion.mine_ref), channel_id=1, source_target_pairs={{0,1},{1,0},{2,3},{3,2},{4,5},{5,4},{6,7},{7,6},{8,9},{9,8},{10,11... | collective-permute-start | bytes 1966088 | tf_op jit(solution)/shard_map/ppermute | solution.py:443
  25.9 0.9 %copy-start.3 = (bf16[4,128,128]{2,1,0:T(8,128)(2,1)S(1)}, bf16[4,128,128]{2,1,0:T(8,128)(2,1)}, u32[]{:S(2)}) copy-start(bf16[4,128,128]{2,1,0:T(8,128)(2,1)} %cot_ref.1) | copy-start | bytes 393220
  26.8 0.9 %copy-start.4 = (bf16[1024,128]{1,0:T(8,128)(2,1)S(1)}, bf16[1024,128]{1,0:T(8,128)(2,1)}, u32[]{:S(2)}) copy-start(bf16[1024,128]{1,0:T(8,128)(2,1)} %out_w_ref.1) | copy-start | bytes 786436
  28.2 0.9 %copy-start.1 = (bf16[256,256]{1,0:T(8,128)(2,1)S(1)}, bf16[256,256]{1,0:T(8,128)(2,1)}, u32[]{:S(2)}) copy-start(bf16[256,256]{1,0:T(8,128)(2,1)} %get-tuple-element.48.normed_ref) | copy-start | bytes 393220
  32.9 4.6 %copy-start.2 = (bf16[256,256]{1,0:T(8,128)(2,1)S(1)}, bf16[256,256]{1,0:T(8,128)(2,1)}, u32[]{:S(2)}) copy-start(bf16[256,256]{1,0:T(8,128)(2,1)} %get-tuple-element.48.normed_ref) | copy-start | bytes 393220
  32.9 4.6 %copy-start.6 = (f32[256,128]{1,0:T(8,128)S(1)}, f32[256,128]{1,0:T(8,128)}, u32[]{:S(2)}) copy-start(f32[256,128]{1,0:T(8,128)} %get-tuple-element.54.recip_ref) | copy-start | bytes 393220
  32.9 4.6 %copy-start.10 = (f32[256]{0:T(256)S(1)}, f32[256]{0:T(256)}, u32[]{:S(2)}) copy-start(f32[256]{0:T(256)} %param.8) | copy-start | bytes 3076
  32.9 4.6 %copy-start.11 = (f32[128]{0:T(128)S(1)}, f32[128]{0:T(128)}, u32[]{:S(2)}) copy-start(f32[128]{0:T(128)} %param.12) | copy-start | bytes 1540
  34.0 1.6 %collective-permute-start.12 = (bf16[512,128]{1,0:T(8,128)(2,1)S(1)}, bf16[512,128]{1,0:T(8,128)(2,1)S(1)}, u32[]{:S(2)}, u32[]{:S(2)}) collective-permute-start(bf16[512,128]{1,0:T(8,128)(2,1)S(1)} %slice.64), channel_id=1, source_target_pairs={{0,1},{1,0},{2,3},{3,2},{4,5},{5,4},{6,7},{7,6},{8,9},{9,8},{10,11... | collective-permute-start | bytes 393224 | tf_op jit(solution)/shard_map/ppermute | solution.py:443
  34.6 1.6 %collective-permute-start.7 = (f32[80,256]{1,0:T(8,128)S(1)}, f32[80,256]{1,0:T(8,128)S(1)}, u32[]{:S(2)}, u32[]{:S(2)}) collective-permute-start(f32[80,256]{1,0:T(8,128)S(1)} %get-tuple-element.51), channel_id=1, source_target_pairs={{0,1},{1,0},{2,3},{3,2},{4,5},{5,4},{6,7},{7,6},{8,9},{9,8},{10,11... | collective-permute-start | bytes 245768 | tf_op jit(solution)/shard_map/ppermute | solution.py:443
  35.6 5.8 %collective-permute-start.13 = (bf16[256,128]{1,0:T(8,128)(2,1)S(1)}, bf16[256,128]{1,0:T(8,128)(2,1)S(1)}, u32[]{:S(2)}, u32[]{:S(2)}) collective-permute-start(bf16[256,128]{1,0:T(8,128)(2,1)S(1)} %slice.65), channel_id=1, source_target_pairs={{0,2},{1,3},{2,0},{3,1},{4,6},{5,7},{6,4},{7,5},{8,10},{9,11},{10,... | collective-permute-start | bytes 196616 | tf_op jit(solution)/shard_map/ppermute | solution.py:443
  36.3 4.1 %collective-permute-start.8 = (bf16[80,256]{1,0:T(8,128)(2,1)S(1)}, bf16[80,256]{1,0:T(8,128)(2,1)S(1)}, u32[]{:S(2)}, u32[]{:S(2)}) collective-permute-start(bf16[80,256]{1,0:T(8,128)(2,1)S(1)} %add_convert_fusion), channel_id=1, source_target_pairs={{0,3},{1,2},{2,1},{3,0},{4,7},{5,6},{6,5},{7,4},{8,11},{9,10},{10,... | collective-permute-start | bytes 122888 | tf_op jit(solution)/shard_map/ppermute | solution.py:443
  40.4 3.5 %collective-permute-start.9 = (bf16[80,256]{1,0:T(8,128)(2,1)S(1)}, bf16[80,256]{1,0:T(8,128)(2,1)S(1)}, u32[]{:S(2)}, u32[]{:S(2)}) collective-permute-start(bf16[80,256]{1,0:T(8,128)(2,1)S(1)} %add.25), channel_id=1, source_target_pairs={{0,5},{1,4},{2,7},{3,6},{4,1},{5,0},{6,3},{7,2},{8,13},{9,12},{10,... | collective-permute-start | bytes 122888 | tf_op jit(solution)/shard_map/ppermute | solution.py:443
  41.5 4.0 %collective-permute-start.14 = (bf16[128,128]{1,0:T(8,128)(2,1)S(1)}, bf16[128,128]{1,0:T(8,128)(2,1)S(1)}, u32[]{:S(2)}, u32[]{:S(2)}) collective-permute-start(bf16[128,128]{1,0:T(8,128)(2,1)S(1)} %slice.66), channel_id=1, source_target_pairs={{0,4},{1,5},{2,6},{3,7},{4,0},{5,1},{6,2},{7,3},{8,12},{9,13},{10,... | collective-permute-start | bytes 98312 | tf_op jit(solution)/shard_map/ppermute | solution.py:443
  43.9 3.5 %collective-permute-start.10 = (bf16[80,256]{1,0:T(8,128)(2,1)S(1)}, bf16[80,256]{1,0:T(8,128)(2,1)S(1)}, u32[]{:S(2)}, u32[]{:S(2)}) collective-permute-start(bf16[80,256]{1,0:T(8,128)(2,1)S(1)} %add.26), channel_id=1, source_target_pairs={{0,9},{1,8},{2,11},{3,10},{4,13},{5,12},{6,15},{7,14},{8,1},{9,0},... | collective-permute-start | bytes 122888 | tf_op jit(solution)/shard_map/ppermute | solution.py:443
  45.5 4.0 %collective-permute-start.15 = (bf16[64,128]{1,0:T(8,128)(2,1)S(1)}, bf16[64,128]{1,0:T(8,128)(2,1)S(1)}, u32[]{:S(2)}, u32[]{:S(2)}) collective-permute-start(bf16[64,128]{1,0:T(8,128)(2,1)S(1)} %slice.67), channel_id=1, source_target_pairs={{0,8},{1,9},{2,10},{3,11},{4,12},{5,13},{6,14},{7,15},{8,0},{9,1},... | collective-permute-start | bytes 49160 | tf_op jit(solution)/shard_map/ppermute | solution.py:443
  47.4 5.5 %collective-permute-start.11 = (bf16[80,256]{1,0:T(8,128)(2,1)S(1)}, bf16[80,256]{1,0:T(8,128)(2,1)S(1)}, u32[]{:S(2)}, u32[]{:S(2)}) collective-permute-start(bf16[80,256]{1,0:T(8,128)(2,1)S(1)} %add.27.own_ref), channel_id=1, source_target_pairs={{0,17},{1,16},{2,19},{3,18},{4,21},{5,20},{6,23},{7,22},{8,25},{9,... | collective-permute-start | bytes 122888 | tf_op jit(solution)/shard_map/ppermute | solution.py:443
  49.5 4.6 %collective-permute-start.16 = (bf16[32,128]{1,0:T(8,128)(2,1)S(1)}, bf16[32,128]{1,0:T(8,128)(2,1)S(1)}, u32[]{:S(2)}, u32[]{:S(2)}) collective-permute-start(bf16[32,128]{1,0:T(8,128)(2,1)S(1)} %slice.68), channel_id=1, source_target_pairs={{0,16},{1,17},{2,18},{3,19},{4,20},{5,21},{6,22},{7,23},{8,24},{9,... | collective-permute-start | bytes 24584 | tf_op jit(solution)/shard_map/ppermute | solution.py:443

commit v3 on v2

--- a/solution.py
+++ b/solution.py
@@ -195,7 +195,7 @@
 def factor_kernel(
     x_hbm, gain_hbm, w1_hbm, w2_hbm, cot_hbm,
     send0_ref, send1_ref, send2_ref, send3_ref, scaled_ref, normed_ref, recip_ref, diag_ref,
-    x_ref, gain_ref, w1_ref, w2_ref, cot_ref, rows, recips, twin, cots, moved, sems,
+    x_ref, gain_ref, w1_ref, w2_ref, cot_ref, rows, twin, cots, moved, sems,
 ):
     copies = fetch(
         [(x_hbm, x_ref), (gain_hbm, gain_ref), (w1_hbm, w1_ref), (w2_hbm, w2_ref), (cot_hbm, cot_ref)],
@@ -207,20 +207,19 @@
     columns = cot_ref.shape[1]
     devices = columns // res
     copies[0].wait()
-    x = x_ref[...].astype(f32)
-    centred = x - jnp.mean(x, axis=-1, keepdims=True)
-    recip = lax.rsqrt(jnp.mean(centred * centred, axis=-1, keepdims=True) + ln_epsilon)
-    rows[...] = centred * recip
-    recips[...] = jnp.broadcast_to(recip, recips.shape)
+    rows[...] = x_ref[...].astype(f32)
     for copy in copies[1:]:
         copy.wait()
     both = jnp.concatenate([w1_ref[...], w2_ref[...]], axis=0)
     low = lax.broadcasted_iota(jnp.int32, (hidden, 2 * seqs), 1) < seqs
     for r in range(res):
-        scaled = rows[:, r, :]
+        x = rows[:, r, :]
+        centred = x - jnp.mean(x, axis=-1, keepdims=True)
+        recip = lax.rsqrt(jnp.mean(centred * centred, axis=-1, keepdims=True) + ln_epsilon)
+        scaled = centred * recip
         at = slice(r * seqs, (r + 1) * seqs)
         scaled_ref[at, :] = scaled
-        recip_ref[at, :] = recips[:, r, :]
+        recip_ref[at, :] = jnp.broadcast_to(recip, (seqs, recip_ref.shape[1]))
         normed = (scaled * gain_ref[...]).astype(bf16)
         normed_ref[at, :] = normed
         twin[r] = mm_t(both, jnp.concatenate([normed, normed], axis=0))
@@ -239,14 +238,20 @@
     for r in range(res):
         for q in range(res):
             block = cots[pl.ds(r * columns + q, devices, stride=res), :]
-            moved[pl.ds(r * res + q, devices, stride=res * res), :] = block
+            at = (r * res + q) * (devices + 1)
+            moved[at : at + devices, :] = block
     index = lax.axis_index("row")
     per = res * res
     plane = devices // len(sends)
     for n in range(devices):
-        at = pl.multiple_of(lax.bitwise_xor(index, n) * per, per)
+        block = moved[pl.ds(lax.bitwise_xor(index, n), per, stride=devices + 1), :]
         to = res * hidden + n % plane * per
-        sends[n // plane][to : to + per, :] = moved[pl.ds(at, per), :].astype(bf16)
+        sends[n // plane][to : to + per, :] = block.astype(bf16)
+
+
+def own_kernel(*refs):
+    for a, b in zip(refs[: len(refs) // 2], refs[len(refs) // 2 :]):
+        b[...] = a[...]
 
 
 def pack_kernel(height, *refs):
@@ -261,12 +266,13 @@
 
 
 def prepare_kernel(
-    out_w_ref, cot_ref,
-    cot_t_ref, twin_left_ref, twin_right_ref, bias_ref,
+    out_w_ref, cot_ref, scaled_in, w1_in, w2_in,
+    cot_t_ref, twin_left_ref, twin_right_ref, bias_ref, scaled_ref, w1_ref, w2_ref,
     wide,
 ):
     hidden = twin_left_ref.shape[0] // 2
     res, columns, pairs = cot_ref.shape
+    own_kernel(scaled_in, w1_in, w2_in, scaled_ref, w1_ref, w2_ref)
     wide[...] = out_w_ref[...].astype(f32)
     for d in range(hidden):
         at = (d % 2) * hidden
@@ -286,13 +292,13 @@
 
 
 def sums_kernel(
-    mine_ref, other_ref, cot_t_ref, twin_left_ref, twin_right_ref, normed_ref, scaled_ref,
-    w1_ref, w2_ref, bias_ref,
-    small_ref, rights_ref, spread_ref, grad_ref,
-    wide, lefts, turned, cots, got_t,
+    yxs, cot_t_ref, twin_left_ref, twin_right_ref, normed_ref, scaled_ref,
+    w1_ref, w2_ref, bias_ref, *refs,
 ):
+    mine, other = refs[:yxs], refs[yxs : 2 * yxs]
+    small_ref, rights_ref, spread_ref, grad_ref, wide, lefts, turned, cots, got_t = refs[2 * yxs :]
     columns = rights_ref.shape[0]
-    yxs, _, lanes = mine_ref.shape
+    lanes = mine[0].shape[1]
     seqs = lanes // 2
     channels = normed_ref.shape[1]
     hidden = w1_ref.shape[0]
@@ -302,32 +308,38 @@
     index = lax.axis_index("row")
     height = res * hidden
     per = res * res
-    zs = wide.shape[0] // (2 * yxs * height)
+    zs = columns // (2 * yxs * res)
     for yx in range(yxs):
         for z in range(zs):
             factors = slice(z * height, (z + 1) * height)
             first = zs * height + z * 2 * per
-            for core, ref in enumerate((mine_ref, other_ref)):
+            for core, ref in enumerate((mine[yx], other[yx])):
                 device = lax.bitwise_xor(index, z * 2 * yxs + yx * 2 + core)
-                at = pl.multiple_of(device * height, height)
-                wide[pl.ds(at, height), :] = ref[yx, factors, :].astype(f32)
-                block = ref[yx, first + core * per : first + (core + 1) * per, :]
+                block = ref[factors, :].astype(f32)
+                for r in range(res):
+                    wide[pl.ds(device * res + r, hidden, stride=columns + 1), :] = block[
+                        r * hidden : (r + 1) * hidden
+                    ]
+                block = ref[first + core * per : first + (core + 1) * per, :]
                 at = pl.multiple_of(device * per, per)
                 cots[pl.ds(at, per), :] = block.astype(f32)
     for r in range(res):
         got_t[r * pairs : (r + 1) * pairs, :] = cots[pl.ds(r, columns, stride=res), :].T.astype(bf16)
     for q in range(twins):
         here = slice(q * lanes, (q + 1) * lanes)
-        lefts[:, here] = wide[pl.ds(q, columns, stride=hidden), :].astype(bf16)
-        rights_ref[:, here] = wide[pl.ds(twins + q, columns, stride=hidden), :].astype(bf16)
+        at = q * (columns + 1)
+        lefts[:, here] = wide[at : at + columns, :].astype(bf16)
+        at = (twins + q) * (columns + 1)
+        rights_ref[:, here] = wide[at : at + columns, :].astype(bf16)
 
     def summed(cots, factors, weights, out):
-        for r in range(res):
-            block = mm(cots[r * pairs : (r + 1) * pairs, :], factors[...]).astype(bf16)
-            for q in range(twins):
-                out[q * pairs : (q + 1) * pairs, r * lanes : (r + 1) * lanes] = block[
-                    :, q * lanes : (q + 1) * lanes
-                ]
+        for q in range(0, twins, 2):
+            block = mm(cots[...], factors[:, q * lanes : (q + 2) * lanes]).astype(bf16)
+            for r in range(res):
+                for e in range(2):
+                    out[(q + e) * pairs : (q + e + 1) * pairs, r * lanes : (r + 1) * lanes] = block[
+                        r * pairs : (r + 1) * pairs, e * lanes : (e + 1) * lanes
+                    ]
         t = mm(weights[...], out[...]).T
         parts = [
             t[r * lanes : r * lanes + seqs, :hidden] + t[r * lanes + seqs : (r + 1) * lanes, hidden:]
@@ -340,13 +352,19 @@
     normed_grad = mm(left_sum.astype(bf16), w1_ref[...]) + mm(right_sum.astype(bf16), w2_ref[...])
     grad_ref[...] = normed_grad
     factors_t = jnp.concatenate([left_sum, right_sum], axis=1).T.astype(bf16)
-    small_ref[: 2 * hidden, :] = mm(factors_t, normed_ref[...])
+    weights = mm(factors_t, normed_ref[...])
     gain_part = jnp.sum(normed_grad * scaled_ref[...], axis=0, keepdims=True)
-    bias_part = jnp.concatenate([bias_ref[:1, :]] * (channels // pairs), axis=1)
-    line = lax.broadcasted_iota(jnp.int32, (16, channels), 0)
-    small_ref[2 * hidden :, :] = jnp.where(
-        line == 0, gain_part, jnp.where(line == 1, bias_part, jnp.zeros((16, channels), f32))
-    )
+    line = lax.broadcasted_iota(jnp.int32, (16, pairs), 0)
+    parts = channels // pairs
+    rows = small_ref.shape[0] // parts
+    for n in range(parts):
+        here = slice(n * pairs, (n + 1) * pairs)
+        small_ref[n * rows : n * rows + 2 * hidden, :] = weights[:, here]
+        small_ref[n * rows + 2 * hidden : (n + 1) * rows, :] = jnp.where(
+            line == 0,
+            gain_part[:, here],
+            jnp.where(line == 1, bias_ref[:1, :], jnp.zeros((16, pairs), f32)),
+        )
 
 
 def share_kernel(res, diag_ref, spread_ref, out_ref, outs):
@@ -356,14 +374,15 @@
     grad = mm_t(diag_ref[...], spread_ref[...]) * (1.0 / seqs)
     for d in range(hidden):
         at = (d % 2) * hidden
-        outs[pl.ds(d, hidden, stride=hidden), :] = grad[
+        outs[d * (hidden + 1) : d * (hidden + 1) + hidden, :] = grad[
             at : at + hidden, (d // 2) * pairs : (d // 2 + 1) * pairs
         ]
     index = lax.axis_index("row")
     for place in range(hidden):
-        chunk = lax.bitwise_xor(index, int(format(place, "05b")[::-1], 2))
-        at = pl.multiple_of(chunk * hidden, hidden)
-        out_ref[place * hidden : (place + 1) * hidden, :] = outs[pl.ds(at, hidden), :]
+        chunk = lax.bitwise_xor(index, place % 4 * 8 + place // 4 % 4 * 2 + place // 16)
+        out_ref[place * hidden : (place + 1) * hidden, :] = outs[
+            pl.ds(chunk, hidden, stride=hidden + 1), :
+        ]
 
 
 def result_kernel(
@@ -396,22 +415,53 @@
     grad_ref[...] = rows[...].astype(bf16)
 
 
+def split(small, out, small_ref, out_ref, sends):
+    small = small.astype(bf16)
+    rows = out_ref.shape[0]
+    small_ref[...] = small
+    out_ref[...] = out[:rows]
+    for k, send in enumerate(sends):
+        send[: small.shape[0], :] = small
+        send[small.shape[0] :, :] = out[(k + 1) * rows : (k + 2) * rows].astype(bf16)
+
+
+def total(small_ref, out_ref, came):
+    height = small_ref.shape[0]
+    one, two, three = (c[:height, :].astype(f32) for c in came)
+    small = (small_ref[...].astype(f32) + one) + (two + three)
+    one, two, three = (c[height:, :].astype(f32) for c in came)
+    return small, (out_ref[...] + one) + (two + three)
+
+
+def join_kernel(small_in, small_came, out_in, out_came, small_ref, out_ref, *sends):
+    kept = out_in[: out_came.shape[0], :] + out_came[...].astype(f32)
+    split(small_in[...] + small_came[...], kept, small_ref, out_ref, sends)
+
+
+def merge_kernel(small_in, out_in, one, two, three, small_ref, out_ref, *sends):
+    small, out = total(small_in, out_in, (one, two, three))
+    split(small, out, small_ref, out_ref, sends)
+
+
 def finish_kernel(
-    scale, own_ref, came_ref, keep_ref, shared_ref,
+    scale, small_in, out_in, one, two, three,
     gain_hbm, left_hbm, right_hbm, out_hbm, bias_hbm,
-    total, out, sems,
+    whole, out_ref, sems,
 ):
     hidden = left_hbm.shape[0]
     pairs = bias_hbm.shape[1]
-    total[...] = (own_ref[...].astype(f32) + came_ref[...].astype(f32)) * scale
-    out[...] = (keep_ref[...] + shared_ref[...].astype(f32)) * scale
+    small, out = total(small_in, out_in, (one, two, three))
+    rows = whole.shape[0]
+    for n in range(whole.shape[1] // pairs):
+        whole[:, n * pairs : (n + 1) * pairs] = small[n * rows : (n + 1) * rows] * scale
+    out_ref[...] = out * scale
     copies = fetch(
         [
-            (total.at[2 * hidden : 2 * hidden + 1, :], gain_hbm),
-            (total.at[:hidden, :], left_hbm),
-            (total.at[hidden : 2 * hidden, :], right_hbm),
-            (out, out_hbm),
-            (total.at[2 * hidden + 1 : 2 * hidden + 2, :pairs], bias_hbm),
+            (whole.at[2 * hidden : 2 * hidden + 1, :], gain_hbm),
+            (whole.at[:hidden, :], left_hbm),
+            (whole.at[hidden : 2 * hidden, :], right_hbm),
+            (out_ref, out_hbm),
+            (whole.at[2 * hidden + 1 : 2 * hidden + 2, :pairs], bias_hbm),
         ],
         sems,
     )
@@ -485,53 +535,65 @@
             ((hidden, channels), bf16),
             ((res, columns, pairs), bf16),
             ((seqs, res, channels), f32),
-            ((seqs, res, 128), f32),
             ((res, 2 * hidden, lanes), f32),
             ((res * columns, pairs), f32),
-            ((res * columns, pairs), f32),
+            ((res * res * (count + 1), pairs), f32),
         ],
         10**6,
         remote_in=True,
         vmem=60,
     )
     swapped = {z: swap(sends[z], z * 2 * yxs) for z in (3, 2, 1)}
+    own_send, normed = call(
+        own_kernel,
+        "own",
+        (sends[0], normed),
+        [(sends[0].shape, bf16), (normed.shape, bf16)],
+        [],
+        10**6,
+    )
     sent = call(
         functools.partial(pack_kernel, height),
         "pack",
-        [sends[0]] + [swapped[z] for z in range(1, zs)],
+        [own_send] + [swapped[z] for z in range(1, zs)],
         [((zs * height + zs * 2 * res * res, lanes), bf16)] * yxs,
         [],
         10**6,
     )
-    mine = jnp.stack([sent[0]] + [swap(sent[yx], yx * 2) for yx in range(1, yxs)])
-    other = swap(mine, 1)
-    cot_t, twin_left, twin_right, bias_part = call(
+    mine = [sent[0]] + [swap(sent[yx], yx * 2) for yx in range(1, yxs)]
+    prepared = call(
         prepare_kernel,
         "prepare",
-        (output_projection_matrix, pair_cotangent),
+        (output_projection_matrix, pair_cotangent, scaled, w1, w2),
         [
             ((res * pairs, columns), bf16),
             (wide, bf16),
             (wide, bf16),
             ((8, pairs), f32),
+            (scaled.shape, f32),
+            (w1.shape, bf16),
+            (w2.shape, bf16),
         ],
         [((hidden * hidden, pairs), f32)],
         10**6,
     )
+    mine[0], prepared = lax.optimization_barrier((mine[0], prepared))
+    cot_t, twin_left, twin_right, bias_part, scaled, w1, w2 = prepared
+    other = [swap(m, 1) for m in mine]
     small, rights, spread, normed_grad = call(
-        sums_kernel,
+        functools.partial(sums_kernel, yxs),
         "sums",
         (
-            mine, other, cot_t, twin_left, twin_right, normed, scaled, w1, w2, bias_part,
+            cot_t, twin_left, twin_right, normed, scaled, w1, w2, bias_part, *mine, *other,
         ),
         [
-            ((2 * hidden + 16, channels), f32),
+            ((channels // pairs * (2 * hidden + 16), pairs), f32),
             ((columns, hidden * seqs), bf16),
             ((twins * pairs, res * lanes), bf16),
             ((own, channels), f32),
         ],
         [
-            ((columns * hidden, lanes), f32),
+            (((columns + 1) * hidden, lanes), f32),
             ((columns, hidden * seqs), bf16),
             ((twins * pairs, res * lanes), bf16),
             ((res * columns, pairs), f32),
@@ -544,7 +606,7 @@
         "shares",
         (diag, spread),
         [((hidden * hidden, pairs), f32)],
-        [((hidden * hidden, pairs), f32)],
+        [((hidden * (hidden + 1), pairs), f32)],
         10**6,
     )
     delta, grad = call(
@@ -555,27 +617,32 @@
         [((seqs, res, channels), f32), ((hidden * seqs, res * pairs), bf16)],
         10**6,
     )
+    height = small.shape[0]
     half = hidden * hidden // 2
-    small = (small + swap(small, 1)).astype(bf16)
-    step = 1
-    while step < count:
-        keep, give = out_part[:half], out_part[half:].astype(bf16)
-        if 2 * step < count:
-            out_part = keep + swap(give, step).astype(f32)
-        if step > 1:
-            small = lax.optimization_barrier(small)
-            came = swap(small, step + 1)
-            if 2 * step < count:
-                small = small + came
-            if step == 2:
-                small, delta, grad = lax.optimization_barrier((small, delta, grad))
-        step *= 2
-        half //= 2
-    shared = swap(give, count // 2)
+
+    def step(kernel, name, args, rows):
+        kept, out, *sends = call(
+            kernel,
+            name,
+            args,
+            [((height, pairs), bf16), ((rows, pairs), f32)] + [((height + rows, pairs), bf16)] * 3,
+            [],
+            10**6,
+        )
+        return kept, out, sends
+
+    out_came = swap(out_part[half:].astype(bf16), 1)
+    kept, out, sends = step(
+        join_kernel, "join", (small, swap(small, 1), out_part, out_came), half // yxs
+    )
+    came = {k: swap(sends[k - 1], k * 2) for k in (3, 1, 2)}
+    kept, delta, grad = lax.optimization_barrier((kept, delta, grad))
+    kept, out, sends = step(merge_kernel, "merge", (kept, out, came[1], came[2], came[3]), half // yxs // zs)
+    came = {k: swap(sends[k - 1], k * 2 * yxs) for k in (3, 2, 1)}
     gain_out, left_out, right_out, out_share, bias_out = call(
         functools.partial(finish_kernel, 1.0 / columns),
         "finish",
-        (small, came, keep, shared),
+        (kept, out, came[1], came[2], came[3]),
         [
             ((1, channels), f32),
             ((hidden, channels), f32),

time: 55.1 us -> 48.4 us (0.88)
  waiting for transfers between devices: 20.8 us -> 13.4 us
  local copies, waits for them, and re-layouts: 3.67 us -> 6.02 us
  Pallas kernels: 10.3 us -> 9 us
    ppermute x17 -> x18, waiting for transfers between devices: 20.8 us -> 13.4 us  [swap(): return lax.ppermute(value, 'row', [(i, i ^ step) for i in range(count)])]
    unnamed x24 -> x22, local copies, waits for them, and re-layouts: 3.63 us -> 6 us
    pallas_call x7 -> x10, Pallas kernels: 10.3 us -> 9 us  [call(): pl.pallas_call(kernel, out_shape=[jax.ShapeDtypeStruct(s, d) for s, d in...]
    ppermute x17 -> x18, starting transfers between devices: 19 us -> 18.9 us  [swap(): return lax.ppermute(value, 'row', [(i, i ^ step) for i in range(count)])]
  transfers between devices with their start and end apart: 17 -> 18, of which waited for: 11 -> 9; matrix products, arithmetic and copies ran while one was open for 0% -> 0% of each run, Pallas kernels for 4% -> 5%
where the time goes in v3:
time: 48.4 us; the launch traced here: 48 us
  starting transfers between devices  18.9 us (39%)
  waiting for transfers between devices  13.4 us (28%)
  Pallas kernels  9 us (19%)
  local copies, waits for them, and re-layouts  6.02 us (12%)
  between operations  0.77 us (2%)
    ppermute x18, starting transfers between devices, swap(): return lax.ppermute(value, 'row', [(i, i ^ step) for i in range(count)])  18.9 us
    ppermute x18, waiting for transfers between devices, swap(): return lax.ppermute(value, 'row', [(i, i ^ step) for i in range(count)])  13.4 us
    pallas_call x10, Pallas kernels, call(): pl.pallas_call(kernel, out_shape=[jax.ShapeDtypeStruct(s, d) for s, d in...  9 us
    unnamed x22, local copies, waits for them, and re-layouts  6 us
  transfers between devices with their start and end apart: 18, of which 9 were waited for; matrix products, arithmetic and copies ran while one was open for 0% of the time, Pallas kernels for 5%

profile of v3, /device:TPU:0, one launch (start us, length us, event | category | flops | bytes accessed | tf_op | source)
XLA Modules:
  0.0 48.0 jit_solution(936213927257573524)
XLA Ops:
  0.6 2.3 %factors.1 = (bf16[256,128]{1,0:T(8,128)(2,1)}, bf16[256,128]{1,0:T(8,128)(2,1)}, bf16[256,128]{1,0:T(8,128)(2,1)}, bf16[256,128]{1,0:T(8,128)(2,1)}, f32[256,25...) custom-call(bf16[64,4,256]{2,1,0:T(4,128)(2,1)} %x_hbm.1, ...), custom_call_target="tpu_custom_call" | custom-call | flops 1000000 | bytes 295936 | tf_op jit(solution)/shard_map/factors/pallas_call | solution.py:479
  3.0 3.1 %collective-permute-start = (bf16[256,128]{1,0:T(8,128)(2,1)}, bf16[256,128]{1,0:T(8,128)(2,1)S(1)}, u32[]{:S(2)}, u32[]{:S(2)}) collective-permute-start(bf16[256,128]{1,0:T(8,128)(2,1)} %get-tuple-element.63), channel_id=1, source_target_pairs={{0,8},{1,9},{2,10},{3,11},{4,12},{5,13},{6,14},{7,15},{8,0},{9,1},... | collective-permute-start | bytes 196616 | tf_op jit(solution)/shard_map/ppermute | solution.py:493
  6.0 2.6 %collective-permute-start.1 = (bf16[256,128]{1,0:T(8,128)(2,1)}, bf16[256,128]{1,0:T(8,128)(2,1)S(1)}, u32[]{:S(2)}, u32[]{:S(2)}) collective-permute-start(bf16[256,128]{1,0:T(8,128)(2,1)} %get-tuple-element.64), channel_id=1, source_target_pairs={{0,16},{1,17},{2,18},{3,19},{4,20},{5,21},{6,22},{7,23},{8,24},{9,... | collective-permute-start | bytes 196616 | tf_op jit(solution)/shard_map/ppermute | solution.py:493
  8.6 0.9 %copy-done.4 = bf16[256,256]{1,0:T(8,128)(2,1)S(1)} copy-done((bf16[256,256]{1,0:T(8,128)(2,1)S(1)}, bf16[256,256]{1,0:T(8,128)(2,1)}, u32[]{:S(2)}) %copy-start.4) | copy-done | bytes 131096
  9.5 0.8 %copy-done.5 = bf16[256,128]{1,0:T(8,128)(2,1)S(1)} copy-done((bf16[256,128]{1,0:T(8,128)(2,1)S(1)}, bf16[256,128]{1,0:T(8,128)(2,1)}, u32[]{:S(2)}) %copy-start.5) | copy-done | bytes 65560
  10.4 3.1 %collective-permute-done.1.refs_2_ = bf16[256,128]{1,0:T(8,128)(2,1)S(1)} collective-permute-done((bf16[256,128]{1,0:T(8,128)(2,1)}, bf16[256,128]{1,0:T(8,128)(2,1)S(1)}, u32[]{:S(2)}, u32[]{:S(2)}) %collective-permute-start.1) | collective-permute-done | bytes 65568 | tf_op jit(solution)/shard_map/ppermute | solution.py:493
  13.5 1.4 %collective-permute-done.2.refs_3_ = bf16[256,128]{1,0:T(8,128)(2,1)S(1)} collective-permute-done((bf16[256,128]{1,0:T(8,128)(2,1)}, bf16[256,128]{1,0:T(8,128)(2,1)S(1)}, u32[]{:S(2)}, u32[]{:S(2)}) %collective-permute-start.2) | collective-permute-done | bytes 65568 | tf_op jit(solution)/shard_map/ppermute | solution.py:493
  15.0 1.6 %collective-permute-start.3 = (bf16[640,128]{1,0:T(8,128)(2,1)S(1)}, bf16[640,128]{1,0:T(8,128)(2,1)S(1)}, u32[]{:S(2)}, u32[]{:S(2)}) collective-permute-start(bf16[640,128]{1,0:T(8,128)(2,1)S(1)} %get-tuple-element.84), channel_id=1, source_target_pairs={{0,2},{1,3},{2,0},{3,1},{4,6},{5,7},{6,4},{7,5},{8,10},{9,11},{10,... | collective-permute-start | bytes 491528 | tf_op jit(solution)/shard_map/ppermute | solution.py:493
  16.6 1.5 %collective-permute-start.4 = (bf16[640,128]{1,0:T(8,128)(2,1)S(1)}, bf16[640,128]{1,0:T(8,128)(2,1)S(1)}, u32[]{:S(2)}, u32[]{:S(2)}) collective-permute-start(bf16[640,128]{1,0:T(8,128)(2,1)S(1)} %get-tuple-element.85), channel_id=1, source_target_pairs={{0,4},{1,5},{2,6},{3,7},{4,0},{5,1},{6,2},{7,3},{8,12},{9,13},{10,... | collective-permute-start | bytes 491528 | tf_op jit(solution)/shard_map/ppermute | solution.py:493
  18.1 0.5 collective-permute-start.5
  18.6 0.9 %copy-done = bf16[4,128,128]{2,1,0:T(8,128)(2,1)S(1)} copy-done((bf16[4,128,128]{2,1,0:T(8,128)(2,1)S(1)}, bf16[4,128,128]{2,1,0:T(8,128)(2,1)}, u32[]{:S(2)}) %copy-start) | copy-done | bytes 131096
  19.5 0.9 %copy-done.1 = bf16[1024,128]{1,0:T(8,128)(2,1)S(1)} copy-done((bf16[1024,128]{1,0:T(8,128)(2,1)S(1)}, bf16[1024,128]{1,0:T(8,128)(2,1)}, u32[]{:S(2)}) %copy-start.1) | copy-done | bytes 262168
  20.4 0.9 %copy-done.2 = f32[256,256]{1,0:T(8,128)S(1)} copy-done((f32[256,256]{1,0:T(8,128)S(1)}, f32[256,256]{1,0:T(8,128)}, u32[]{:S(2)}) %copy-start.2) | copy-done | bytes 262168
  21.4 0.7 %copy-done.6 = bf16[256,32]{0,1:T(8,128)(2,1)S(1)} copy-done((bf16[256,32]{0,1:T(8,128)(2,1)S(1)}, bf16[256,32]{0,1:T(8,128)(2,1)}, u32[]{:S(2)}) %copy-start.6) | copy-done | bytes 16408
  22.1 0.7 %copy-done.7 = bf16[256,32]{0,1:T(8,128)(2,1)S(1)} copy-done((bf16[256,32]{0,1:T(8,128)(2,1)S(1)}, bf16[256,32]{0,1:T(8,128)(2,1)}, u32[]{:S(2)}) %copy-start.7) | copy-done | bytes 16408
  23.3 0.5 %collective-permute-start.7 = (bf16[640,128]{1,0:T(8,128)(2,1)S(1)}, bf16[640,128]{1,0:T(8,128)(2,1)S(1)}, u32[]{:S(2)}, u32[]{:S(2)}) collective-permute-start(bf16[640,128]{1,0:T(8,128)(2,1)S(1)} %collective-permute-done.3.refs_1_), channel_id=1, source_target_pairs={{0,1},{1,0},{2,3},{3,2},{4,5},{5,4},{6,7},{7,6},{8,9},{9,8},{10,11... | collective-permute-start | bytes 491528 | tf_op jit(solution)/shard_map/ppermute | solution.py:493
  23.8 1.0 %collective-permute-done.4.refs_2_ = bf16[640,128]{1,0:T(8,128)(2,1)S(1)} collective-permute-done((bf16[640,128]{1,0:T(8,128)(2,1)S(1)}, bf16[640,128]{1,0:T(8,128)(2,1)S(1)}, u32[]{:S(2)}, u32[]{:S(2)}) %collective-permute-start.4) | collective-permute-done | bytes 163872 | tf_op jit(solution)/shard_map/ppermute | solution.py:493
  24.8 0.5 %collective-permute-start.9 = (bf16[640,128]{1,0:T(8,128)(2,1)S(1)}, bf16[640,128]{1,0:T(8,128)(2,1)S(1)}, u32[]{:S(2)}, u32[]{:S(2)}) collective-permute-start(bf16[640,128]{1,0:T(8,128)(2,1)S(1)} %collective-permute-done.5.refs_3_), channel_id=1, source_target_pairs={{0,1},{1,0},{2,3},{3,2},{4,5},{5,4},{6,7},{7,6},{8,9},{9,8},{10,11... | collective-permute-start | bytes 491528 | tf_op jit(solution)/shard_map/ppermute | solution.py:493
  25.3 0.9 %collective-permute-done.8.refs_6_ = bf16[640,128]{1,0:T(8,128)(2,1)S(1)} collective-permute-done((bf16[640,128]{1,0:T(8,128)(2,1)S(1)}, bf16[640,128]{1,0:T(8,128)(2,1)S(1)}, u32[]{:S(2)}, u32[]{:S(2)}) %collective-permute-start.8) | collective-permute-done | bytes 163872 | tf_op jit(solution)/shard_map/ppermute | solution.py:493
  26.4 2.7 %sums.1 = (f32[160,128]{1,0:T(8,128)S(1)}, bf16[128,2048]{1,0:T(8,128)(2,1)S(1)}, bf16[2048,512]{1,0:T(8,128)(2,1)S(1)}, f32[256,256]{1,0:T(8,128)S(1)}) custom-call(bf16[512,128]{1,0:T(8,128)(2,1)S(1)} %get-tuple-element.75.cot_t_ref, bf16[64,2048]{1,0:T(8,128)(2,1)S(1)} %get-tuple-element.76.twin_left_ref, ...), custom_call_target="tpu_custom_call" | custom-call | flops 1000000 | bytes 2396160 | tf_op jit(solution)/shard_map/sums/pallas_call | solution.py:479
  29.1 0.8 %shares.1.out_in = f32[1024,128]{1,0:T(8,128)S(1)} custom-call(bf16[64,512]{1,0:T(8,128)(2,1)S(1)} %copy-done.8, bf16[2048,512]{1,0:T(8,128)(2,1)S(1)} %get-tuple-element.89.spread_ref), custom_call_target="tpu_custom_call" | custom-call | flops 1000000 | bytes 2162688 | tf_op jit(solution)/shard_map/shares/pallas_call | solution.py:479
  30.5 1.1 %collective-permute-done.10.small_came = f32[160,128]{1,0:T(8,128)S(1)} collective-permute-done((f32[160,128]{1,0:T(8,128)S(1)}, f32[160,128]{1,0:T(8,128)S(1)}, u32[]{:S(2)}, u32[]{:S(2)}) %collective-permute-start.10) | collective-permute-done | bytes 81952 | tf_op jit(solution)/shard_map/ppermute | solution.py:493
  31.6 0.6 %collective-permute-start.12 = (bf16[288,128]{1,0:T(8,128)(2,1)S(1)}, bf16[288,128]{1,0:T(8,128)(2,1)S(1)}, u32[]{:S(2)}, u32[]{:S(2)}) collective-permute-start(bf16[288,128]{1,0:T(8,128)(2,1)S(1)} %get-tuple-element.100), channel_id=1, source_target_pairs={{0,2},{1,3},{2,0},{3,1},{4,6},{5,7},{6,4},{7,5},{8,10},{9,11},{10,... | collective-permute-start | bytes 221192 | tf_op jit(solution)/shard_map/ppermute | solution.py:493
  32.2 1.5 %collective-permute-start.13 = (bf16[288,128]{1,0:T(8,128)(2,1)S(1)}, bf16[288,128]{1,0:T(8,128)(2,1)S(1)}, u32[]{:S(2)}, u32[]{:S(2)}) collective-permute-start(bf16[288,128]{1,0:T(8,128)(2,1)S(1)} %get-tuple-element.101), channel_id=1, source_target_pairs={{0,4},{1,5},{2,6},{3,7},{4,0},{5,1},{6,2},{7,3},{8,12},{9,13},{10,... | collective-permute-start | bytes 221192 | tf_op jit(solution)/shard_map/ppermute | solution.py:493
  33.7 1.5 %collective-permute-start.14 = (bf16[288,128]{1,0:T(8,128)(2,1)S(1)}, bf16[288,128]{1,0:T(8,128)(2,1)S(1)}, u32[]{:S(2)}, u32[]{:S(2)}) collective-permute-start(bf16[288,128]{1,0:T(8,128)(2,1)S(1)} %get-tuple-element.102), channel_id=1, source_target_pairs={{0,6},{1,7},{2,4},{3,5},{4,2},{5,3},{6,0},{7,1},{8,14},{9,15},{10,... | collective-permute-start | bytes 221192 | tf_op jit(solution)/shard_map/ppermute | solution.py:493
  35.2 1.9 %results.1 = (bf16[4,128,128]{2,1,0:T(8,128)(2,1)}, bf16[64,4,256]{2,1,0:T(4,128)(2,1)}) custom-call(bf16[128,2048]{1,0:T(8,128)(2,1)S(1)} %get-tuple-element.91.rights_ref, bf16[64,2048]{1,0:T(8,128)(2,1)S(1)} %get-tuple-element.76.twin_left_ref, bf16[32,256]{1,0:T(8,128)(2,1)S(1)} %get-tuple-element.80.w1_ref, ...), custom_call_target="tpu_custom_call" | custom-call | flops 1000000 | bytes 1590784 | tf_op jit(solution)/shard_map/results/pallas_call | solution.py:479
  37.1 1.8 %collective-permute-done.14.three = bf16[288,128]{1,0:T(8,128)(2,1)S(1)} collective-permute-done((bf16[288,128]{1,0:T(8,128)(2,1)S(1)}, bf16[288,128]{1,0:T(8,128)(2,1)S(1)}, u32[]{:S(2)}, u32[]{:S(2)}) %collective-permute-start.14) | collective-permute-done | bytes 73760 | tf_op jit(solution)/shard_map/ppermute | solution.py:493
  39.1 2.3 %collective-permute-start.16 = (bf16[192,128]{1,0:T(8,128)(2,1)S(1)}, bf16[192,128]{1,0:T(8,128)(2,1)S(1)}, u32[]{:S(2)}, u32[]{:S(2)}) collective-permute-start(bf16[192,128]{1,0:T(8,128)(2,1)S(1)} %get-tuple-element.106), channel_id=1, source_target_pairs={{0,16},{1,17},{2,18},{3,19},{4,20},{5,21},{6,22},{7,23},{8,24},{9,... | collective-permute-start | bytes 147464 | tf_op jit(solution)/shard_map/ppermute | solution.py:493
  41.4 2.0 %collective-permute-start.17 = (bf16[192,128]{1,0:T(8,128)(2,1)S(1)}, bf16[192,128]{1,0:T(8,128)(2,1)S(1)}, u32[]{:S(2)}, u32[]{:S(2)}) collective-permute-start(bf16[192,128]{1,0:T(8,128)(2,1)S(1)} %get-tuple-element.107), channel_id=1, source_target_pairs={{0,24},{1,25},{2,26},{3,27},{4,28},{5,29},{6,30},{7,31},{8,16},{9,... | collective-permute-start | bytes 147464 | tf_op jit(solution)/shard_map/ppermute | solution.py:493
  43.5 1.0 %collective-permute-done.16.two = bf16[192,128]{1,0:T(8,128)(2,1)S(1)} collective-permute-done((bf16[192,128]{1,0:T(8,128)(2,1)S(1)}, bf16[192,128]{1,0:T(8,128)(2,1)S(1)}, u32[]{:S(2)}, u32[]{:S(2)}) %collective-permute-start.16) | collective-permute-done | bytes 49184 | tf_op jit(solution)/shard_map/ppermute | solution.py:493
  44.5 2.8 %collective-permute-done.17.three = bf16[192,128]{1,0:T(8,128)(2,1)S(1)} collective-permute-done((bf16[192,128]{1,0:T(8,128)(2,1)S(1)}, bf16[192,128]{1,0:T(8,128)(2,1)S(1)}, u32[]{:S(2)}, u32[]{:S(2)}) %collective-permute-start.17) | collective-permute-done | bytes 49184 | tf_op jit(solution)/shard_map/ppermute | solution.py:493
  47.3 0.7 %finish.1 = (f32[1,256]{1,0:T(1,128)}, f32[32,256]{1,0:T(8,128)}, f32[32,256]{1,0:T(8,128)}, f32[32,128]{1,0:T(8,128)}, f32[1,128]{1,0:T(1,128)}) custom-call(bf16[160,128]{1,0:T(8,128)(2,1)S(1)} %get-tuple-element.103.small_in, f32[32,128]{1,0:T(8,128)S(1)} %get-tuple-element.104.out_in, bf16[192,128]{1,0:T(8,128)(2,1)S(1)} %collective-permute-done.15.one, ...), custom_call_target="tpu_custom_call" | custom-call | flops 1000000 | bytes 204800 | tf_op jit(solution)/shard_map/finish/pallas_call | solution.py:479
  (37 shorter events, 1.6 us)
Async XLA Ops:
  3.0 7.4 %collective-permute-start = (bf16[256,128]{1,0:T(8,128)(2,1)}, bf16[256,128]{1,0:T(8,128)(2,1)S(1)}, u32[]{:S(2)}, u32[]{:S(2)}) collective-permute-start(bf16[256,128]{1,0:T(8,128)(2,1)} %get-tuple-element.63), channel_id=1, source_target_pairs={{0,8},{1,9},{2,10},{3,11},{4,12},{5,13},{6,14},{7,15},{8,0},{9,1},... | collective-permute-start | bytes 196616 | tf_op jit(solution)/shard_map/ppermute | solution.py:493
  6.0 7.5 %collective-permute-start.1 = (bf16[256,128]{1,0:T(8,128)(2,1)}, bf16[256,128]{1,0:T(8,128)(2,1)S(1)}, u32[]{:S(2)}, u32[]{:S(2)}) collective-permute-start(bf16[256,128]{1,0:T(8,128)(2,1)} %get-tuple-element.64), channel_id=1, source_target_pairs={{0,16},{1,17},{2,18},{3,19},{4,20},{5,21},{6,22},{7,23},{8,24},{9,... | collective-permute-start | bytes 196616 | tf_op jit(solution)/shard_map/ppermute | solution.py:493
  8.6 6.3 %collective-permute-start.2 = (bf16[256,128]{1,0:T(8,128)(2,1)}, bf16[256,128]{1,0:T(8,128)(2,1)S(1)}, u32[]{:S(2)}, u32[]{:S(2)}) collective-permute-start(bf16[256,128]{1,0:T(8,128)(2,1)} %get-tuple-element.65), channel_id=1, source_target_pairs={{0,24},{1,25},{2,26},{3,27},{4,28},{5,29},{6,30},{7,31},{8,16},{9,... | collective-permute-start | bytes 196616 | tf_op jit(solution)/shard_map/ppermute | solution.py:493
  8.6 0.9 %copy-start.4 = (bf16[256,256]{1,0:T(8,128)(2,1)S(1)}, bf16[256,256]{1,0:T(8,128)(2,1)}, u32[]{:S(2)}) copy-start(bf16[256,256]{1,0:T(8,128)(2,1)} %get-tuple-element.61.refs_1_) | copy-start | bytes 393220
  9.5 0.8 %copy-start.5 = (bf16[256,128]{1,0:T(8,128)(2,1)S(1)}, bf16[256,128]{1,0:T(8,128)(2,1)}, u32[]{:S(2)}) copy-start(bf16[256,128]{1,0:T(8,128)(2,1)} %get-tuple-element.60.refs_0_) | copy-start | bytes 196612
  10.4 18.8 %copy-start.8 = (bf16[64,512]{1,0:T(8,128)(2,1)S(1)}, bf16[64,512]{1,0:T(8,128)(2,1)}, u32[]{:S(2)}) copy-start(bf16[64,512]{1,0:T(8,128)(2,1)} %get-tuple-element.88.diag_ref) | copy-start | bytes 196612
  15.0 8.3 %collective-permute-start.3 = (bf16[640,128]{1,0:T(8,128)(2,1)S(1)}, bf16[640,128]{1,0:T(8,128)(2,1)S(1)}, u32[]{:S(2)}, u32[]{:S(2)}) collective-permute-start(bf16[640,128]{1,0:T(8,128)(2,1)S(1)} %get-tuple-element.84), channel_id=1, source_target_pairs={{0,2},{1,3},{2,0},{3,1},{4,6},{5,7},{6,4},{7,5},{8,10},{9,11},{10,... | collective-permute-start | bytes 491528 | tf_op jit(solution)/shard_map/ppermute | solution.py:493
  16.6 8.2 %collective-permute-start.4 = (bf16[640,128]{1,0:T(8,128)(2,1)S(1)}, bf16[640,128]{1,0:T(8,128)(2,1)S(1)}, u32[]{:S(2)}, u32[]{:S(2)}) collective-permute-start(bf16[640,128]{1,0:T(8,128)(2,1)S(1)} %get-tuple-element.85), channel_id=1, source_target_pairs={{0,4},{1,5},{2,6},{3,7},{4,0},{5,1},{6,2},{7,3},{8,12},{9,13},{10,... | collective-permute-start | bytes 491528 | tf_op jit(solution)/shard_map/ppermute | solution.py:493
  18.1 6.7 %collective-permute-start.5 = (bf16[640,128]{1,0:T(8,128)(2,1)S(1)}, bf16[640,128]{1,0:T(8,128)(2,1)S(1)}, u32[]{:S(2)}, u32[]{:S(2)}) collective-permute-start(bf16[640,128]{1,0:T(8,128)(2,1)S(1)} %get-tuple-element.86), channel_id=1, source_target_pairs={{0,6},{1,7},{2,4},{3,5},{4,2},{5,3},{6,0},{7,1},{8,14},{9,15},{10,... | collective-permute-start | bytes 491528 | tf_op jit(solution)/shard_map/ppermute | solution.py:493
  18.6 0.9 %copy-start = (bf16[4,128,128]{2,1,0:T(8,128)(2,1)S(1)}, bf16[4,128,128]{2,1,0:T(8,128)(2,1)}, u32[]{:S(2)}) copy-start(bf16[4,128,128]{2,1,0:T(8,128)(2,1)} %cot_ref.1) | copy-start | bytes 393220
  19.5 0.9 %copy-start.1 = (bf16[1024,128]{1,0:T(8,128)(2,1)S(1)}, bf16[1024,128]{1,0:T(8,128)(2,1)}, u32[]{:S(2)}) copy-start(bf16[1024,128]{1,0:T(8,128)(2,1)} %out_w_ref.1) | copy-start | bytes 786436
  20.4 0.9 %copy-start.2 = (f32[256,256]{1,0:T(8,128)S(1)}, f32[256,256]{1,0:T(8,128)}, u32[]{:S(2)}) copy-start(f32[256,256]{1,0:T(8,128)} %get-tuple-element.67.scaled_in) | copy-start | bytes 786436
  21.4 0.7 %copy-start.6 = (bf16[256,32]{0,1:T(8,128)(2,1)S(1)}, bf16[256,32]{0,1:T(8,128)(2,1)}, u32[]{:S(2)}) copy-start(bf16[256,32]{0,1:T(8,128)(2,1)} %param.9) | copy-start | bytes 49156
  22.1 0.7 %copy-start.7 = (bf16[256,32]{0,1:T(8,128)(2,1)S(1)}, bf16[256,32]{0,1:T(8,128)(2,1)}, u32[]{:S(2)}) copy-start(bf16[256,32]{0,1:T(8,128)(2,1)} %param.10) | copy-start | bytes 49156
  23.2 2.1 %collective-permute-start.6 = (bf16[640,128]{1,0:T(8,128)(2,1)S(1)}, bf16[640,128]{1,0:T(8,128)(2,1)S(1)}, u32[]{:S(2)}, u32[]{:S(2)}) collective-permute-start(bf16[640,128]{1,0:T(8,128)(2,1)S(1)} %get-tuple-element.83.refs_0_), channel_id=1, source_target_pairs={{0,1},{1,0},{2,3},{3,2},{4,5},{5,4},{6,7},{7,6},{8,9},{9,8},{10,11... | collective-permute-start | bytes 491528 | tf_op jit(solution)/shard_map/ppermute | solution.py:493
  23.3 2.0 %collective-permute-start.7 = (bf16[640,128]{1,0:T(8,128)(2,1)S(1)}, bf16[640,128]{1,0:T(8,128)(2,1)S(1)}, u32[]{:S(2)}, u32[]{:S(2)}) collective-permute-start(bf16[640,128]{1,0:T(8,128)(2,1)S(1)} %collective-permute-done.3.refs_1_), channel_id=1, source_target_pairs={{0,1},{1,0},{2,3},{3,2},{4,5},{5,4},{6,7},{7,6},{8,9},{9,8},{10,11... | collective-permute-start | bytes 491528 | tf_op jit(solution)/shard_map/ppermute | solution.py:493
  24.8 1.4 %collective-permute-start.8 = (bf16[640,128]{1,0:T(8,128)(2,1)S(1)}, bf16[640,128]{1,0:T(8,128)(2,1)S(1)}, u32[]{:S(2)}, u32[]{:S(2)}) collective-permute-start(bf16[640,128]{1,0:T(8,128)(2,1)S(1)} %collective-permute-done.4.refs_2_), channel_id=1, source_target_pairs={{0,1},{1,0},{2,3},{3,2},{4,5},{5,4},{6,7},{7,6},{8,9},{9,8},{10,11... | collective-permute-start | bytes 491528 | tf_op jit(solution)/shard_map/ppermute | solution.py:493
  24.8 1.6 %collective-permute-start.9 = (bf16[640,128]{1,0:T(8,128)(2,1)S(1)}, bf16[640,128]{1,0:T(8,128)(2,1)S(1)}, u32[]{:S(2)}, u32[]{:S(2)}) collective-permute-start(bf16[640,128]{1,0:T(8,128)(2,1)S(1)} %collective-permute-done.5.refs_3_), channel_id=1, source_target_pairs={{0,1},{1,0},{2,3},{3,2},{4,5},{5,4},{6,7},{7,6},{8,9},{9,8},{10,11... | collective-permute-start | bytes 491528 | tf_op jit(solution)/shard_map/ppermute | solution.py:493
  29.1 6.1 %copy-start.3 = (f32[256,128]{1,0:T(8,128)S(1)}, f32[256,128]{1,0:T(8,128)}, u32[]{:S(2)}) copy-start(f32[256,128]{1,0:T(8,128)} %get-tuple-element.93.recip_ref) | copy-start | bytes 393220
  29.1 6.1 %copy-start.9 = (f32[256]{0:T(256)S(1)}, f32[256]{0:T(256)}, u32[]{:S(2)}) copy-start(f32[256]{0:T(256)} %param.8) | copy-start | bytes 3076
  29.1 6.1 %copy-start.10 = (f32[128]{0:T(128)S(1)}, f32[128]{0:T(128)}, u32[]{:S(2)}) copy-start(f32[128]{0:T(128)} %param.12) | copy-start | bytes 1540
  30.0 1.6 %collective-permute-start.11 = (bf16[512,128]{1,0:T(8,128)(2,1)S(1)}, bf16[512,128]{1,0:T(8,128)(2,1)S(1)}, u32[]{:S(2)}, u32[]{:S(2)}) collective-permute-start(bf16[512,128]{1,0:T(8,128)(2,1)S(1)} %slice.7), channel_id=1, source_target_pairs={{0,1},{1,0},{2,3},{3,2},{4,5},{5,4},{6,7},{7,6},{8,9},{9,8},{10,11... | collective-permute-start | bytes 393224 | tf_op jit(solution)/shard_map/ppermute | solution.py:493
  30.3 1.3 %collective-permute-start.10 = (f32[160,128]{1,0:T(8,128)S(1)}, f32[160,128]{1,0:T(8,128)S(1)}, u32[]{:S(2)}, u32[]{:S(2)}) collective-permute-start(f32[160,128]{1,0:T(8,128)S(1)} %get-tuple-element.87.small_in), channel_id=1, source_target_pairs={{0,1},{1,0},{2,3},{3,2},{4,5},{5,4},{6,7},{7,6},{8,9},{9,8},{10,11... | collective-permute-start | bytes 245768 | tf_op jit(solution)/shard_map/ppermute | solution.py:493
  31.6 5.5 %collective-permute-start.12 = (bf16[288,128]{1,0:T(8,128)(2,1)S(1)}, bf16[288,128]{1,0:T(8,128)(2,1)S(1)}, u32[]{:S(2)}, u32[]{:S(2)}) collective-permute-start(bf16[288,128]{1,0:T(8,128)(2,1)S(1)} %get-tuple-element.100), channel_id=1, source_target_pairs={{0,2},{1,3},{2,0},{3,1},{4,6},{5,7},{6,4},{7,5},{8,10},{9,11},{10,... | collective-permute-start | bytes 221192 | tf_op jit(solution)/shard_map/ppermute | solution.py:493
  32.2 4.9 %collective-permute-start.13 = (bf16[288,128]{1,0:T(8,128)(2,1)S(1)}, bf16[288,128]{1,0:T(8,128)(2,1)S(1)}, u32[]{:S(2)}, u32[]{:S(2)}) collective-permute-start(bf16[288,128]{1,0:T(8,128)(2,1)S(1)} %get-tuple-element.101), channel_id=1, source_target_pairs={{0,4},{1,5},{2,6},{3,7},{4,0},{5,1},{6,2},{7,3},{8,12},{9,13},{10,... | collective-permute-start | bytes 221192 | tf_op jit(solution)/shard_map/ppermute | solution.py:493
  33.7 5.3 %collective-permute-start.14 = (bf16[288,128]{1,0:T(8,128)(2,1)S(1)}, bf16[288,128]{1,0:T(8,128)(2,1)S(1)}, u32[]{:S(2)}, u32[]{:S(2)}) collective-permute-start(bf16[288,128]{1,0:T(8,128)(2,1)S(1)} %get-tuple-element.102), channel_id=1, source_target_pairs={{0,6},{1,7},{2,4},{3,5},{4,2},{5,3},{6,0},{7,1},{8,14},{9,15},{10,... | collective-permute-start | bytes 221192 | tf_op jit(solution)/shard_map/ppermute | solution.py:493
  39.0 4.5 %collective-permute-start.15 = (bf16[192,128]{1,0:T(8,128)(2,1)S(1)}, bf16[192,128]{1,0:T(8,128)(2,1)S(1)}, u32[]{:S(2)}, u32[]{:S(2)}) collective-permute-start(bf16[192,128]{1,0:T(8,128)(2,1)S(1)} %get-tuple-element.105), channel_id=1, source_target_pairs={{0,8},{1,9},{2,10},{3,11},{4,12},{5,13},{6,14},{7,15},{8,0},{9,1},... | collective-permute-start | bytes 147464 | tf_op jit(solution)/shard_map/ppermute | solution.py:493
  39.1 5.4 %collective-permute-start.16 = (bf16[192,128]{1,0:T(8,128)(2,1)S(1)}, bf16[192,128]{1,0:T(8,128)(2,1)S(1)}, u32[]{:S(2)}, u32[]{:S(2)}) collective-permute-start(bf16[192,128]{1,0:T(8,128)(2,1)S(1)} %get-tuple-element.106), channel_id=1, source_target_pairs={{0,16},{1,17},{2,18},{3,19},{4,20},{5,21},{6,22},{7,23},{8,24},{9,... | collective-permute-start | bytes 147464 | tf_op jit(solution)/shard_map/ppermute | solution.py:493
  41.4 5.9 %collective-permute-start.17 = (bf16[192,128]{1,0:T(8,128)(2,1)S(1)}, bf16[192,128]{1,0:T(8,128)(2,1)S(1)}, u32[]{:S(2)}, u32[]{:S(2)}) collective-permute-start(bf16[192,128]{1,0:T(8,128)(2,1)S(1)} %get-tuple-element.107), channel_id=1, source_target_pairs={{0,24},{1,25},{2,26},{3,27},{4,28},{5,29},{6,30},{7,31},{8,16},{9,... | collective-permute-start | bytes 147464 | tf_op jit(solution)/shard_map/ppermute | solution.py:493

commit v4 on v3

--- a/solution.py
+++ b/solution.py
@@ -192,9 +192,15 @@
     return copies
 
 
+def normalise(x):
+    centred = x - jnp.mean(x, axis=-1, keepdims=True)
+    recip = lax.rsqrt(jnp.mean(centred * centred, axis=-1, keepdims=True) + ln_epsilon)
+    return centred * recip, recip
+
+
 def factor_kernel(
     x_hbm, gain_hbm, w1_hbm, w2_hbm, cot_hbm,
-    send0_ref, send1_ref, send2_ref, send3_ref, scaled_ref, normed_ref, recip_ref, diag_ref,
+    send0_ref, send1_ref, send2_ref, send3_ref,
     x_ref, gain_ref, w1_ref, w2_ref, cot_ref, rows, twin, cots, moved, sems,
 ):
     copies = fetch(
@@ -213,26 +219,14 @@
     both = jnp.concatenate([w1_ref[...], w2_ref[...]], axis=0)
     low = lax.broadcasted_iota(jnp.int32, (hidden, 2 * seqs), 1) < seqs
     for r in range(res):
-        x = rows[:, r, :]
-        centred = x - jnp.mean(x, axis=-1, keepdims=True)
-        recip = lax.rsqrt(jnp.mean(centred * centred, axis=-1, keepdims=True) + ln_epsilon)
-        scaled = centred * recip
-        at = slice(r * seqs, (r + 1) * seqs)
-        scaled_ref[at, :] = scaled
-        recip_ref[at, :] = jnp.broadcast_to(recip, (seqs, recip_ref.shape[1]))
+        scaled, _ = normalise(rows[:, r, :])
         normed = (scaled * gain_ref[...]).astype(bf16)
-        normed_ref[at, :] = normed
         twin[r] = mm_t(both, jnp.concatenate([normed, normed], axis=0))
         even = twin[r, pl.ds(0, hidden, stride=2), :]
         odd = twin[r, pl.ds(1, hidden, stride=2), :]
         piece = jnp.where(low, even, odd).astype(bf16)
         for send_ref in sends:
             send_ref[r * hidden : (r + 1) * hidden, :] = piece
-        left = twin[r, :hidden, :]
-        zero = jnp.zeros_like(left)
-        lanes = slice(r * 2 * seqs, (r + 1) * 2 * seqs)
-        diag_ref[:hidden, lanes] = jnp.where(low, left, zero).astype(bf16)
-        diag_ref[hidden:, lanes] = jnp.where(low, zero, left).astype(bf16)
     for r in range(res):
         cots[r * columns : (r + 1) * columns, :] = cot_ref[r].astype(f32)
     for r in range(res):
@@ -249,9 +243,33 @@
         sends[n // plane][to : to + per, :] = block.astype(bf16)
 
 
-def own_kernel(*refs):
+def copy_kernel(*refs):
     for a, b in zip(refs[: len(refs) // 2], refs[len(refs) // 2 :]):
         b[...] = a[...]
+
+
+def own_kernel(
+    send_in, x_ref, gain_ref, w1_ref,
+    send_ref, scaled_ref, normed_ref, recip_ref, diag_ref,
+    rows,
+):
+    send_ref[...] = send_in[...]
+    seqs, res, _ = x_ref.shape
+    hidden = w1_ref.shape[0]
+    rows[...] = x_ref[...].astype(f32)
+    low = lax.broadcasted_iota(jnp.int32, (hidden, 2 * seqs), 1) < seqs
+    for r in range(res):
+        scaled, recip = normalise(rows[:, r, :])
+        at = slice(r * seqs, (r + 1) * seqs)
+        scaled_ref[at, :] = scaled
+        recip_ref[at, :] = jnp.broadcast_to(recip, (seqs, recip_ref.shape[1]))
+        normed = (scaled * gain_ref[...]).astype(bf16)
+        normed_ref[at, :] = normed
+        left = mm_t(w1_ref[...], jnp.concatenate([normed, normed], axis=0))
+        zero = jnp.zeros_like(left)
+        lanes = slice(r * 2 * seqs, (r + 1) * 2 * seqs)
+        diag_ref[:hidden, lanes] = jnp.where(low, left, zero).astype(bf16)
+        diag_ref[hidden:, lanes] = jnp.where(low, zero, left).astype(bf16)
 
 
 def pack_kernel(height, *refs):
@@ -266,13 +284,13 @@
 
 
 def prepare_kernel(
-    out_w_ref, cot_ref, scaled_in, w1_in, w2_in,
-    cot_t_ref, twin_left_ref, twin_right_ref, bias_ref, scaled_ref, w1_ref, w2_ref,
+    out_w_ref, cot_ref, w1_in, w2_in,
+    cot_t_ref, twin_left_ref, twin_right_ref, bias_ref, w1_ref, w2_ref,
     wide,
 ):
     hidden = twin_left_ref.shape[0] // 2
     res, columns, pairs = cot_ref.shape
-    own_kernel(scaled_in, w1_in, w2_in, scaled_ref, w1_ref, w2_ref)
+    copy_kernel(w1_in, w2_in, w1_ref, w2_ref)
     wide[...] = out_w_ref[...].astype(f32)
     for d in range(hidden):
         at = (d % 2) * hidden
@@ -517,16 +535,12 @@
 
     zs, yxs = 4, 4
     height = res * hidden
-    *sends, scaled, normed, recip, diag = call(
+    sends = call(
         factor_kernel,
         "factors",
         (homolog_features, gain, w1, w2, pair_cotangent),
         [
             *[((height + res * columns // zs, lanes), bf16)] * zs,
-            ((own, channels), f32),
-            ((own, channels), bf16),
-            ((own, 128), f32),
-            ((2 * hidden, res * lanes), bf16),
         ],
         [
             ((seqs, res, channels), bf16),
@@ -544,12 +558,18 @@
         vmem=60,
     )
     swapped = {z: swap(sends[z], z * 2 * yxs) for z in (3, 2, 1)}
-    own_send, normed = call(
+    own_send, scaled, normed, recip, diag = call(
         own_kernel,
         "own",
-        (sends[0], normed),
-        [(sends[0].shape, bf16), (normed.shape, bf16)],
-        [],
+        (sends[0], homolog_features, gain, w1),
+        [
+            (sends[0].shape, bf16),
+            ((own, channels), f32),
+            ((own, channels), bf16),
+            ((own, 128), f32),
+            ((2 * hidden, res * lanes), bf16),
+        ],
+        [((seqs, res, channels), f32)],
         10**6,
     )
     sent = call(
@@ -564,13 +584,12 @@
     prepared = call(
         prepare_kernel,
         "prepare",
-        (output_projection_matrix, pair_cotangent, scaled, w1, w2),
+        (output_projection_matrix, pair_cotangent, w1, w2),
         [
             ((res * pairs, columns), bf16),
             (wide, bf16),
             (wide, bf16),
             ((8, pairs), f32),
-            (scaled.shape, f32),
             (w1.shape, bf16),
             (w2.shape, bf16),
         ],
@@ -578,7 +597,7 @@
         10**6,
     )
     mine[0], prepared = lax.optimization_barrier((mine[0], prepared))
-    cot_t, twin_left, twin_right, bias_part, scaled, w1, w2 = prepared
+    cot_t, twin_left, twin_right, bias_part, w1, w2 = prepared
     other = [swap(m, 1) for m in mine]
     small, rights, spread, normed_grad = call(
         functools.partial(sums_kernel, yxs),

time: 48.4 us -> 47.8 us (0.988)
  waiting for transfers between devices: 13.4 us -> 12 us
    ppermute x18, waiting for transfers between devices: 13.4 us -> 12 us  [swap(): return lax.ppermute(value, 'row', [(i, i ^ step) for i in range(count)])]
    unnamed x22 -> x20, local copies, waits for them, and re-layouts: 6 us -> 6.44 us
  transfers between devices with their start and end apart: 18 -> 18, of which waited for: 9 -> 9; matrix products, arithmetic and copies ran while one was open for 0% -> 0% of each run, Pallas kernels for 5% -> 6%
where the time goes in v4:
time: 47.8 us; the launch traced here: 47.4 us
  starting transfers between devices  18.9 us (40%)
  waiting for transfers between devices  12 us (25%)
  Pallas kernels  9.25 us (19%)
  local copies, waits for them, and re-layouts  6.45 us (13%)
  between operations  0.75 us (2%)
    ppermute x18, starting transfers between devices, swap(): return lax.ppermute(value, 'row', [(i, i ^ step) for i in range(count)])  18.9 us
    ppermute x18, waiting for transfers between devices, swap(): return lax.ppermute(value, 'row', [(i, i ^ step) for i in range(count)])  12 us
    pallas_call x10, Pallas kernels, call(): pl.pallas_call(kernel, out_shape=[jax.ShapeDtypeStruct(s, d) for s, d in...  9.25 us
    unnamed x20, local copies, waits for them, and re-layouts  6.44 us
  transfers between devices with their start and end apart: 18, of which 9 were waited for; matrix products, arithmetic and copies ran while one was open for 0% of the time, Pallas kernels for 6%

profile of v4, /device:TPU:0, one launch (start us, length us, event | category | flops | bytes accessed | tf_op | source)
XLA Modules:
  0.0 47.4 jit_solution(13278661802325821716)
XLA Ops:
  0.6 2.2 %factors.1 = (bf16[256,128]{1,0:T(8,128)(2,1)}, bf16[256,128]{1,0:T(8,128)(2,1)}, bf16[256,128]{1,0:T(8,128)(2,1)}, bf16[256,128]{1,0:T(8,128)(2,1)}) custom-call(bf16[64,4,256]{2,1,0:T(4,128)(2,1)} %x_ref.1, f32[1,256]{1,0:T(1,128)} %bitcast.13, bf16[32,256]{1,0:T(8,128)(2,1)} %bitcast.8, bf16[32,256]{1,0:T(8,128)(2,1)} %bitcast.11, ...), custom_call_target="tpu_custom_call" | custom-call | flops 1000000 | bytes 295936 | tf_op jit(solution)/shard_map/factors/pallas_call | solution.py:497
  2.8 3.1 %collective-permute-start = (bf16[256,128]{1,0:T(8,128)(2,1)}, bf16[256,128]{1,0:T(8,128)(2,1)S(1)}, u32[]{:S(2)}, u32[]{:S(2)}) collective-permute-start(bf16[256,128]{1,0:T(8,128)(2,1)} %get-tuple-element.59), channel_id=1, source_target_pairs={{0,8},{1,9},{2,10},{3,11},{4,12},{5,13},{6,14},{7,15},{8,0},{9,1},... | collective-permute-start | bytes 196616 | tf_op jit(solution)/shard_map/ppermute | solution.py:511
  5.9 2.6 %collective-permute-start.1 = (bf16[256,128]{1,0:T(8,128)(2,1)}, bf16[256,128]{1,0:T(8,128)(2,1)S(1)}, u32[]{:S(2)}, u32[]{:S(2)}) collective-permute-start(bf16[256,128]{1,0:T(8,128)(2,1)} %get-tuple-element.60), channel_id=1, source_target_pairs={{0,16},{1,17},{2,18},{3,19},{4,20},{5,21},{6,22},{7,23},{8,24},{9,... | collective-permute-start | bytes 196616 | tf_op jit(solution)/shard_map/ppermute | solution.py:511
  8.5 0.9 %copy-done = bf16[64,4,256]{2,1,0:T(4,128)(2,1)S(1)} copy-done((bf16[64,4,256]{2,1,0:T(4,128)(2,1)S(1)}, bf16[64,4,256]{2,1,0:T(4,128)(2,1)}, u32[]{:S(2)}) %copy-start) | copy-done | bytes 131096
  9.4 0.7 %copy-done.3 = bf16[256,32]{0,1:T(8,128)(2,1)S(1)} copy-done((bf16[256,32]{0,1:T(8,128)(2,1)S(1)}, bf16[256,32]{0,1:T(8,128)(2,1)}, u32[]{:S(2)}) %copy-start.3) | copy-done | bytes 16408
  10.1 0.8 %copy-done.5 = bf16[256,128]{1,0:T(8,128)(2,1)S(1)} copy-done((bf16[256,128]{1,0:T(8,128)(2,1)S(1)}, bf16[256,128]{1,0:T(8,128)(2,1)}, u32[]{:S(2)}) %copy-start.5) | copy-done | bytes 65560
  11.0 0.7 %copy-done.7 = f32[256]{0:T(256)S(1)} copy-done((f32[256]{0:T(256)S(1)}, f32[256]{0:T(256)}, u32[]{:S(2)}) %copy-start.7) | copy-done | bytes 1048
  12.1 1.3 %collective-permute-done.1.refs_2_ = bf16[256,128]{1,0:T(8,128)(2,1)S(1)} collective-permute-done((bf16[256,128]{1,0:T(8,128)(2,1)}, bf16[256,128]{1,0:T(8,128)(2,1)S(1)}, u32[]{:S(2)}, u32[]{:S(2)}) %collective-permute-start.1) | collective-permute-done | bytes 65568 | tf_op jit(solution)/shard_map/ppermute | solution.py:511
  13.4 1.4 %collective-permute-done.2.refs_3_ = bf16[256,128]{1,0:T(8,128)(2,1)S(1)} collective-permute-done((bf16[256,128]{1,0:T(8,128)(2,1)}, bf16[256,128]{1,0:T(8,128)(2,1)S(1)}, u32[]{:S(2)}, u32[]{:S(2)}) %collective-permute-start.2) | collective-permute-done | bytes 65568 | tf_op jit(solution)/shard_map/ppermute | solution.py:511
  14.9 1.6 %collective-permute-start.3 = (bf16[640,128]{1,0:T(8,128)(2,1)S(1)}, bf16[640,128]{1,0:T(8,128)(2,1)S(1)}, u32[]{:S(2)}, u32[]{:S(2)}) collective-permute-start(bf16[640,128]{1,0:T(8,128)(2,1)S(1)} %get-tuple-element.78), channel_id=1, source_target_pairs={{0,2},{1,3},{2,0},{3,1},{4,6},{5,7},{6,4},{7,5},{8,10},{9,11},{10,... | collective-permute-start | bytes 491528 | tf_op jit(solution)/shard_map/ppermute | solution.py:511
  16.4 1.5 %collective-permute-start.4 = (bf16[640,128]{1,0:T(8,128)(2,1)S(1)}, bf16[640,128]{1,0:T(8,128)(2,1)S(1)}, u32[]{:S(2)}, u32[]{:S(2)}) collective-permute-start(bf16[640,128]{1,0:T(8,128)(2,1)S(1)} %get-tuple-element.79), channel_id=1, source_target_pairs={{0,4},{1,5},{2,6},{3,7},{4,0},{5,1},{6,2},{7,3},{8,12},{9,13},{10,... | collective-permute-start | bytes 491528 | tf_op jit(solution)/shard_map/ppermute | solution.py:511
  18.4 0.9 %copy-done.1 = bf16[4,128,128]{2,1,0:T(8,128)(2,1)S(1)} copy-done((bf16[4,128,128]{2,1,0:T(8,128)(2,1)S(1)}, bf16[4,128,128]{2,1,0:T(8,128)(2,1)}, u32[]{:S(2)}) %copy-start.1) | copy-done | bytes 131096
  19.3 0.9 %copy-done.2 = bf16[1024,128]{1,0:T(8,128)(2,1)S(1)} copy-done((bf16[1024,128]{1,0:T(8,128)(2,1)S(1)}, bf16[1024,128]{1,0:T(8,128)(2,1)}, u32[]{:S(2)}) %copy-start.2) | copy-done | bytes 262168
  20.3 0.7 %copy-done.4 = bf16[256,32]{0,1:T(8,128)(2,1)S(1)} copy-done((bf16[256,32]{0,1:T(8,128)(2,1)S(1)}, bf16[256,32]{0,1:T(8,128)(2,1)}, u32[]{:S(2)}) %copy-start.4) | copy-done | bytes 16408
  21.0 0.7 %copy-done.6 = bf16[256,32]{0,1:T(8,128)(2,1)S(1)} copy-done((bf16[256,32]{0,1:T(8,128)(2,1)S(1)}, bf16[256,32]{0,1:T(8,128)(2,1)}, u32[]{:S(2)}) %copy-start.6) | copy-done | bytes 16408
  22.2 0.5 %collective-permute-start.7 = (bf16[640,128]{1,0:T(8,128)(2,1)S(1)}, bf16[640,128]{1,0:T(8,128)(2,1)S(1)}, u32[]{:S(2)}, u32[]{:S(2)}) collective-permute-start(bf16[640,128]{1,0:T(8,128)(2,1)S(1)} %collective-permute-done.3.refs_1_), channel_id=1, source_target_pairs={{0,1},{1,0},{2,3},{3,2},{4,5},{5,4},{6,7},{7,6},{8,9},{9,8},{10,11... | collective-permute-start | bytes 491528 | tf_op jit(solution)/shard_map/ppermute | solution.py:511
  22.7 2.0 %collective-permute-done.4.refs_2_ = bf16[640,128]{1,0:T(8,128)(2,1)S(1)} collective-permute-done((bf16[640,128]{1,0:T(8,128)(2,1)S(1)}, bf16[640,128]{1,0:T(8,128)(2,1)S(1)}, u32[]{:S(2)}, u32[]{:S(2)}) %collective-permute-start.4) | collective-permute-done | bytes 163872 | tf_op jit(solution)/shard_map/ppermute | solution.py:511
  24.7 0.5 %collective-permute-start.9 = (bf16[640,128]{1,0:T(8,128)(2,1)S(1)}, bf16[640,128]{1,0:T(8,128)(2,1)S(1)}, u32[]{:S(2)}, u32[]{:S(2)}) collective-permute-start(bf16[640,128]{1,0:T(8,128)(2,1)S(1)} %collective-permute-done.5.refs_3_), channel_id=1, source_target_pairs={{0,1},{1,0},{2,3},{3,2},{4,5},{5,4},{6,7},{7,6},{8,9},{9,8},{10,11... | collective-permute-start | bytes 491528 | tf_op jit(solution)/shard_map/ppermute | solution.py:511
  25.2 0.9 %collective-permute-done.8.refs_6_ = bf16[640,128]{1,0:T(8,128)(2,1)S(1)} collective-permute-done((bf16[640,128]{1,0:T(8,128)(2,1)S(1)}, bf16[640,128]{1,0:T(8,128)(2,1)S(1)}, u32[]{:S(2)}, u32[]{:S(2)}) %collective-permute-start.8) | collective-permute-done | bytes 163872 | tf_op jit(solution)/shard_map/ppermute | solution.py:511
  26.3 2.7 %sums.1 = (f32[160,128]{1,0:T(8,128)S(1)}, bf16[128,2048]{1,0:T(8,128)(2,1)S(1)}, bf16[2048,512]{1,0:T(8,128)(2,1)S(1)}, f32[256,256]{1,0:T(8,128)S(1)}) custom-call(bf16[512,128]{1,0:T(8,128)(2,1)S(1)} %get-tuple-element.69.cot_t_ref, bf16[64,2048]{1,0:T(8,128)(2,1)S(1)} %get-tuple-element.70.twin_left_ref, ...), custom_call_target="tpu_custom_call" | custom-call | flops 1000000 | bytes 2396160 | tf_op jit(solution)/shard_map/sums/pallas_call | solution.py:497
  29.0 0.8 %shares.1.out_in = f32[1024,128]{1,0:T(8,128)S(1)} custom-call(bf16[64,512]{1,0:T(8,128)(2,1)S(1)} %get-tuple-element.82.diag_ref, bf16[2048,512]{1,0:T(8,128)(2,1)S(1)} %get-tuple-element.83.spread_ref), custom_call_target="tpu_custom_call" | custom-call | flops 1000000 | bytes 2162688 | tf_op jit(solution)/shard_map/shares/pallas_call | solution.py:497
  30.4 1.1 %collective-permute-done.10.small_came = f32[160,128]{1,0:T(8,128)S(1)} collective-permute-done((f32[160,128]{1,0:T(8,128)S(1)}, f32[160,128]{1,0:T(8,128)S(1)}, u32[]{:S(2)}, u32[]{:S(2)}) %collective-permute-start.10) | collective-permute-done | bytes 81952 | tf_op jit(solution)/shard_map/ppermute | solution.py:511
  31.8 1.1 %collective-permute-start.13 = (bf16[288,128]{1,0:T(8,128)(2,1)S(1)}, bf16[288,128]{1,0:T(8,128)(2,1)S(1)}, u32[]{:S(2)}, u32[]{:S(2)}) collective-permute-start(bf16[288,128]{1,0:T(8,128)(2,1)S(1)} %get-tuple-element.95), channel_id=1, source_target_pairs={{0,4},{1,5},{2,6},{3,7},{4,0},{5,1},{6,2},{7,3},{8,12},{9,13},{10,... | collective-permute-start | bytes 221192 | tf_op jit(solution)/shard_map/ppermute | solution.py:511
  32.9 2.1 %collective-permute-start.14 = (bf16[288,128]{1,0:T(8,128)(2,1)S(1)}, bf16[288,128]{1,0:T(8,128)(2,1)S(1)}, u32[]{:S(2)}, u32[]{:S(2)}) collective-permute-start(bf16[288,128]{1,0:T(8,128)(2,1)S(1)} %get-tuple-element.96), channel_id=1, source_target_pairs={{0,6},{1,7},{2,4},{3,5},{4,2},{5,3},{6,0},{7,1},{8,14},{9,15},{10,... | collective-permute-start | bytes 221192 | tf_op jit(solution)/shard_map/ppermute | solution.py:511
  35.1 1.9 %results.1 = (bf16[4,128,128]{2,1,0:T(8,128)(2,1)}, bf16[64,4,256]{2,1,0:T(4,128)(2,1)}) custom-call(bf16[128,2048]{1,0:T(8,128)(2,1)S(1)} %get-tuple-element.85.rights_ref, bf16[64,2048]{1,0:T(8,128)(2,1)S(1)} %get-tuple-element.70.twin_left_ref, bf16[32,256]{1,0:T(8,128)(2,1)S(1)} %get-tuple-element.74.w1_ref, ...), custom_call_target="tpu_custom_call" | custom-call | flops 1000000 | bytes 1590784 | tf_op jit(solution)/shard_map/results/pallas_call | solution.py:497
  37.0 1.2 %collective-permute-done.14.three = bf16[288,128]{1,0:T(8,128)(2,1)S(1)} collective-permute-done((bf16[288,128]{1,0:T(8,128)(2,1)S(1)}, bf16[288,128]{1,0:T(8,128)(2,1)S(1)}, u32[]{:S(2)}, u32[]{:S(2)}) %collective-permute-start.14) | collective-permute-done | bytes 73760 | tf_op jit(solution)/shard_map/ppermute | solution.py:511
  38.2 0.7 %collective-permute-start.15 = (bf16[192,128]{1,0:T(8,128)(2,1)S(1)}, bf16[192,128]{1,0:T(8,128)(2,1)S(1)}, u32[]{:S(2)}, u32[]{:S(2)}) collective-permute-start(bf16[192,128]{1,0:T(8,128)(2,1)S(1)} %get-tuple-element.99), channel_id=1, source_target_pairs={{0,8},{1,9},{2,10},{3,11},{4,12},{5,13},{6,14},{7,15},{8,0},{9,1},... | collective-permute-start | bytes 147464 | tf_op jit(solution)/shard_map/ppermute | solution.py:511
  38.9 1.8 %collective-permute-start.16 = (bf16[192,128]{1,0:T(8,128)(2,1)S(1)}, bf16[192,128]{1,0:T(8,128)(2,1)S(1)}, u32[]{:S(2)}, u32[]{:S(2)}) collective-permute-start(bf16[192,128]{1,0:T(8,128)(2,1)S(1)} %get-tuple-element.100), channel_id=1, source_target_pairs={{0,16},{1,17},{2,18},{3,19},{4,20},{5,21},{6,22},{7,23},{8,24},{9,... | collective-permute-start | bytes 147464 | tf_op jit(solution)/shard_map/ppermute | solution.py:511
  40.8 1.9 %collective-permute-start.17 = (bf16[192,128]{1,0:T(8,128)(2,1)S(1)}, bf16[192,128]{1,0:T(8,128)(2,1)S(1)}, u32[]{:S(2)}, u32[]{:S(2)}) collective-permute-start(bf16[192,128]{1,0:T(8,128)(2,1)S(1)} %get-tuple-element.101), channel_id=1, source_target_pairs={{0,24},{1,25},{2,26},{3,27},{4,28},{5,29},{6,30},{7,31},{8,16},{9,... | collective-permute-start | bytes 147464 | tf_op jit(solution)/shard_map/ppermute | solution.py:511
  42.7 2.3 %collective-permute-done.16.two = bf16[192,128]{1,0:T(8,128)(2,1)S(1)} collective-permute-done((bf16[192,128]{1,0:T(8,128)(2,1)S(1)}, bf16[192,128]{1,0:T(8,128)(2,1)S(1)}, u32[]{:S(2)}, u32[]{:S(2)}) %collective-permute-start.16) | collective-permute-done | bytes 49184 | tf_op jit(solution)/shard_map/ppermute | solution.py:511
  45.0 1.7 %collective-permute-done.17.three = bf16[192,128]{1,0:T(8,128)(2,1)S(1)} collective-permute-done((bf16[192,128]{1,0:T(8,128)(2,1)S(1)}, bf16[192,128]{1,0:T(8,128)(2,1)S(1)}, u32[]{:S(2)}, u32[]{:S(2)}) %collective-permute-start.17) | collective-permute-done | bytes 49184 | tf_op jit(solution)/shard_map/ppermute | solution.py:511
  46.7 0.7 %finish.1 = (f32[1,256]{1,0:T(1,128)}, f32[32,256]{1,0:T(8,128)}, f32[32,256]{1,0:T(8,128)}, f32[32,128]{1,0:T(8,128)}, f32[1,128]{1,0:T(1,128)}) custom-call(bf16[160,128]{1,0:T(8,128)(2,1)S(1)} %get-tuple-element.97.small_in, f32[32,128]{1,0:T(8,128)S(1)} %get-tuple-element.98.out_in, bf16[192,128]{1,0:T(8,128)(2,1)S(1)} %collective-permute-done.15.one, ...), custom_call_target="tpu_custom_call" | custom-call | flops 1000000 | bytes 204800 | tf_op jit(solution)/shard_map/finish/pallas_call | solution.py:497
  (35 shorter events, 2.7 us)
Async XLA Ops:
  2.8 9.2 %collective-permute-start = (bf16[256,128]{1,0:T(8,128)(2,1)}, bf16[256,128]{1,0:T(8,128)(2,1)S(1)}, u32[]{:S(2)}, u32[]{:S(2)}) collective-permute-start(bf16[256,128]{1,0:T(8,128)(2,1)} %get-tuple-element.59), channel_id=1, source_target_pairs={{0,8},{1,9},{2,10},{3,11},{4,12},{5,13},{6,14},{7,15},{8,0},{9,1},... | collective-permute-start | bytes 196616 | tf_op jit(solution)/shard_map/ppermute | solution.py:511
  5.9 7.5 %collective-permute-start.1 = (bf16[256,128]{1,0:T(8,128)(2,1)}, bf16[256,128]{1,0:T(8,128)(2,1)S(1)}, u32[]{:S(2)}, u32[]{:S(2)}) collective-permute-start(bf16[256,128]{1,0:T(8,128)(2,1)} %get-tuple-element.60), channel_id=1, source_target_pairs={{0,16},{1,17},{2,18},{3,19},{4,20},{5,21},{6,22},{7,23},{8,24},{9,... | collective-permute-start | bytes 196616 | tf_op jit(solution)/shard_map/ppermute | solution.py:511
  8.5 6.3 %collective-permute-start.2 = (bf16[256,128]{1,0:T(8,128)(2,1)}, bf16[256,128]{1,0:T(8,128)(2,1)S(1)}, u32[]{:S(2)}, u32[]{:S(2)}) collective-permute-start(bf16[256,128]{1,0:T(8,128)(2,1)} %get-tuple-element.61), channel_id=1, source_target_pairs={{0,24},{1,25},{2,26},{3,27},{4,28},{5,29},{6,30},{7,31},{8,16},{9,... | collective-permute-start | bytes 196616 | tf_op jit(solution)/shard_map/ppermute | solution.py:511
  8.5 0.9 %copy-start = (bf16[64,4,256]{2,1,0:T(4,128)(2,1)S(1)}, bf16[64,4,256]{2,1,0:T(4,128)(2,1)}, u32[]{:S(2)}) copy-start(bf16[64,4,256]{2,1,0:T(4,128)(2,1)} %x_ref.1) | copy-start | bytes 393220
  9.4 0.7 %copy-start.3 = (bf16[256,32]{0,1:T(8,128)(2,1)S(1)}, bf16[256,32]{0,1:T(8,128)(2,1)}, u32[]{:S(2)}) copy-start(bf16[256,32]{0,1:T(8,128)(2,1)} %param.9) | copy-start | bytes 49156
  10.1 0.8 %copy-start.5 = (bf16[256,128]{1,0:T(8,128)(2,1)S(1)}, bf16[256,128]{1,0:T(8,128)(2,1)}, u32[]{:S(2)}) copy-start(bf16[256,128]{1,0:T(8,128)(2,1)} %get-tuple-element.57.send_in) | copy-start | bytes 196612
  11.0 0.7 %copy-start.7 = (f32[256]{0:T(256)S(1)}, f32[256]{0:T(256)}, u32[]{:S(2)}) copy-start(f32[256]{0:T(256)} %param.8) | copy-start | bytes 3076
  14.9 7.3 %collective-permute-start.3 = (bf16[640,128]{1,0:T(8,128)(2,1)S(1)}, bf16[640,128]{1,0:T(8,128)(2,1)S(1)}, u32[]{:S(2)}, u32[]{:S(2)}) collective-permute-start(bf16[640,128]{1,0:T(8,128)(2,1)S(1)} %get-tuple-element.78), channel_id=1, source_target_pairs={{0,2},{1,3},{2,0},{3,1},{4,6},{5,7},{6,4},{7,5},{8,10},{9,11},{10,... | collective-permute-start | bytes 491528 | tf_op jit(solution)/shard_map/ppermute | solution.py:511
  16.4 8.2 %collective-permute-start.4 = (bf16[640,128]{1,0:T(8,128)(2,1)S(1)}, bf16[640,128]{1,0:T(8,128)(2,1)S(1)}, u32[]{:S(2)}, u32[]{:S(2)}) collective-permute-start(bf16[640,128]{1,0:T(8,128)(2,1)S(1)} %get-tuple-element.79), channel_id=1, source_target_pairs={{0,4},{1,5},{2,6},{3,7},{4,0},{5,1},{6,2},{7,3},{8,12},{9,13},{10,... | collective-permute-start | bytes 491528 | tf_op jit(solution)/shard_map/ppermute | solution.py:511
  17.9 6.7 %collective-permute-start.5 = (bf16[640,128]{1,0:T(8,128)(2,1)S(1)}, bf16[640,128]{1,0:T(8,128)(2,1)S(1)}, u32[]{:S(2)}, u32[]{:S(2)}) collective-permute-start(bf16[640,128]{1,0:T(8,128)(2,1)S(1)} %get-tuple-element.80), channel_id=1, source_target_pairs={{0,6},{1,7},{2,4},{3,5},{4,2},{5,3},{6,0},{7,1},{8,14},{9,15},{10,... | collective-permute-start | bytes 491528 | tf_op jit(solution)/shard_map/ppermute | solution.py:511
  18.4 0.9 %copy-start.1 = (bf16[4,128,128]{2,1,0:T(8,128)(2,1)S(1)}, bf16[4,128,128]{2,1,0:T(8,128)(2,1)}, u32[]{:S(2)}) copy-start(bf16[4,128,128]{2,1,0:T(8,128)(2,1)} %cot_ref.1) | copy-start | bytes 393220
  19.3 0.9 %copy-start.2 = (bf16[1024,128]{1,0:T(8,128)(2,1)S(1)}, bf16[1024,128]{1,0:T(8,128)(2,1)}, u32[]{:S(2)}) copy-start(bf16[1024,128]{1,0:T(8,128)(2,1)} %out_w_ref.1) | copy-start | bytes 786436
  20.3 0.7 %copy-start.4 = (bf16[256,32]{0,1:T(8,128)(2,1)S(1)}, bf16[256,32]{0,1:T(8,128)(2,1)}, u32[]{:S(2)}) copy-start(bf16[256,32]{0,1:T(8,128)(2,1)} %param.9) | copy-start | bytes 49156
  21.0 0.7 %copy-start.6 = (bf16[256,32]{0,1:T(8,128)(2,1)S(1)}, bf16[256,32]{0,1:T(8,128)(2,1)}, u32[]{:S(2)}) copy-start(bf16[256,32]{0,1:T(8,128)(2,1)} %param.10) | copy-start | bytes 49156
  22.1 3.1 %collective-permute-start.6 = (bf16[640,128]{1,0:T(8,128)(2,1)S(1)}, bf16[640,128]{1,0:T(8,128)(2,1)S(1)}, u32[]{:S(2)}, u32[]{:S(2)}) collective-permute-start(bf16[640,128]{1,0:T(8,128)(2,1)S(1)} %get-tuple-element.77.refs_0_), channel_id=1, source_target_pairs={{0,1},{1,0},{2,3},{3,2},{4,5},{5,4},{6,7},{7,6},{8,9},{9,8},{10,11... | collective-permute-start | bytes 491528 | tf_op jit(solution)/shard_map/ppermute | solution.py:511
  22.2 3.0 %collective-permute-start.7 = (bf16[640,128]{1,0:T(8,128)(2,1)S(1)}, bf16[640,128]{1,0:T(8,128)(2,1)S(1)}, u32[]{:S(2)}, u32[]{:S(2)}) collective-permute-start(bf16[640,128]{1,0:T(8,128)(2,1)S(1)} %collective-permute-done.3.refs_1_), channel_id=1, source_target_pairs={{0,1},{1,0},{2,3},{3,2},{4,5},{5,4},{6,7},{7,6},{8,9},{9,8},{10,11... | collective-permute-start | bytes 491528 | tf_op jit(solution)/shard_map/ppermute | solution.py:511
  24.7 1.4 %collective-permute-start.8 = (bf16[640,128]{1,0:T(8,128)(2,1)S(1)}, bf16[640,128]{1,0:T(8,128)(2,1)S(1)}, u32[]{:S(2)}, u32[]{:S(2)}) collective-permute-start(bf16[640,128]{1,0:T(8,128)(2,1)S(1)} %collective-permute-done.4.refs_2_), channel_id=1, source_target_pairs={{0,1},{1,0},{2,3},{3,2},{4,5},{5,4},{6,7},{7,6},{8,9},{9,8},{10,11... | collective-permute-start | bytes 491528 | tf_op jit(solution)/shard_map/ppermute | solution.py:511
  24.7 1.6 %collective-permute-start.9 = (bf16[640,128]{1,0:T(8,128)(2,1)S(1)}, bf16[640,128]{1,0:T(8,128)(2,1)S(1)}, u32[]{:S(2)}, u32[]{:S(2)}) collective-permute-start(bf16[640,128]{1,0:T(8,128)(2,1)S(1)} %collective-permute-done.5.refs_3_), channel_id=1, source_target_pairs={{0,1},{1,0},{2,3},{3,2},{4,5},{5,4},{6,7},{7,6},{8,9},{9,8},{10,11... | collective-permute-start | bytes 491528 | tf_op jit(solution)/shard_map/ppermute | solution.py:511
  29.0 6.1 %copy-start.8 = (f32[256]{0:T(256)S(1)}, f32[256]{0:T(256)}, u32[]{:S(2)}) copy-start(f32[256]{0:T(256)} %param.8) | copy-start | bytes 3076
  29.0 6.1 %copy-start.9 = (f32[128]{0:T(128)S(1)}, f32[128]{0:T(128)}, u32[]{:S(2)}) copy-start(f32[128]{0:T(128)} %param.12) | copy-start | bytes 1540
  29.8 1.6 %collective-permute-start.11 = (bf16[512,128]{1,0:T(8,128)(2,1)S(1)}, bf16[512,128]{1,0:T(8,128)(2,1)S(1)}, u32[]{:S(2)}, u32[]{:S(2)}) collective-permute-start(bf16[512,128]{1,0:T(8,128)(2,1)S(1)} %slice.7), channel_id=1, source_target_pairs={{0,1},{1,0},{2,3},{3,2},{4,5},{5,4},{6,7},{7,6},{8,9},{9,8},{10,11... | collective-permute-start | bytes 393224 | tf_op jit(solution)/shard_map/ppermute | solution.py:511
  30.2 1.3 %collective-permute-start.10 = (f32[160,128]{1,0:T(8,128)S(1)}, f32[160,128]{1,0:T(8,128)S(1)}, u32[]{:S(2)}, u32[]{:S(2)}) collective-permute-start(f32[160,128]{1,0:T(8,128)S(1)} %get-tuple-element.81.small_in), channel_id=1, source_target_pairs={{0,1},{1,0},{2,3},{3,2},{4,5},{5,4},{6,7},{7,6},{8,9},{9,8},{10,11... | collective-permute-start | bytes 245768 | tf_op jit(solution)/shard_map/ppermute | solution.py:511
  31.5 5.5 %collective-permute-start.12 = (bf16[288,128]{1,0:T(8,128)(2,1)S(1)}, bf16[288,128]{1,0:T(8,128)(2,1)S(1)}, u32[]{:S(2)}, u32[]{:S(2)}) collective-permute-start(bf16[288,128]{1,0:T(8,128)(2,1)S(1)} %get-tuple-element.94), channel_id=1, source_target_pairs={{0,2},{1,3},{2,0},{3,1},{4,6},{5,7},{6,4},{7,5},{8,10},{9,11},{10,... | collective-permute-start | bytes 221192 | tf_op jit(solution)/shard_map/ppermute | solution.py:511
  31.8 5.2 %collective-permute-start.13 = (bf16[288,128]{1,0:T(8,128)(2,1)S(1)}, bf16[288,128]{1,0:T(8,128)(2,1)S(1)}, u32[]{:S(2)}, u32[]{:S(2)}) collective-permute-start(bf16[288,128]{1,0:T(8,128)(2,1)S(1)} %get-tuple-element.95), channel_id=1, source_target_pairs={{0,4},{1,5},{2,6},{3,7},{4,0},{5,1},{6,2},{7,3},{8,12},{9,13},{10,... | collective-permute-start | bytes 221192 | tf_op jit(solution)/shard_map/ppermute | solution.py:511
  32.9 5.3 %collective-permute-start.14 = (bf16[288,128]{1,0:T(8,128)(2,1)S(1)}, bf16[288,128]{1,0:T(8,128)(2,1)S(1)}, u32[]{:S(2)}, u32[]{:S(2)}) collective-permute-start(bf16[288,128]{1,0:T(8,128)(2,1)S(1)} %get-tuple-element.96), channel_id=1, source_target_pairs={{0,6},{1,7},{2,4},{3,5},{4,2},{5,3},{6,0},{7,1},{8,14},{9,15},{10,... | collective-permute-start | bytes 221192 | tf_op jit(solution)/shard_map/ppermute | solution.py:511
  38.2 4.5 %collective-permute-start.15 = (bf16[192,128]{1,0:T(8,128)(2,1)S(1)}, bf16[192,128]{1,0:T(8,128)(2,1)S(1)}, u32[]{:S(2)}, u32[]{:S(2)}) collective-permute-start(bf16[192,128]{1,0:T(8,128)(2,1)S(1)} %get-tuple-element.99), channel_id=1, source_target_pairs={{0,8},{1,9},{2,10},{3,11},{4,12},{5,13},{6,14},{7,15},{8,0},{9,1},... | collective-permute-start | bytes 147464 | tf_op jit(solution)/shard_map/ppermute | solution.py:511
  38.9 6.0 %collective-permute-start.16 = (bf16[192,128]{1,0:T(8,128)(2,1)S(1)}, bf16[192,128]{1,0:T(8,128)(2,1)S(1)}, u32[]{:S(2)}, u32[]{:S(2)}) collective-permute-start(bf16[192,128]{1,0:T(8,128)(2,1)S(1)} %get-tuple-element.100), channel_id=1, source_target_pairs={{0,16},{1,17},{2,18},{3,19},{4,20},{5,21},{6,22},{7,23},{8,24},{9,... | collective-permute-start | bytes 147464 | tf_op jit(solution)/shard_map/ppermute | solution.py:511
  40.8 5.9 %collective-permute-start.17 = (bf16[192,128]{1,0:T(8,128)(2,1)S(1)}, bf16[192,128]{1,0:T(8,128)(2,1)S(1)}, u32[]{:S(2)}, u32[]{:S(2)}) collective-permute-start(bf16[192,128]{1,0:T(8,128)(2,1)S(1)} %get-tuple-element.101), channel_id=1, source_target_pairs={{0,24},{1,25},{2,26},{3,27},{4,28},{5,29},{6,30},{7,31},{8,16},{9,... | collective-permute-start | bytes 147464 | tf_op jit(solution)/shard_map/ppermute | solution.py:511

commit v5 on v4

--- a/solution.py
+++ b/solution.py
@@ -311,10 +311,10 @@
 
 def sums_kernel(
     yxs, cot_t_ref, twin_left_ref, twin_right_ref, normed_ref, scaled_ref,
-    w1_ref, w2_ref, bias_ref, *refs,
+    w1_ref, w2_ref, bias_ref, diag_ref, *refs,
 ):
     mine, other = refs[:yxs], refs[yxs : 2 * yxs]
-    small_ref, rights_ref, spread_ref, grad_ref, wide, lefts, turned, cots, got_t = refs[2 * yxs :]
+    small_ref, rights_ref, out_ref, grad_ref, spread_ref, wide, lefts, turned, cots, got_t, outs = refs[2 * yxs :]
     columns = rights_ref.shape[0]
     lanes = mine[0].shape[1]
     seqs = lanes // 2
@@ -322,7 +322,7 @@
     hidden = w1_ref.shape[0]
     twins = hidden // 2
     pairs = bias_ref.shape[1]
-    res = spread_ref.shape[1] // lanes
+    res = cot_t_ref.shape[0] // pairs
     index = lax.axis_index("row")
     height = res * hidden
     per = res * res
@@ -366,13 +366,14 @@
         return jnp.concatenate(parts, axis=0) * (1.0 / seqs)
 
     left_sum = summed(cot_t_ref, rights_ref, twin_left_ref, spread_ref)
+    share_kernel(res, diag_ref, spread_ref, out_ref, outs)
     right_sum = summed(got_t, lefts, twin_right_ref, turned)
     normed_grad = mm(left_sum.astype(bf16), w1_ref[...]) + mm(right_sum.astype(bf16), w2_ref[...])
     grad_ref[...] = normed_grad
     factors_t = jnp.concatenate([left_sum, right_sum], axis=1).T.astype(bf16)
     weights = mm(factors_t, normed_ref[...])
     gain_part = jnp.sum(normed_grad * scaled_ref[...], axis=0, keepdims=True)
-    line = lax.broadcasted_iota(jnp.int32, (16, pairs), 0)
+    line = lax.broadcasted_iota(jnp.int32, (8, pairs), 0)
     parts = channels // pairs
     rows = small_ref.shape[0] // parts
     for n in range(parts):
@@ -381,7 +382,7 @@
         small_ref[n * rows + 2 * hidden : (n + 1) * rows, :] = jnp.where(
             line == 0,
             gain_part[:, here],
-            jnp.where(line == 1, bias_ref[:1, :], jnp.zeros((16, pairs), f32)),
+            jnp.where(line == 1, bias_ref[:1, :], jnp.zeros((8, pairs), f32)),
         )
 
 
@@ -599,33 +600,27 @@
     mine[0], prepared = lax.optimization_barrier((mine[0], prepared))
     cot_t, twin_left, twin_right, bias_part, w1, w2 = prepared
     other = [swap(m, 1) for m in mine]
-    small, rights, spread, normed_grad = call(
+    small, rights, out_part, normed_grad = call(
         functools.partial(sums_kernel, yxs),
         "sums",
         (
-            cot_t, twin_left, twin_right, normed, scaled, w1, w2, bias_part, *mine, *other,
+            cot_t, twin_left, twin_right, normed, scaled, w1, w2, bias_part, diag, *mine, *other,
         ),
         [
-            ((channels // pairs * (2 * hidden + 16), pairs), f32),
+            ((channels // pairs * (2 * hidden + 8), pairs), f32),
             ((columns, hidden * seqs), bf16),
+            ((hidden * hidden, pairs), f32),
+            ((own, channels), f32),
+        ],
+        [
             ((twins * pairs, res * lanes), bf16),
-            ((own, channels), f32),
-        ],
-        [
             (((columns + 1) * hidden, lanes), f32),
             ((columns, hidden * seqs), bf16),
             ((twins * pairs, res * lanes), bf16),
             ((res * columns, pairs), f32),
             ((res * pairs, columns), bf16),
-        ],
-        10**6,
-    )
-    (out_part,) = call(
-        functools.partial(share_kernel, res),
-        "shares",
-        (diag, spread),
-        [((hidden * hidden, pairs), f32)],
-        [((hidden * (hidden + 1), pairs), f32)],
+            ((hidden * (hidden + 1), pairs), f32),
+        ],
         10**6,
     )
     delta, grad = call(
@@ -669,7 +664,7 @@
             ((hidden * hidden // count, pairs), f32),
             ((1, pairs), f32),
         ],
-        [((2 * hidden + 16, channels), f32), ((hidden * hidden // count, pairs), f32)],
+        [((2 * hidden + 8, channels), f32), ((hidden * hidden // count, pairs), f32)],
         10**6,
         remote_out=True,
     )

time: 47.8 us -> 47.1 us (0.985)
  waiting for transfers between devices: 12 us -> 17 us
  local copies, waits for them, and re-layouts: 6.45 us -> 1.53 us
  starting transfers between devices: 18.9 us -> 18.4 us
    ppermute x18, waiting for transfers between devices: 12 us -> 17 us  [swap(): return lax.ppermute(value, 'row', [(i, i ^ step) for i in range(count)])]
    unnamed x20 -> x16, local copies, waits for them, and re-layouts: 6.44 us -> 1.52 us
    ppermute x18, starting transfers between devices: 18.9 us -> 18.4 us  [swap(): return lax.ppermute(value, 'row', [(i, i ^ step) for i in range(count)])]
    pallas_call x10 -> x9, Pallas kernels: 9.25 us -> 9.21 us  [call(): pl.pallas_call(kernel, out_shape=[jax.ShapeDtypeStruct(s, d) for s, d in...]
  transfers between devices with their start and end apart: 18 -> 18, of which waited for: 9 -> 10; matrix products, arithmetic and copies ran while one was open for 0% -> 0% of each run, Pallas kernels for 6% -> 6%
where the time goes in v5:
time: 47.1 us; the launch traced here: 46.9 us
  starting transfers between devices  18.4 us (39%)
  waiting for transfers between devices  17 us (36%)
  Pallas kernels  9.21 us (20%)
  local copies, waits for them, and re-layouts  1.53 us (3%)
  between operations  0.76 us (2%)
    ppermute x18, starting transfers between devices, swap(): return lax.ppermute(value, 'row', [(i, i ^ step) for i in range(count)])  18.4 us
    ppermute x18, waiting for transfers between devices, swap(): return lax.ppermute(value, 'row', [(i, i ^ step) for i in range(count)])  17 us
    pallas_call x9, Pallas kernels, call(): pl.pallas_call(kernel, out_shape=[jax.ShapeDtypeStruct(s, d) for s, d in...  9.21 us
    unnamed x16, local copies, waits for them, and re-layouts  1.52 us
  transfers between devices with their start and end apart: 18, of which 10 were waited for; matrix products, arithmetic and copies ran while one was open for 0% of the time, Pallas kernels for 6%

profile of v5, /device:TPU:0, one launch (start us, length us, event | category | flops | bytes accessed | tf_op | source)
XLA Modules:
  0.0 46.9 jit_solution(13230115641156129256)
XLA Ops:
  0.7 2.2 %factors.1 = (bf16[256,128]{1,0:T(8,128)(2,1)}, bf16[256,128]{1,0:T(8,128)(2,1)}, bf16[256,128]{1,0:T(8,128)(2,1)}, bf16[256,128]{1,0:T(8,128)(2,1)}) custom-call(bf16[64,4,256]{2,1,0:T(4,128)(2,1)} %x_ref.1, f32[1,256]{1,0:T(1,128)} %bitcast.13, bf16[32,256]{1,0:T(8,128)(2,1)} %bitcast.8, bf16[32,256]{1,0:T(8,128)(2,1)} %bitcast.11, ...), custom_call_target="tpu_custom_call" | custom-call | flops 1000000 | bytes 295936 | tf_op jit(solution)/shard_map/factors/pallas_call | solution.py:498
  2.9 3.1 %collective-permute-start = (bf16[256,128]{1,0:T(8,128)(2,1)}, bf16[256,128]{1,0:T(8,128)(2,1)S(1)}, u32[]{:S(2)}, u32[]{:S(2)}) collective-permute-start(bf16[256,128]{1,0:T(8,128)(2,1)} %get-tuple-element.59), channel_id=1, source_target_pairs={{0,8},{1,9},{2,10},{3,11},{4,12},{5,13},{6,14},{7,15},{8,0},{9,1},... | collective-permute-start | bytes 196616 | tf_op jit(solution)/shard_map/ppermute | solution.py:512
  6.0 2.6 %collective-permute-start.1 = (bf16[256,128]{1,0:T(8,128)(2,1)}, bf16[256,128]{1,0:T(8,128)(2,1)S(1)}, u32[]{:S(2)}, u32[]{:S(2)}) collective-permute-start(bf16[256,128]{1,0:T(8,128)(2,1)} %get-tuple-element.60), channel_id=1, source_target_pairs={{0,16},{1,17},{2,18},{3,19},{4,20},{5,21},{6,22},{7,23},{8,24},{9,... | collective-permute-start | bytes 196616 | tf_op jit(solution)/shard_map/ppermute | solution.py:512
  8.6 0.8 %copy-done.4 = bf16[256,128]{1,0:T(8,128)(2,1)S(1)} copy-done((bf16[256,128]{1,0:T(8,128)(2,1)S(1)}, bf16[256,128]{1,0:T(8,128)(2,1)}, u32[]{:S(2)}) %copy-start.4) | copy-done | bytes 65560
  9.5 0.4 own.1
  9.9 3.6 %collective-permute-done.1.refs_2_ = bf16[256,128]{1,0:T(8,128)(2,1)S(1)} collective-permute-done((bf16[256,128]{1,0:T(8,128)(2,1)}, bf16[256,128]{1,0:T(8,128)(2,1)S(1)}, u32[]{:S(2)}, u32[]{:S(2)}) %collective-permute-start.1) | collective-permute-done | bytes 65568 | tf_op jit(solution)/shard_map/ppermute | solution.py:512
  13.5 1.4 %collective-permute-done.2.refs_3_ = bf16[256,128]{1,0:T(8,128)(2,1)S(1)} collective-permute-done((bf16[256,128]{1,0:T(8,128)(2,1)}, bf16[256,128]{1,0:T(8,128)(2,1)S(1)}, u32[]{:S(2)}, u32[]{:S(2)}) %collective-permute-start.2) | collective-permute-done | bytes 65568 | tf_op jit(solution)/shard_map/ppermute | solution.py:512
  15.0 1.6 %collective-permute-start.3 = (bf16[640,128]{1,0:T(8,128)(2,1)S(1)}, bf16[640,128]{1,0:T(8,128)(2,1)S(1)}, u32[]{:S(2)}, u32[]{:S(2)}) collective-permute-start(bf16[640,128]{1,0:T(8,128)(2,1)S(1)} %get-tuple-element.79), channel_id=1, source_target_pairs={{0,2},{1,3},{2,0},{3,1},{4,6},{5,7},{6,4},{7,5},{8,10},{9,11},{10,... | collective-permute-start | bytes 491528 | tf_op jit(solution)/shard_map/ppermute | solution.py:512
  16.5 1.5 %collective-permute-start.4 = (bf16[640,128]{1,0:T(8,128)(2,1)S(1)}, bf16[640,128]{1,0:T(8,128)(2,1)S(1)}, u32[]{:S(2)}, u32[]{:S(2)}) collective-permute-start(bf16[640,128]{1,0:T(8,128)(2,1)S(1)} %get-tuple-element.80), channel_id=1, source_target_pairs={{0,4},{1,5},{2,6},{3,7},{4,0},{5,1},{6,2},{7,3},{8,12},{9,13},{10,... | collective-permute-start | bytes 491528 | tf_op jit(solution)/shard_map/ppermute | solution.py:512
  18.1 0.5 %collective-permute-start.5 = (bf16[640,128]{1,0:T(8,128)(2,1)S(1)}, bf16[640,128]{1,0:T(8,128)(2,1)S(1)}, u32[]{:S(2)}, u32[]{:S(2)}) collective-permute-start(bf16[640,128]{1,0:T(8,128)(2,1)S(1)} %get-tuple-element.81), channel_id=1, source_target_pairs={{0,6},{1,7},{2,4},{3,5},{4,2},{5,3},{6,0},{7,1},{8,14},{9,15},{10,... | collective-permute-start | bytes 491528 | tf_op jit(solution)/shard_map/ppermute | solution.py:512
  18.5 0.4 prepare.1
  19.0 2.7 %collective-permute-done.3.refs_1_ = bf16[640,128]{1,0:T(8,128)(2,1)S(1)} collective-permute-done((bf16[640,128]{1,0:T(8,128)(2,1)S(1)}, bf16[640,128]{1,0:T(8,128)(2,1)S(1)}, u32[]{:S(2)}, u32[]{:S(2)}) %collective-permute-start.3) | collective-permute-done | bytes 163872 | tf_op jit(solution)/shard_map/ppermute | solution.py:512
  21.8 3.0 %collective-permute-done.4.refs_2_ = bf16[640,128]{1,0:T(8,128)(2,1)S(1)} collective-permute-done((bf16[640,128]{1,0:T(8,128)(2,1)S(1)}, bf16[640,128]{1,0:T(8,128)(2,1)S(1)}, u32[]{:S(2)}, u32[]{:S(2)}) %collective-permute-start.4) | collective-permute-done | bytes 163872 | tf_op jit(solution)/shard_map/ppermute | solution.py:512
  24.8 0.5 %collective-permute-start.9 = (bf16[640,128]{1,0:T(8,128)(2,1)S(1)}, bf16[640,128]{1,0:T(8,128)(2,1)S(1)}, u32[]{:S(2)}, u32[]{:S(2)}) collective-permute-start(bf16[640,128]{1,0:T(8,128)(2,1)S(1)} %collective-permute-done.5.refs_3_), channel_id=1, source_target_pairs={{0,1},{1,0},{2,3},{3,2},{4,5},{5,4},{6,7},{7,6},{8,9},{9,8},{10,11... | collective-permute-start | bytes 491528 | tf_op jit(solution)/shard_map/ppermute | solution.py:512
  25.3 0.9 %collective-permute-done.8.refs_6_ = bf16[640,128]{1,0:T(8,128)(2,1)S(1)} collective-permute-done((bf16[640,128]{1,0:T(8,128)(2,1)S(1)}, bf16[640,128]{1,0:T(8,128)(2,1)S(1)}, u32[]{:S(2)}, u32[]{:S(2)}) %collective-permute-start.8) | collective-permute-done | bytes 163872 | tf_op jit(solution)/shard_map/ppermute | solution.py:512
  26.2 0.2 collective-permute-done.9.refs_7_
  26.4 3.3 %sums.1 = (f32[144,128]{1,0:T(8,128)S(1)}, bf16[128,2048]{1,0:T(8,128)(2,1)S(1)}, f32[1024,128]{1,0:T(8,128)S(1)}, f32[256,256]{1,0:T(8,128)S(1)}) custom-call(bf16[512,128]{1,0:T(8,128)(2,1)S(1)} %get-tuple-element.69.cot_t_ref, bf16[64,2048]{1,0:T(8,128)(2,1)S(1)} %get-tuple-element.70.twin_left_ref, ...), custom_call_target="tpu_custom_call" | custom-call | flops 1000000 | bytes 2461696 | tf_op jit(solution)/shard_map/sums/pallas_call | solution.py:498
  29.8 0.3 collective-permute-start.11
  30.1 0.2 collective-permute-start.10
  30.4 1.0 %collective-permute-done.10.small_came = f32[144,128]{1,0:T(8,128)S(1)} collective-permute-done((f32[144,128]{1,0:T(8,128)S(1)}, f32[144,128]{1,0:T(8,128)S(1)}, u32[]{:S(2)}, u32[]{:S(2)}) %collective-permute-start.10) | collective-permute-done | bytes 73760 | tf_op jit(solution)/shard_map/ppermute | solution.py:512
  31.4 0.3 collective-permute-start.12
  31.7 1.1 %collective-permute-start.13 = (bf16[272,128]{1,0:T(8,128)(2,1)S(1)}, bf16[272,128]{1,0:T(8,128)(2,1)S(1)}, u32[]{:S(2)}, u32[]{:S(2)}) collective-permute-start(bf16[272,128]{1,0:T(8,128)(2,1)S(1)} %get-tuple-element.95), channel_id=1, source_target_pairs={{0,4},{1,5},{2,6},{3,7},{4,0},{5,1},{6,2},{7,3},{8,12},{9,13},{10,... | collective-permute-start | bytes 208904 | tf_op jit(solution)/shard_map/ppermute | solution.py:512
  32.9 2.1 %collective-permute-start.14 = (bf16[272,128]{1,0:T(8,128)(2,1)S(1)}, bf16[272,128]{1,0:T(8,128)(2,1)S(1)}, u32[]{:S(2)}, u32[]{:S(2)}) collective-permute-start(bf16[272,128]{1,0:T(8,128)(2,1)S(1)} %get-tuple-element.96), channel_id=1, source_target_pairs={{0,6},{1,7},{2,4},{3,5},{4,2},{5,3},{6,0},{7,1},{8,14},{9,15},{10,... | collective-permute-start | bytes 208904 | tf_op jit(solution)/shard_map/ppermute | solution.py:512
  35.0 0.7 %copy-done.7 = f32[128]{0:T(128)S(1)} copy-done((f32[128]{0:T(128)S(1)}, f32[128]{0:T(128)}, u32[]{:S(2)}) %copy-start.7) | copy-done | bytes 536
  35.7 1.9 %results.1 = (bf16[4,128,128]{2,1,0:T(8,128)(2,1)}, bf16[64,4,256]{2,1,0:T(4,128)(2,1)}) custom-call(bf16[128,2048]{1,0:T(8,128)(2,1)S(1)} %get-tuple-element.85.rights_ref, bf16[64,2048]{1,0:T(8,128)(2,1)S(1)} %get-tuple-element.70.twin_left_ref, bf16[32,256]{1,0:T(8,128)(2,1)S(1)} %get-tuple-element.74.w1_ref, ...), custom_call_target="tpu_custom_call" | custom-call | flops 1000000 | bytes 1590784 | tf_op jit(solution)/shard_map/results/pallas_call | solution.py:498
  37.6 0.5 %collective-permute-done.14.three = bf16[272,128]{1,0:T(8,128)(2,1)S(1)} collective-permute-done((bf16[272,128]{1,0:T(8,128)(2,1)S(1)}, bf16[272,128]{1,0:T(8,128)(2,1)S(1)}, u32[]{:S(2)}, u32[]{:S(2)}) %collective-permute-start.14) | collective-permute-done | bytes 69664 | tf_op jit(solution)/shard_map/ppermute | solution.py:512
  38.1 0.7 %collective-permute-start.15 = (bf16[176,128]{1,0:T(8,128)(2,1)S(1)}, bf16[176,128]{1,0:T(8,128)(2,1)S(1)}, u32[]{:S(2)}, u32[]{:S(2)}) collective-permute-start(bf16[176,128]{1,0:T(8,128)(2,1)S(1)} %get-tuple-element.99), channel_id=1, source_target_pairs={{0,8},{1,9},{2,10},{3,11},{4,12},{5,13},{6,14},{7,15},{8,0},{9,1},... | collective-permute-start | bytes 135176 | tf_op jit(solution)/shard_map/ppermute | solution.py:512
  38.8 1.4 %collective-permute-start.16 = (bf16[176,128]{1,0:T(8,128)(2,1)S(1)}, bf16[176,128]{1,0:T(8,128)(2,1)S(1)}, u32[]{:S(2)}, u32[]{:S(2)}) collective-permute-start(bf16[176,128]{1,0:T(8,128)(2,1)S(1)} %get-tuple-element.100), channel_id=1, source_target_pairs={{0,16},{1,17},{2,18},{3,19},{4,20},{5,21},{6,22},{7,23},{8,24},{9,... | collective-permute-start | bytes 135176 | tf_op jit(solution)/shard_map/ppermute | solution.py:512
  40.3 2.3 %collective-permute-start.17 = (bf16[176,128]{1,0:T(8,128)(2,1)S(1)}, bf16[176,128]{1,0:T(8,128)(2,1)S(1)}, u32[]{:S(2)}, u32[]{:S(2)}) collective-permute-start(bf16[176,128]{1,0:T(8,128)(2,1)S(1)} %get-tuple-element.101), channel_id=1, source_target_pairs={{0,24},{1,25},{2,26},{3,27},{4,28},{5,29},{6,30},{7,31},{8,16},{9,... | collective-permute-start | bytes 135176 | tf_op jit(solution)/shard_map/ppermute | solution.py:512
  42.6 1.6 %collective-permute-done.16.two = bf16[176,128]{1,0:T(8,128)(2,1)S(1)} collective-permute-done((bf16[176,128]{1,0:T(8,128)(2,1)S(1)}, bf16[176,128]{1,0:T(8,128)(2,1)S(1)}, u32[]{:S(2)}, u32[]{:S(2)}) %collective-permute-start.16) | collective-permute-done | bytes 45088 | tf_op jit(solution)/shard_map/ppermute | solution.py:512
  44.2 2.0 %collective-permute-done.17.three = bf16[176,128]{1,0:T(8,128)(2,1)S(1)} collective-permute-done((bf16[176,128]{1,0:T(8,128)(2,1)S(1)}, bf16[176,128]{1,0:T(8,128)(2,1)S(1)}, u32[]{:S(2)}, u32[]{:S(2)}) %collective-permute-start.17) | collective-permute-done | bytes 45088 | tf_op jit(solution)/shard_map/ppermute | solution.py:512
  46.2 0.7 %finish.1 = (f32[1,256]{1,0:T(1,128)}, f32[32,256]{1,0:T(8,128)}, f32[32,256]{1,0:T(8,128)}, f32[32,128]{1,0:T(8,128)}, f32[1,128]{1,0:T(1,128)}) custom-call(bf16[144,128]{1,0:T(8,128)(2,1)S(1)} %get-tuple-element.97.small_in, f32[32,128]{1,0:T(8,128)S(1)} %get-tuple-element.98.out_in, bf16[176,128]{1,0:T(8,128)(2,1)S(1)} %collective-permute-done.15.one, ...), custom_call_target="tpu_custom_call" | custom-call | flops 1000000 | bytes 188416 | tf_op jit(solution)/shard_map/finish/pallas_call | solution.py:498
  (30 shorter events, 0.3 us)
Async XLA Ops:
  0.6 8.0 %copy-start = (bf16[64,4,256]{2,1,0:T(4,128)(2,1)S(1)}, bf16[64,4,256]{2,1,0:T(4,128)(2,1)}, u32[]{:S(2)}) copy-start(bf16[64,4,256]{2,1,0:T(4,128)(2,1)} %x_ref.1) | copy-start | bytes 393220
  0.6 8.0 %copy-start.3 = (bf16[256,32]{0,1:T(8,128)(2,1)S(1)}, bf16[256,32]{0,1:T(8,128)(2,1)}, u32[]{:S(2)}) copy-start(bf16[256,32]{0,1:T(8,128)(2,1)} %param.9) | copy-start | bytes 49156
  0.7 8.0 %copy-start.6 = (f32[256]{0:T(256)S(1)}, f32[256]{0:T(256)}, u32[]{:S(2)}) copy-start(f32[256]{0:T(256)} %param.8) | copy-start | bytes 3076
  2.9 15.6 %copy-start.2 = (bf16[1024,128]{1,0:T(8,128)(2,1)S(1)}, bf16[1024,128]{1,0:T(8,128)(2,1)}, u32[]{:S(2)}) copy-start(bf16[1024,128]{1,0:T(8,128)(2,1)} %out_w_ref.1) | copy-start | bytes 786436
  2.9 7.0 %collective-permute-start = (bf16[256,128]{1,0:T(8,128)(2,1)}, bf16[256,128]{1,0:T(8,128)(2,1)S(1)}, u32[]{:S(2)}, u32[]{:S(2)}) collective-permute-start(bf16[256,128]{1,0:T(8,128)(2,1)} %get-tuple-element.59), channel_id=1, source_target_pairs={{0,8},{1,9},{2,10},{3,11},{4,12},{5,13},{6,14},{7,15},{8,0},{9,1},... | collective-permute-start | bytes 196616 | tf_op jit(solution)/shard_map/ppermute | solution.py:512
  6.0 7.5 %collective-permute-start.1 = (bf16[256,128]{1,0:T(8,128)(2,1)}, bf16[256,128]{1,0:T(8,128)(2,1)S(1)}, u32[]{:S(2)}, u32[]{:S(2)}) collective-permute-start(bf16[256,128]{1,0:T(8,128)(2,1)} %get-tuple-element.60), channel_id=1, source_target_pairs={{0,16},{1,17},{2,18},{3,19},{4,20},{5,21},{6,22},{7,23},{8,24},{9,... | collective-permute-start | bytes 196616 | tf_op jit(solution)/shard_map/ppermute | solution.py:512
  8.6 6.3 %collective-permute-start.2 = (bf16[256,128]{1,0:T(8,128)(2,1)}, bf16[256,128]{1,0:T(8,128)(2,1)S(1)}, u32[]{:S(2)}, u32[]{:S(2)}) collective-permute-start(bf16[256,128]{1,0:T(8,128)(2,1)} %get-tuple-element.61), channel_id=1, source_target_pairs={{0,24},{1,25},{2,26},{3,27},{4,28},{5,29},{6,30},{7,31},{8,16},{9,... | collective-permute-start | bytes 196616 | tf_op jit(solution)/shard_map/ppermute | solution.py:512
  8.6 0.8 %copy-start.4 = (bf16[256,128]{1,0:T(8,128)(2,1)S(1)}, bf16[256,128]{1,0:T(8,128)(2,1)}, u32[]{:S(2)}) copy-start(bf16[256,128]{1,0:T(8,128)(2,1)} %get-tuple-element.57.send_in) | copy-start | bytes 196612
  14.9 3.6 %copy-start.1 = (bf16[4,128,128]{2,1,0:T(8,128)(2,1)S(1)}, bf16[4,128,128]{2,1,0:T(8,128)(2,1)}, u32[]{:S(2)}) copy-start(bf16[4,128,128]{2,1,0:T(8,128)(2,1)} %cot_ref.1) | copy-start | bytes 393220
  14.9 3.6 %copy-start.5 = (bf16[256,32]{0,1:T(8,128)(2,1)S(1)}, bf16[256,32]{0,1:T(8,128)(2,1)}, u32[]{:S(2)}) copy-start(bf16[256,32]{0,1:T(8,128)(2,1)} %param.10) | copy-start | bytes 49156
  15.0 6.8 %collective-permute-start.3 = (bf16[640,128]{1,0:T(8,128)(2,1)S(1)}, bf16[640,128]{1,0:T(8,128)(2,1)S(1)}, u32[]{:S(2)}, u32[]{:S(2)}) collective-permute-start(bf16[640,128]{1,0:T(8,128)(2,1)S(1)} %get-tuple-element.79), channel_id=1, source_target_pairs={{0,2},{1,3},{2,0},{3,1},{4,6},{5,7},{6,4},{7,5},{8,10},{9,11},{10,... | collective-permute-start | bytes 491528 | tf_op jit(solution)/shard_map/ppermute | solution.py:512
  16.5 8.2 %collective-permute-start.4 = (bf16[640,128]{1,0:T(8,128)(2,1)S(1)}, bf16[640,128]{1,0:T(8,128)(2,1)S(1)}, u32[]{:S(2)}, u32[]{:S(2)}) collective-permute-start(bf16[640,128]{1,0:T(8,128)(2,1)S(1)} %get-tuple-element.80), channel_id=1, source_target_pairs={{0,4},{1,5},{2,6},{3,7},{4,0},{5,1},{6,2},{7,3},{8,12},{9,13},{10,... | collective-permute-start | bytes 491528 | tf_op jit(solution)/shard_map/ppermute | solution.py:512
  18.1 6.7 %collective-permute-start.5 = (bf16[640,128]{1,0:T(8,128)(2,1)S(1)}, bf16[640,128]{1,0:T(8,128)(2,1)S(1)}, u32[]{:S(2)}, u32[]{:S(2)}) collective-permute-start(bf16[640,128]{1,0:T(8,128)(2,1)S(1)} %get-tuple-element.81), channel_id=1, source_target_pairs={{0,6},{1,7},{2,4},{3,5},{4,2},{5,3},{6,0},{7,1},{8,14},{9,15},{10,... | collective-permute-start | bytes 491528 | tf_op jit(solution)/shard_map/ppermute | solution.py:512
  19.0 6.3 %collective-permute-start.6 = (bf16[640,128]{1,0:T(8,128)(2,1)S(1)}, bf16[640,128]{1,0:T(8,128)(2,1)S(1)}, u32[]{:S(2)}, u32[]{:S(2)}) collective-permute-start(bf16[640,128]{1,0:T(8,128)(2,1)S(1)} %get-tuple-element.78.refs_0_), channel_id=1, source_target_pairs={{0,1},{1,0},{2,3},{3,2},{4,5},{5,4},{6,7},{7,6},{8,9},{9,8},{10,11... | collective-permute-start | bytes 491528 | tf_op jit(solution)/shard_map/ppermute | solution.py:512
  21.8 3.5 %collective-permute-start.7 = (bf16[640,128]{1,0:T(8,128)(2,1)S(1)}, bf16[640,128]{1,0:T(8,128)(2,1)S(1)}, u32[]{:S(2)}, u32[]{:S(2)}) collective-permute-start(bf16[640,128]{1,0:T(8,128)(2,1)S(1)} %collective-permute-done.3.refs_1_), channel_id=1, source_target_pairs={{0,1},{1,0},{2,3},{3,2},{4,5},{5,4},{6,7},{7,6},{8,9},{9,8},{10,11... | collective-permute-start | bytes 491528 | tf_op jit(solution)/shard_map/ppermute | solution.py:512
  24.8 1.4 %collective-permute-start.8 = (bf16[640,128]{1,0:T(8,128)(2,1)S(1)}, bf16[640,128]{1,0:T(8,128)(2,1)S(1)}, u32[]{:S(2)}, u32[]{:S(2)}) collective-permute-start(bf16[640,128]{1,0:T(8,128)(2,1)S(1)} %collective-permute-done.4.refs_2_), channel_id=1, source_target_pairs={{0,1},{1,0},{2,3},{3,2},{4,5},{5,4},{6,7},{7,6},{8,9},{9,8},{10,11... | collective-permute-start | bytes 491528 | tf_op jit(solution)/shard_map/ppermute | solution.py:512
  24.8 1.6 %collective-permute-start.9 = (bf16[640,128]{1,0:T(8,128)(2,1)S(1)}, bf16[640,128]{1,0:T(8,128)(2,1)S(1)}, u32[]{:S(2)}, u32[]{:S(2)}) collective-permute-start(bf16[640,128]{1,0:T(8,128)(2,1)S(1)} %collective-permute-done.5.refs_3_), channel_id=1, source_target_pairs={{0,1},{1,0},{2,3},{3,2},{4,5},{5,4},{6,7},{7,6},{8,9},{9,8},{10,11... | collective-permute-start | bytes 491528 | tf_op jit(solution)/shard_map/ppermute | solution.py:512
  29.8 1.6 %collective-permute-start.11 = (bf16[512,128]{1,0:T(8,128)(2,1)S(1)}, bf16[512,128]{1,0:T(8,128)(2,1)S(1)}, u32[]{:S(2)}, u32[]{:S(2)}) collective-permute-start(bf16[512,128]{1,0:T(8,128)(2,1)S(1)} %slice.7), channel_id=1, source_target_pairs={{0,1},{1,0},{2,3},{3,2},{4,5},{5,4},{6,7},{7,6},{8,9},{9,8},{10,11... | collective-permute-start | bytes 393224 | tf_op jit(solution)/shard_map/ppermute | solution.py:512
  30.1 1.3 %collective-permute-start.10 = (f32[144,128]{1,0:T(8,128)S(1)}, f32[144,128]{1,0:T(8,128)S(1)}, u32[]{:S(2)}, u32[]{:S(2)}) collective-permute-start(f32[144,128]{1,0:T(8,128)S(1)} %get-tuple-element.82.small_in), channel_id=1, source_target_pairs={{0,1},{1,0},{2,3},{3,2},{4,5},{5,4},{6,7},{7,6},{8,9},{9,8},{10,11... | collective-permute-start | bytes 221192 | tf_op jit(solution)/shard_map/ppermute | solution.py:512
  31.4 6.2 %collective-permute-start.12 = (bf16[272,128]{1,0:T(8,128)(2,1)S(1)}, bf16[272,128]{1,0:T(8,128)(2,1)S(1)}, u32[]{:S(2)}, u32[]{:S(2)}) collective-permute-start(bf16[272,128]{1,0:T(8,128)(2,1)S(1)} %get-tuple-element.94), channel_id=1, source_target_pairs={{0,2},{1,3},{2,0},{3,1},{4,6},{5,7},{6,4},{7,5},{8,10},{9,11},{10,... | collective-permute-start | bytes 208904 | tf_op jit(solution)/shard_map/ppermute | solution.py:512
  31.7 5.9 %collective-permute-start.13 = (bf16[272,128]{1,0:T(8,128)(2,1)S(1)}, bf16[272,128]{1,0:T(8,128)(2,1)S(1)}, u32[]{:S(2)}, u32[]{:S(2)}) collective-permute-start(bf16[272,128]{1,0:T(8,128)(2,1)S(1)} %get-tuple-element.95), channel_id=1, source_target_pairs={{0,4},{1,5},{2,6},{3,7},{4,0},{5,1},{6,2},{7,3},{8,12},{9,13},{10,... | collective-permute-start | bytes 208904 | tf_op jit(solution)/shard_map/ppermute | solution.py:512
  32.9 5.2 %collective-permute-start.14 = (bf16[272,128]{1,0:T(8,128)(2,1)S(1)}, bf16[272,128]{1,0:T(8,128)(2,1)S(1)}, u32[]{:S(2)}, u32[]{:S(2)}) collective-permute-start(bf16[272,128]{1,0:T(8,128)(2,1)S(1)} %get-tuple-element.96), channel_id=1, source_target_pairs={{0,6},{1,7},{2,4},{3,5},{4,2},{5,3},{6,0},{7,1},{8,14},{9,15},{10,... | collective-permute-start | bytes 208904 | tf_op jit(solution)/shard_map/ppermute | solution.py:512
  35.0 0.7 %copy-start.7 = (f32[128]{0:T(128)S(1)}, f32[128]{0:T(128)}, u32[]{:S(2)}) copy-start(f32[128]{0:T(128)} %param.12) | copy-start | bytes 1540
  38.1 4.5 %collective-permute-start.15 = (bf16[176,128]{1,0:T(8,128)(2,1)S(1)}, bf16[176,128]{1,0:T(8,128)(2,1)S(1)}, u32[]{:S(2)}, u32[]{:S(2)}) collective-permute-start(bf16[176,128]{1,0:T(8,128)(2,1)S(1)} %get-tuple-element.99), channel_id=1, source_target_pairs={{0,8},{1,9},{2,10},{3,11},{4,12},{5,13},{6,14},{7,15},{8,0},{9,1},... | collective-permute-start | bytes 135176 | tf_op jit(solution)/shard_map/ppermute | solution.py:512
  38.8 5.4 %collective-permute-start.16 = (bf16[176,128]{1,0:T(8,128)(2,1)S(1)}, bf16[176,128]{1,0:T(8,128)(2,1)S(1)}, u32[]{:S(2)}, u32[]{:S(2)}) collective-permute-start(bf16[176,128]{1,0:T(8,128)(2,1)S(1)} %get-tuple-element.100), channel_id=1, source_target_pairs={{0,16},{1,17},{2,18},{3,19},{4,20},{5,21},{6,22},{7,23},{8,24},{9,... | collective-permute-start | bytes 135176 | tf_op jit(solution)/shard_map/ppermute | solution.py:512
  40.3 5.9 %collective-permute-start.17 = (bf16[176,128]{1,0:T(8,128)(2,1)S(1)}, bf16[176,128]{1,0:T(8,128)(2,1)S(1)}, u32[]{:S(2)}, u32[]{:S(2)}) collective-permute-start(bf16[176,128]{1,0:T(8,128)(2,1)S(1)} %get-tuple-element.101), channel_id=1, source_target_pairs={{0,24},{1,25},{2,26},{3,27},{4,28},{5,29},{6,30},{7,31},{8,16},{9,... | collective-permute-start | bytes 135176 | tf_op jit(solution)/shard_map/ppermute | solution.py:512
